TPU v7x, 1024 devices: a whole 4x8x16 slice. The times are simulated.
1024 devices in a mesh: row: 32 (over y, x), col: 4 (over z_hi, core), depth: 8 (over z_lo).
Axes of the slice: x: 4, y: 8, z: 16 (z_hi: 2, z_lo: 8; z = z_hi * 8 + z_lo), core: 2. Of those that a mesh axis runs over, the one named last changes fastest.
Arguments:
- blocks: float32 [1024, 10, 128, 128], P(('row', 'col', 'depth')), may hold values from -1.5 to 1.5
- columns: int32 [1024, 10], replicated, may hold values from 0 to 1023, as said below
Outputs:
- product: float32 [1024, 10, 128, 128], P(('row', 'col', 'depth'))
Inputs may be any that keep to these rules, and one draw needn't show every extreme that they name: The columns of a block row are distinct. Slot s of block row i holds block column (i + t) mod 1024 with t ≡ s − i (mod 8) and -16 < t < 16; slot i mod 8 holds column i itself.
All inputs are finite; a program needn't handle non-finite values.
Results may differ from a plain program's by a relative error of at most 0.0003.
Values sent between devices are 32-bit elements; how exact they have to be, the bound alone decides.
No kernel may reach another device: no remote copies, remote signals or barrier semaphores. Data moves between devices by JAX's collectives and lax.ppermute only.
A program may use at most 64 MiB of HBM per device.

v0:
```python
import jax
import jax.numpy as jnp
from jax import lax
from jax.sharding import PartitionSpec as P


def from_behind(value, axis, steps):
    count = lax.axis_size(axis)
    pairs = [(source, (source + steps) % count) for source in range(count)]
    return lax.ppermute(value, axis, pairs)


def body(blocks, columns):
    depth_count = lax.axis_size("depth")
    depth_pos = lax.axis_index("depth")
    group_pos = lax.axis_index("row") * lax.axis_size("col") + lax.axis_index("col")
    block_rows = columns.shape[0]
    slot_count = columns.shape[1]
    edge = blocks.shape[2]
    rounds = (slot_count + depth_count - 1) // depth_count
    first_row = group_pos * depth_count
    local_cols = lax.dynamic_slice_in_dim(columns, first_row, depth_count, 0)
    offsets = jnp.arange(depth_count, dtype=jnp.int32)
    own_rows = first_row + offsets
    slot_ids = depth_pos + depth_count * jnp.arange(rounds, dtype=jnp.int32)
    valid = (slot_ids < slot_count).astype(jnp.float32)
    safe_ids = jnp.minimum(slot_ids, slot_count - 1)
    target = jnp.take(local_cols, safe_ids, axis=1)
    reach = rounds * depth_count
    distance = (target - own_rows[:, None] + reach) % block_rows - reach
    source = (offsets[:, None] + distance - depth_pos) // depth_count + rounds
    target_cols = jnp.take(columns, target, axis=0)
    matched = (target_cols[:, :, :, None] == local_cols[:, None, None, :]).astype(
        jnp.float32
    ) * valid[None, :, None, None]
    pieces = []
    for group_offset in range(-rounds, rounds + 1):
        if group_offset == 0:
            pieces.append(blocks)
        else:
            pieces.append(from_behind(blocks, ("row", "col"), -group_offset))
    nearby = jnp.concatenate(pieces, axis=0)
    filler = jnp.zeros((1, reach - slot_count, edge, edge), jnp.float32)
    padded = jnp.concatenate([blocks, filler], axis=1).reshape(1, rounds, depth_count, edge, edge)
    gathered = lax.all_to_all(padded, "depth", split_axis=2, concat_axis=0, tiled=True)
    operand = gathered[:, :, 0]
    total = jnp.zeros((depth_count, slot_count, edge, edge), jnp.float32)
    for turn in range(rounds):
        partner = jnp.take(nearby, source[:, turn], axis=0)
        chosen = jnp.einsum(
            "lro,lrbc->lobc", matched[:, turn], partner, precision=lax.Precision.HIGHEST
        )
        total = total + jnp.einsum(
            "lab,lobc->loac", operand[:, turn], chosen, precision=lax.Precision.HIGHEST
        )
    return lax.psum_scatter(total, "depth", scatter_dimension=0, tiled=True)


def solution(mesh):
    placed = (P(("row", "col", "depth"), None, None, None), P())
    return jax.shard_map(
        body,
        mesh=mesh,
        in_specs=placed,
        out_specs=P(("row", "col", "depth"), None, None, None),
        check_vma=False,
    )
```

profile of v0, /device:TPU:1, one launch (start us, length us, event | category | flops | bytes accessed | tf_op | source)
XLA Modules:
  0.0 412.3 jit_solution(17998838834661639902)
XLA Ops:
  6.5 0.0 copy-start.2
  6.5 20.0 %collective-permute-start = (f32[1,10,128,128]{3,2,1,0:T(8,128)}, f32[1,10,128,128]{3,2,1,0:T(8,128)}, u32[]{:S(2)}, u32[]{:S(2)}) collective-permute-start(f32[1,10,128,128]{3,2,1,0:T(8,128)} %param.4), channel_id=1, source_target_pairs={{0,16},{8,24},{16,32},{24,40},{32,48},{40,56},{48,64},{56,72},{64,... | collective-permute-start | bytes 1966088 | tf_op jit(solution)/shard_map/ppermute | solution.py:10
  26.6 2.5 collective-permute-start.1
  29.1 2.3 collective-permute-start.2
  31.4 16.2 %collective-permute-start.3 = (f32[1,10,128,128]{3,2,1,0:T(8,128)}, f32[1,10,128,128]{3,2,1,0:T(8,128)}, u32[]{:S(2)}, u32[]{:S(2)}) collective-permute-start(f32[1,10,128,128]{3,2,1,0:T(8,128)} %param.4), channel_id=1, source_target_pairs={{0,1008},{8,1016},{16,0},{24,8},{32,16},{40,24},{48,32},{56,40},{6... | collective-permute-start | bytes 1966088 | tf_op jit(solution)/shard_map/ppermute | solution.py:10
  47.6 1.2 concatenate.7
  48.8 1.1 copy.28
  49.9 7.9 %all-to-all-start = ((f32[1,2,8,128,128]{4,3,1,0,2:T(8,128)}), f32[1,2,8,128,128]{4,3,1,0,2:T(8,128)}, u32[]{:S(2)}, u32[]{:S(2)}) async-start(f32[1,2,8,128,128]{4,3,1,0,2:T(8,128)} %copy.28), calls=%async_computation | async-start | bytes 2097152 | tf_op jit(solution)/shard_map/all_to_all | solution.py:45
  57.8 0.0 reduce-scatter.2.cloned.1.call-start
  57.9 0.0 copy-done.2
  57.9 0.2 copy.24
  58.1 0.1 constant_dynamic-slice_fusion
  58.2 0.6 gather_fusion
  58.8 0.1 compare_select_fusion.1
  58.8 0.1 compare_and_fusion.2
  58.9 0.1 copy.26
  59.0 0.1 copy.23
  59.1 0.1 reshape.120
  59.2 0.6 gather_fusion.1
  59.7 0.1 copy_select_fusion
  59.8 0.1 compare_select_fusion
  59.9 0.1 fusion.13
  60.1 0.0 collective-permute-done
  60.1 1.1 constant_dynamic-update-slice_fusion.4
  61.2 0.0 collective-permute-done.1
  61.2 1.1 constant_dynamic-update-slice_fusion.3
  62.4 1.1 constant_dynamic-update-slice_fusion.2
  63.5 0.0 collective-permute-done.2
  63.5 1.1 constant_dynamic-update-slice_fusion.1
  64.6 10.2 %collective-permute-done.3 = f32[1,10,128,128]{3,2,1,0:T(8,128)} collective-permute-done((f32[1,10,128,128]{3,2,1,0:T(8,128)}, f32[1,10,128,128]{3,2,1,0:T(8,128)}, u32[]{:S(2)}, u32[]{:S(2)}) %collective-permute-start.3) | collective-permute-done | bytes 655392 | tf_op jit(solution)/shard_map/ppermute | solution.py:10
  74.8 1.1 constant_dynamic-update-slice_fusion
  75.9 3.2 gather_fusion.3
  79.1 3.2 gather_fusion.2
  82.3 0.0 copy-start.1
  82.3 3.3 broadcast_select_fusion
  85.6 0.7 copy-done.1
  86.4 0.9 broadcast_select_fusion.1
  87.3 12.4 %fusion = f32[8,10,128,128]{3,1,2,0:T(8,128)} fusion(f32[8,10,128,128]{3,2,1,0:T(8,128)S(1)} %broadcast_select_fusion, f32[8,2,10,10]{2,3,0,1:T(8,128)S(1)} %compare_select_fusion), kind=kOutput, calls=%fused_computation.4 | convolution fusion | flops 157286400 | bytes 10551296 | tf_op jit(solution)/shard_map/lro,lrbc->lobc/dot_general | solution.py:50
  99.7 12.1 %fusion.2 = f32[8,10,128,128]{3,1,2,0:T(8,128)} fusion(f32[8,10,128,128]{3,2,1,0:T(8,128)S(1)} %broadcast_select_fusion.1, f32[8,2,10,10]{2,3,0,1:T(8,128)S(1)} %compare_select_fusion), kind=kOutput, calls=%fused_computation.6 | convolution fusion | flops 157286400 | bytes 10551296 | tf_op jit(solution)/shard_map/lro,lrbc->lobc/dot_general | solution.py:50
  111.8 130.9 %all-to-all-done = f32[1,2,8,128,128]{4,3,1,0,2:T(8,128)} async-done(((f32[1,2,8,128,128]{4,3,1,0,2:T(8,128)}), f32[1,2,8,128,128]{4,3,1,0,2:T(8,128)}, u32[]{:S(2)}, u32[]{:S(2)}) %all-to-all-start) | async-done | bytes 1048608 | tf_op jit(solution)/shard_map/all_to_all | solution.py:45
  242.8 1.3 copy.50
  244.1 0.0 copy-start
  244.1 12.7 %fusion.4 = f32[8,10,128,128]{3,2,1,0:T(8,128)S(1)} fusion(f32[8,10,128,128]{3,1,2,0:T(8,128)} %fusion, f32[8,2,128,128]{3,2,0,1:T(8,128)S(1)} %bitcast.57), kind=kOutput, calls=%fused_computation.8 | convolution fusion | flops 2013265920 | bytes 11010048 | tf_op jit(solution)/shard_map/lab,lobc->loac/dot_general | solution.py:53
  256.8 0.0 copy-done
  256.8 10.3 %add_bitcast_fusion = f32[8,10,128,128]{2,3,1,0:T(8,128)} fusion(f32[8,10,128,128]{3,2,1,0:T(8,128)S(1)} %fusion.4, f32[8,10,128,128]{3,1,2,0:T(8,128)S(1)} %copy-done, f32[8,2,128,128]{3,2,0,1:T(8,128)S(1)} %bitcast.58), kind=kOutput, calls=%fused_computation.12 | convolution fusion | flops 2014576640 | bytes 19398656 | tf_op jit(solution)/shard_map/lab,lobc->loac/dot_general | solution.py:53
  267.0 0.0 reduce-scatter.2.cloned.1.call-update
  267.0 136.3 %reduce-scatter.2.cloned.1.call-done = f32[1,10,128,128]{2,3,1,0:T(8,128)} async-done(((f32[8,10,128,128]{2,3,1,0:T(8,128)}), f32[1,10,128,128]{2,3,1,0:T(8,128)}) %reduce-scatter.2.cloned.1.call-update) | async-done | bytes 655376 | tf_op jit(solution)/shard_map/reduce_scatter | solution.py:56
  403.3 2.2 copy.33
  (8 shorter events, 0.1 us)
Async XLA Ops:
  6.5 51.4 %copy-start.2 = (s32[1024,10]{0,1:T(8,128)S(1)}, s32[1024,10]{0,1:T(8,128)}, u32[]{:S(2)}) copy-start(s32[1024,10]{0,1:T(8,128)} %param.5) | copy-start | bytes 122884
  6.5 53.5 %collective-permute-start = (f32[1,10,128,128]{3,2,1,0:T(8,128)}, f32[1,10,128,128]{3,2,1,0:T(8,128)}, u32[]{:S(2)}, u32[]{:S(2)}) collective-permute-start(f32[1,10,128,128]{3,2,1,0:T(8,128)} %param.4), channel_id=1, source_target_pairs={{0,16},{8,24},{16,32},{24,40},{32,48},{40,56},{48,64},{56,72},{64,... | collective-permute-start | bytes 1966088 | tf_op jit(solution)/shard_map/ppermute | solution.py:10
  26.6 34.6 %collective-permute-start.1 = (f32[1,10,128,128]{3,2,1,0:T(8,128)}, f32[1,10,128,128]{3,2,1,0:T(8,128)}, u32[]{:S(2)}, u32[]{:S(2)}) collective-permute-start(f32[1,10,128,128]{3,2,1,0:T(8,128)} %param.4), channel_id=1, source_target_pairs={{0,8},{8,16},{16,24},{24,32},{32,40},{40,48},{48,56},{56,64},{64,7... | collective-permute-start | bytes 1966088 | tf_op jit(solution)/shard_map/ppermute | solution.py:10
  29.1 34.4 %collective-permute-start.2 = (f32[1,10,128,128]{3,2,1,0:T(8,128)}, f32[1,10,128,128]{3,2,1,0:T(8,128)}, u32[]{:S(2)}, u32[]{:S(2)}) collective-permute-start(f32[1,10,128,128]{3,2,1,0:T(8,128)} %param.4), channel_id=1, source_target_pairs={{0,1016},{8,0},{16,8},{24,16},{32,24},{40,32},{48,40},{56,48},{64,... | collective-permute-start | bytes 1966088 | tf_op jit(solution)/shard_map/ppermute | solution.py:10
  31.4 43.4 %collective-permute-start.3 = (f32[1,10,128,128]{3,2,1,0:T(8,128)}, f32[1,10,128,128]{3,2,1,0:T(8,128)}, u32[]{:S(2)}, u32[]{:S(2)}) collective-permute-start(f32[1,10,128,128]{3,2,1,0:T(8,128)} %param.4), channel_id=1, source_target_pairs={{0,1008},{8,1016},{16,0},{24,8},{32,16},{40,24},{48,32},{56,40},{6... | collective-permute-start | bytes 1966088 | tf_op jit(solution)/shard_map/ppermute | solution.py:10
  49.9 192.9 %all-to-all-start = ((f32[1,2,8,128,128]{4,3,1,0,2:T(8,128)}), f32[1,2,8,128,128]{4,3,1,0,2:T(8,128)}, u32[]{:S(2)}, u32[]{:S(2)}) async-start(f32[1,2,8,128,128]{4,3,1,0,2:T(8,128)} %copy.28), calls=%async_computation | async-start | bytes 2097152 | tf_op jit(solution)/shard_map/all_to_all | solution.py:45
  57.8 345.5 %reduce-scatter.2.cloned.1.call-start = ((), (), s32[]{:S(2)}) async-start(), calls=%async_computation.2 | async-start | bytes 5898240 | tf_op jit(solution)/shard_map/reduce_scatter | solution.py:56
  82.3 4.0 copy-start.1
  244.1 12.7 %copy-start = (f32[8,10,128,128]{3,1,2,0:T(8,128)S(1)}, f32[8,10,128,128]{3,1,2,0:T(8,128)}, u32[]{:S(2)}) copy-start(f32[8,10,128,128]{3,1,2,0:T(8,128)} %fusion.2) | copy-start | bytes 15728644
Sparse Core Ops, SparseCore 0:
  267.2 136.1 reduce-scatter.1
where the time goes:
time: 413 us; the launch traced here: 412 us
  waiting for transfers between devices  277 us (67%)
  starting transfers between devices  49 us (12%)
  matrix products  47.4 us (11%)
  local copies, waits for them, and re-layouts  20.2 us (5%)
  between operations  13.6 us (3%)
  other arithmetic  4.69 us (1%)
    reduce_scatter x1, waiting for transfers between devices, body(): return lax.psum_scatter(total, 'depth', scatter_dimension=0, tiled=True)  136 us
    all_to_all x1, waiting for transfers between devices, body(): lax.all_to_all(padded, 'depth', split_axis=2, concat_axis=0, tiled=True)  131 us
    ppermute x4, starting transfers between devices, from_behind(): return lax.ppermute(value, axis, pairs)  41 us
    dot_general x2, matrix products, body(): jnp.einsum('lro,lrbc->lobc', matched[:, turn], partner, precision=lax.Pre...  24.5 us
    dot_general x2, matrix products, body(): jnp.einsum('lab,lobc->loac', operand[:, turn], chosen, precision=lax.Prec...  22.9 us
    ppermute x4, waiting for transfers between devices, from_behind(): return lax.ppermute(value, axis, pairs)  10.2 us
  transfers between devices with their start and end apart: 6, of which 3 were waited for; matrix products, arithmetic and copies ran while one was open for 11% of the time, Pallas kernels for 0%

commit v1 on v0

v1 whole, which is shorter than its diff:
```python
import functools

import jax
import jax.numpy as jnp
from jax import lax
from jax.experimental import pallas as pl
from jax.experimental.pallas import tpu as pltpu
from jax.sharding import PartitionSpec as P


def ring_pairs(depth, chips, steps):
    pairs = []
    for chip in chips:
        for core in range(2):
            to = (chip + (steps if core == 0 else -steps)) % (2 * depth)
            pairs.append(
                (
                    (chip // depth * 2 + core) * depth + chip % depth,
                    (to // depth * 2 + core) * depth + to % depth,
                )
            )
    return pairs


def flip_pairs(depth):
    return [(n, n ^ depth) for n in range(4 * depth)]


def ghost_pairs(lines, depth, flip):
    pairs = []
    for line in range(lines):
        for n in range(4 * depth):
            other = (line - 1 if n < 2 * depth else line + 1) % lines
            pairs.append((line * 4 * depth + n, other * 4 * depth + (n ^ depth if flip else n)))
    return pairs


def split(value):
    high = value.astype(jnp.bfloat16)
    return high, (value - high.astype(jnp.float32)).astype(jnp.bfloat16)


def step_kernel(depth, slots, step, rows, targets, fresh, info, *refs):
    held, refs = refs[: len(rows)], refs[len(rows) :]
    factors, refs = refs[: len(targets)], refs[len(targets) :]
    if not fresh:
        refs = refs[len(targets) :]
    sums, refs = refs[: len(targets)], refs[len(targets) :]
    row_buf, factor_buf, sum_buf, row_sem, factor_sem, sum_sem = refs

    place, core = info[0], info[1]
    half, low = place // depth, place % depth
    there = (place + 2 * depth - step + 2 * step * core) % (2 * depth)
    cls = there % depth
    line_rows = 4 * depth

    def column(row, slot):
        return info[2 + row * slots + slot]

    def held_row(which):
        q = core + which * (1 - 2 * core)
        return line_rows + 2 * depth * (there // depth) + depth * q + cls

    def target_row(which):
        q = core + (which % 2) * (1 - 2 * core)
        mine = line_rows + 2 * depth * half + depth * q + low
        return mine + (line_rows - 2 * line_rows * half if which >= 2 else 0)

    def find(k, i):
        more = jnp.minimum(cls + depth, slots - 1)
        first = column(i, cls) == k
        second = jnp.logical_and(cls + depth < slots, column(i, more) == k)
        return jnp.logical_or(first, second), jnp.where(first, cls, more)

    k_of = [held_row(r) for r in rows]
    i_of = [target_row(t) for t in targets]
    found = [[find(k, i) for i in i_of] for k in k_of]
    row_used = [functools.reduce(jnp.logical_or, [f[0] for f in per]) for per in found]
    sum_used = [
        functools.reduce(jnp.logical_or, [found[r][t][0] for r in range(len(rows))])
        for t in range(len(targets))
    ]

    def row_copy(r):
        return pltpu.make_async_copy(held[r], row_buf.at[r], row_sem.at[r])

    def factor_copy(r, t):
        n = r * len(targets) + t
        return pltpu.make_async_copy(
            factors[t].at[found[r][t][1]], factor_buf.at[n], factor_sem.at[n]
        )

    def sum_load(t):
        return pltpu.make_async_copy(sums[t], sum_buf.at[t], sum_sem.at[t])

    def sum_store(t):
        return pltpu.make_async_copy(sum_buf.at[t], sums[t], sum_sem.at[t])

    for phase in ("start", "wait"):
        for r in range(len(rows)):
            pl.when(row_used[r])(getattr(row_copy(r), phase))
            for t in range(len(targets)):
                pl.when(found[r][t][0])(getattr(factor_copy(r, t), phase))
        if not fresh:
            for t in range(len(targets)):
                pl.when(sum_used[t])(getattr(sum_load(t), phase))
        elif phase == "start":
            for t in range(len(targets)):
                sum_buf[t] = jnp.zeros(sum_buf.shape[1:], jnp.float32)

    def select(options, n):
        out = options[0]
        for m in range(1, len(options)):
            out = jnp.where(n == m, options[m], out)
        return out

    def product(n, carry):
        r, t = n // len(targets), n % len(targets)
        k, i = select(k_of, r), select(i_of, t)

        @pl.when(find(k, i)[0])
        def _():
            a_high, a_low = split(factor_buf[n])
            for pair in range(0, slots, 2):
                blocks = []
                for o in (pair, pair + 1):
                    goal = column(i, o)
                    match, where = column(k, o) == goal, o
                    twin = o + depth if o + depth < slots else o - depth
                    if twin >= 0:
                        second = column(k, twin) == goal
                        match, where = jnp.logical_or(match, second), jnp.where(second, twin, o)
                    block = row_buf[r, where]
                    blocks.append(jnp.where(match, block, jnp.zeros_like(block)))
                b_high, b_low = split(jnp.concatenate(blocks, axis=1))
                dot = functools.partial(jnp.dot, preferred_element_type=jnp.float32)
                part = dot(a_high, b_high) + (dot(a_high, b_low) + dot(a_low, b_high))
                edge = part.shape[0]
                sum_buf[t, pair] += part[:, :edge]
                sum_buf[t, pair + 1] += part[:, edge:]

        return carry

    lax.fori_loop(0, len(rows) * len(targets), product, 0)

    for phase in ("start", "wait"):
        for t in range(len(targets)):
            if fresh:
                getattr(sum_store(t), phase)()
            else:
                pl.when(sum_used[t])(getattr(sum_store(t), phase))


def step_call(depth, step, rows, targets, info, held, factors, sums=None):
    slots, edge = held[0].shape[:2]
    fresh = sums is None
    shape = jax.ShapeDtypeStruct(held[0].shape, jnp.float32)
    hbm = pl.BlockSpec(memory_space=pl.ANY)
    operands = [info, *held, *factors] + ([] if fresh else list(sums))
    first = 1 + len(held) + len(factors)
    count = len(rows) * len(targets)
    return pl.pallas_call(
        functools.partial(step_kernel, depth, slots, step, rows, targets, fresh),
        out_shape=[shape] * len(targets),
        in_specs=[pl.BlockSpec(memory_space=pltpu.SMEM)] + [hbm] * (len(operands) - 1),
        out_specs=[hbm] * len(targets),
        input_output_aliases={} if fresh else {first + t: t for t in range(len(targets))},
        scratch_shapes=[
            pltpu.VMEM((len(rows), *shape.shape), jnp.float32),
            pltpu.VMEM((count, edge, edge), jnp.float32),
            pltpu.VMEM((len(targets), *shape.shape), jnp.float32),
            pltpu.SemaphoreType.DMA((len(rows),)),
            pltpu.SemaphoreType.DMA((count,)),
            pltpu.SemaphoreType.DMA((len(targets),)),
        ],
        compiler_params=pltpu.CompilerParams(vmem_limit_bytes=24 << 20),
        cost_estimate=pl.CostEstimate(
            flops=200_000_000, bytes_accessed=8_000_000, transcendentals=0
        ),
        name="products",
    )(*operands)


def body(blocks, columns):
    depth = lax.axis_size("depth")
    lines = lax.axis_size("row")
    block_rows, slots = columns.shape
    line_rows = 4 * depth
    ring, every = ("col", "depth"), ("row", "col", "depth")
    col = lax.axis_index("col")
    place = (col // 2) * depth + lax.axis_index("depth")
    base = (lax.axis_index("row") - 1) * line_rows + block_rows
    near = jnp.take(columns, (base + jnp.arange(3 * line_rows)) % block_rows, axis=0)
    near = (near - base + 2 * block_rows) % block_rows
    info = jnp.concatenate(
        [jnp.stack([place, col % 2]).astype(jnp.int32), near.reshape(-1)]
    )

    own = blocks[0]
    chips = range(2 * depth)
    onward = ring_pairs(depth, chips, 1)
    last = [p for p in onward if p[1] % depth < slots - depth]
    homeward = [(b, a) for a, b in ghost_pairs(lines, depth, False)]
    homeward_flip = [(b, a) for a, b in ghost_pairs(lines, depth, True)]

    held = [own, lax.ppermute(own, ring, flip_pairs(depth))]
    ghost = lax.ppermute(own, every, ghost_pairs(lines, depth, False))
    ghost_flip = lax.ppermute(own, every, ghost_pairs(lines, depth, True))
    factors = [held[0], held[1], ghost, ghost_flip]
    (mine,) = step_call(depth, 0, (0, 1), (0,), info, held, factors[:1])
    sums = [mine] + [jnp.zeros_like(own) for _ in range(3)]
    held = [lax.ppermute(h, ring, onward) for h in held]
    for step in range(1, depth):
        held[0], sums = lax.optimization_barrier((held[0], sums))
        if step < depth - 1:
            after = [lax.ppermute(h, ring, onward) for h in held]
        else:
            after = [lax.ppermute(held[1], ring, last)]
        sums = list(step_call(depth, step, (0, 1), (0, 1, 2, 3), info, held, factors, sums))
        held = after
    sums[0], sums[2] = step_call(
        depth, depth, (1,), (0, 2), info, held, [factors[0], factors[2]], [sums[0], sums[2]]
    )
    total = sums[0] + lax.ppermute(sums[1], ring, flip_pairs(depth))
    total = total + lax.ppermute(sums[2], every, homeward)
    total = total + lax.ppermute(sums[3], every, homeward_flip)
    return total[None]


def solution(mesh):
    placed = (P(("row", "col", "depth"), None, None, None), P())
    return jax.shard_map(
        body,
        mesh=mesh,
        in_specs=placed,
        out_specs=P(("row", "col", "depth"), None, None, None),
        check_vma=False,
    )
```

time: 413 us -> 176 us (0.43)
  waiting for transfers between devices: 277 us -> 51.6 us
  matrix products: 47.4 us -> 0 us
  starting transfers between devices: 49 us -> 94.9 us
  Pallas kernels: 0 us -> 23.5 us
  local copies, waits for them, and re-layouts: 20.2 us -> 3.79 us
  between operations: 13.6 us -> 0.43 us
    reduce_scatter x1 -> x0, waiting for transfers between devices: 136 us -> none  [body(): return lax.psum_scatter(total, 'depth', scatter_dimension=0, tiled=True)]
    all_to_all x1 -> x0, waiting for transfers between devices: 131 us -> none  [body(): lax.all_to_all(padded, 'depth', split_axis=2, concat_axis=0, tiled=True)]
    ppermute x4 -> x21, starting transfers between devices: 41 us -> 94.9 us  [the longest x12 53 us: body(): after = [lax.ppermute(h, ring, onward) for h in held]]
    dot_general x4 -> x0, matrix products: 47.4 us -> none  [the longest x2 24.5 us: body(): jnp.einsum('lro,lrbc->lobc', matched[:, turn], partner, precision=lax.Pre...]
    ppermute x4 -> x21, waiting for transfers between devices: 10.2 us -> 51.6 us  [the longest x1 16.4 us: body(): total = total + lax.ppermute(sums[3], every, homeward_flip)]
    pallas_call x0 -> x9, Pallas kernels: none -> 23.5 us  [step_call(): pl.pallas_call(functools.partial(step_kernel, depth, slots, step, rows, t...]
    all_to_all x1 -> x0, starting transfers between devices: 7.93 us -> none  [body(): lax.all_to_all(padded, 'depth', split_axis=2, concat_axis=0, tiled=True)]
    gather x4 -> x1, local copies, waits for them, and re-layouts: 7.52 us -> 1.66 us  [body(): jnp.take(columns, (base + jnp.arange(3 * line_rows)) % block_rows, axis=0)]
  transfers between devices with their start and end apart: 6 -> 21, of which waited for: 3 -> 11; matrix products, arithmetic and copies ran while one was open for 11% -> 2% of each run, Pallas kernels for 0% -> 13%
where the time goes in v1:
time: 176 us; the launch traced here: 175 us
  starting transfers between devices  94.9 us (54%)
  waiting for transfers between devices  51.6 us (29%)
  Pallas kernels  23.5 us (13%)
  local copies, waits for them, and re-layouts  3.79 us (2%)
    ppermute x12, starting transfers between devices, body(): after = [lax.ppermute(h, ring, onward) for h in held]  53 us
    pallas_call x9, Pallas kernels, step_call(): pl.pallas_call(functools.partial(step_kernel, depth, slots, step, rows, t...  23.5 us
    ppermute x1, waiting for transfers between devices, body(): total = total + lax.ppermute(sums[3], every, homeward_flip)  16.4 us
    ppermute x1, starting transfers between devices, body(): held = [own, lax.ppermute(own, ring, flip_pairs(depth))]  16.2 us
    ppermute x12, waiting for transfers between devices, body(): after = [lax.ppermute(h, ring, onward) for h in held]  15.8 us
    ppermute x1, waiting for transfers between devices, body(): total = total + lax.ppermute(sums[2], every, homeward)  13.1 us
    ppermute x2, starting transfers between devices, body(): held = [lax.ppermute(h, ring, onward) for h in held]  7.46 us
    ppermute x1, starting transfers between devices, body(): ghost = lax.ppermute(own, every, ghost_pairs(lines, depth, False))  7.29 us
  transfers between devices with their start and end apart: 21, of which 11 were waited for; matrix products, arithmetic and copies ran while one was open for 2% of the time, Pallas kernels for 13%

profile of v1, /device:TPU:1, one launch (start us, length us, event | category | flops | bytes accessed | tf_op | source)
XLA Modules:
  0.0 175.4 jit_solution(12588980877284804765)
XLA Ops:
  0.0 0.0 copy-start
  0.0 16.2 %collective-permute-start = (f32[10,128,128]{2,1,0:T(8,128)}, f32[10,128,128]{2,1,0:T(8,128)S(1)}, u32[]{:S(2)}, u32[]{:S(2)}) collective-permute-start(f32[10,128,128]{2,1,0:T(8,128)} %bitcast.7), channel_id=1, source_target_pairs={{0,8},{1,9},{2,10},{3,11},{4,12},{5,13},{6,14},{7,15},{8,0},{9,1},... | collective-permute-start | bytes 1966088 | tf_op jit(solution)/shard_map/ppermute | solution.py:206
  16.2 1.9 %collective-permute-done.refs_1_.refs_3_ = f32[10,128,128]{2,1,0:T(8,128)S(1)} collective-permute-done((f32[10,128,128]{2,1,0:T(8,128)}, f32[10,128,128]{2,1,0:T(8,128)S(1)}, u32[]{:S(2)}, u32[]{:S(2)}) %collective-permute-start) | collective-permute-done | bytes 655392 | tf_op jit(solution)/shard_map/ppermute | solution.py:206
  18.1 5.3 %collective-permute-start.1 = (f32[10,128,128]{2,1,0:T(8,128)S(1)}, f32[10,128,128]{2,1,0:T(8,128)}, u32[]{:S(2)}, u32[]{:S(2)}) collective-permute-start(f32[10,128,128]{2,1,0:T(8,128)S(1)} %collective-permute-done.refs_1_.refs_3_), channel_id=1, source_target_pairs={{0,1},{8,31},{1,2},{9,8},{2,3},{10,9},{3,4},{11,10},{4,5},{12,11},... | collective-permute-start | bytes 1966088 | tf_op jit(solution)/shard_map/ppermute | solution.py:212
  23.4 2.2 %collective-permute-start.10 = (f32[10,128,128]{2,1,0:T(8,128)}, f32[10,128,128]{2,1,0:T(8,128)S(1)}, u32[]{:S(2)}, u32[]{:S(2)}) collective-permute-start(f32[10,128,128]{2,1,0:T(8,128)} %bitcast.8), channel_id=1, source_target_pairs={{0,1},{8,31},{1,2},{9,8},{2,3},{10,9},{3,4},{11,10},{4,5},{12,11},... | collective-permute-start | bytes 1966088 | tf_op jit(solution)/shard_map/ppermute | solution.py:212
  25.6 7.3 %collective-permute-start.9 = (f32[10,128,128]{2,1,0:T(8,128)}, f32[10,128,128]{2,1,0:T(8,128)S(1)}, u32[]{:S(2)}, u32[]{:S(2)}) collective-permute-start(f32[10,128,128]{2,1,0:T(8,128)} %bitcast.9), channel_id=1, source_target_pairs={{0,992},{1,993},{2,994},{3,995},{4,996},{5,997},{6,998},{7,999},{8... | collective-permute-start | bytes 1966088 | tf_op jit(solution)/shard_map/ppermute | solution.py:207
  32.9 1.9 %collective-permute-start.12 = (f32[10,128,128]{2,1,0:T(8,128)}, f32[10,128,128]{2,1,0:T(8,128)S(1)}, u32[]{:S(2)}, u32[]{:S(2)}) collective-permute-start(f32[10,128,128]{2,1,0:T(8,128)} %bitcast.10), channel_id=1, source_target_pairs={{0,1000},{1,1001},{2,1002},{3,1003},{4,1004},{5,1005},{6,1006},{7,... | collective-permute-start | bytes 1966088 | tf_op jit(solution)/shard_map/ppermute | solution.py:208
  34.9 0.0 collective-permute-done.1.refs_1_
  34.9 1.9 %collective-permute-start.2 = (f32[10,128,128]{2,1,0:T(8,128)}, f32[10,128,128]{2,1,0:T(8,128)}, u32[]{:S(2)}, u32[]{:S(2)}) collective-permute-start(f32[10,128,128]{2,1,0:T(8,128)} %collective-permute-done.1.refs_1_), channel_id=1, source_target_pairs={{0,1},{8,31},{1,2},{9,8},{2,3},{10,9},{3,4},{11,10},{4,5},{12,11},... | collective-permute-start | bytes 1966088 | tf_op jit(solution)/shard_map/ppermute | solution.py:216
  36.8 1.9 %copy.34 = s32[1024,10]{1,0:T(8,128)} copy(s32[1024,10]{0,1:T(8,128)} %param.3) | data formatting | bytes 81920 | tf_op args[1]
  38.7 1.7 gather_fusion
  40.3 0.1 subtract_add_fusion
  40.4 0.1 add.104
  40.6 0.1 pad_add_fusion.info
  40.7 0.0 copy-done
  40.7 1.7 products.9.refs_6_
  42.4 0.0 collective-permute-done.10.refs_0_
  42.4 1.9 %collective-permute-start.11 = (f32[10,128,128]{2,1,0:T(8,128)S(1)}, f32[10,128,128]{2,1,0:T(8,128)S(1)}, u32[]{:S(2)}, u32[]{:S(2)}) collective-permute-start(f32[10,128,128]{2,1,0:T(8,128)S(1)} %collective-permute-done.10.refs_0_), channel_id=1, source_target_pairs={{0,1},{8,31},{1,2},{9,8},{2,3},{10,9},{3,4},{11,10},{4,5},{12,11},... | collective-permute-start | bytes 1966088 | tf_op jit(solution)/shard_map/ppermute | solution.py:216
  44.3 2.5 %collective-permute-done.2.refs_1_ = f32[10,128,128]{2,1,0:T(8,128)} collective-permute-done((f32[10,128,128]{2,1,0:T(8,128)}, f32[10,128,128]{2,1,0:T(8,128)}, u32[]{:S(2)}, u32[]{:S(2)}) %collective-permute-start.2) | collective-permute-done | bytes 655392 | tf_op jit(solution)/shard_map/ppermute | solution.py:216
  46.8 3.5 %collective-permute-start.3 = (f32[10,128,128]{2,1,0:T(8,128)}, f32[10,128,128]{2,1,0:T(8,128)S(1)}, u32[]{:S(2)}, u32[]{:S(2)}) collective-permute-start(f32[10,128,128]{2,1,0:T(8,128)} %collective-permute-done.2.refs_1_), channel_id=1, source_target_pairs={{0,1},{8,31},{1,2},{9,8},{2,3},{10,9},{3,4},{11,10},{4,5},{12,11},... | collective-permute-start | bytes 1966088 | tf_op jit(solution)/shard_map/ppermute | solution.py:216
  50.4 0.0 collective-permute-done.9.refs_4_.refs_2_
  50.4 4.3 %collective-permute-done.12.refs_5_ = f32[10,128,128]{2,1,0:T(8,128)S(1)} collective-permute-done((f32[10,128,128]{2,1,0:T(8,128)}, f32[10,128,128]{2,1,0:T(8,128)S(1)}, u32[]{:S(2)}, u32[]{:S(2)}) %collective-permute-start.12) | collective-permute-done | bytes 655392 | tf_op jit(solution)/shard_map/ppermute | solution.py:208
  54.8 2.7 %products.10 = (f32[10,128,128]{2,1,0:T(8,128)S(1)}, f32[10,128,128]{2,1,0:T(8,128)S(1)}, f32[10,128,128]{2,1,0:T(8,128)S(1)}, f32[10,128,128]{2,1,0:T(8,128)S(1)}) custom-call(s32[962]{0:T(1024)S(1)} %pad_add_fusion.info, ...), custom_call_target="tpu_custom_call", output_to_operand_aliasing={{0}: (7, {}), {1}: (8, {}), {2}: (9, {}), {3}: (10, {})} | custom-call | flops 200000000 | bytes 8000000 | tf_op jit(solution)/shard_map/products/pallas_call | solution.py:162
  57.4 0.0 collective-permute-done.11.refs_0_
  57.4 10.8 %collective-permute-start.13 = (f32[10,128,128]{2,1,0:T(8,128)S(1)}, f32[10,128,128]{2,1,0:T(8,128)S(1)}, u32[]{:S(2)}, u32[]{:S(2)}) collective-permute-start(f32[10,128,128]{2,1,0:T(8,128)S(1)} %collective-permute-done.11.refs_0_), channel_id=1, source_target_pairs={{0,1},{8,31},{1,2},{9,8},{2,3},{10,9},{3,4},{11,10},{4,5},{12,11},... | collective-permute-start | bytes 1966088 | tf_op jit(solution)/shard_map/ppermute | solution.py:216
  68.3 0.0 collective-permute-done.3.refs_1_
  68.3 1.9 %collective-permute-start.4 = (f32[10,128,128]{2,1,0:T(8,128)S(1)}, f32[10,128,128]{2,1,0:T(8,128)S(1)}, u32[]{:S(2)}, u32[]{:S(2)}) collective-permute-start(f32[10,128,128]{2,1,0:T(8,128)S(1)} %collective-permute-done.3.refs_1_), channel_id=1, source_target_pairs={{0,1},{8,31},{1,2},{9,8},{2,3},{10,9},{3,4},{11,10},{4,5},{12,11},... | collective-permute-start | bytes 1966088 | tf_op jit(solution)/shard_map/ppermute | solution.py:216
  70.2 3.7 %products.11 = (f32[10,128,128]{2,1,0:T(8,128)S(1)}, f32[10,128,128]{2,1,0:T(8,128)S(1)}, f32[10,128,128]{2,1,0:T(8,128)S(1)}, f32[10,128,128]{2,1,0:T(8,128)S(1)}) custom-call(s32[962]{0:T(1024)S(1)} %pad_add_fusion.info, ...), custom_call_target="tpu_custom_call", output_to_operand_aliasing={{0}: (7, {}), {1}: (8, {}), {2}: (9, {}), {3}: (10, {})} | custom-call | flops 200000000 | bytes 8000000 | tf_op jit(solution)/shard_map/products/pallas_call | solution.py:162
  73.9 1.8 %collective-permute-done.13.refs_0_ = f32[10,128,128]{2,1,0:T(8,128)S(1)} collective-permute-done((f32[10,128,128]{2,1,0:T(8,128)S(1)}, f32[10,128,128]{2,1,0:T(8,128)S(1)}, u32[]{:S(2)}, u32[]{:S(2)}) %collective-permute-start.13) | collective-permute-done | bytes 655392 | tf_op jit(solution)/shard_map/ppermute | solution.py:216
  75.8 5.0 %collective-permute-start.14 = (f32[10,128,128]{2,1,0:T(8,128)S(1)}, f32[10,128,128]{2,1,0:T(8,128)S(1)}, u32[]{:S(2)}, u32[]{:S(2)}) collective-permute-start(f32[10,128,128]{2,1,0:T(8,128)S(1)} %collective-permute-done.13.refs_0_), channel_id=1, source_target_pairs={{0,1},{8,31},{1,2},{9,8},{2,3},{10,9},{3,4},{11,10},{4,5},{12,11},... | collective-permute-start | bytes 1966088 | tf_op jit(solution)/shard_map/ppermute | solution.py:216
  80.8 2.0 %collective-permute-done.4.refs_1_ = f32[10,128,128]{2,1,0:T(8,128)S(1)} collective-permute-done((f32[10,128,128]{2,1,0:T(8,128)S(1)}, f32[10,128,128]{2,1,0:T(8,128)S(1)}, u32[]{:S(2)}, u32[]{:S(2)}) %collective-permute-start.4) | collective-permute-done | bytes 655392 | tf_op jit(solution)/shard_map/ppermute | solution.py:216
  82.8 5.0 %collective-permute-start.5 = (f32[10,128,128]{2,1,0:T(8,128)S(1)}, f32[10,128,128]{2,1,0:T(8,128)S(1)}, u32[]{:S(2)}, u32[]{:S(2)}) collective-permute-start(f32[10,128,128]{2,1,0:T(8,128)S(1)} %collective-permute-done.4.refs_1_), channel_id=1, source_target_pairs={{0,1},{8,31},{1,2},{9,8},{2,3},{10,9},{3,4},{11,10},{4,5},{12,11},... | collective-permute-start | bytes 1966088 | tf_op jit(solution)/shard_map/ppermute | solution.py:216
  87.8 3.5 %products.12 = (f32[10,128,128]{2,1,0:T(8,128)S(1)}, f32[10,128,128]{2,1,0:T(8,128)S(1)}, f32[10,128,128]{2,1,0:T(8,128)S(1)}, f32[10,128,128]{2,1,0:T(8,128)S(1)}) custom-call(s32[962]{0:T(1024)S(1)} %pad_add_fusion.info, ...), custom_call_target="tpu_custom_call", output_to_operand_aliasing={{0}: (7, {}), {1}: (8, {}), {2}: (9, {}), {3}: (10, {})} | custom-call | flops 200000000 | bytes 8000000 | tf_op jit(solution)/shard_map/products/pallas_call | solution.py:162
  91.3 0.0 collective-permute-done.14.refs_0_
  91.3 3.5 %collective-permute-start.15 = (f32[10,128,128]{2,1,0:T(8,128)S(1)}, f32[10,128,128]{2,1,0:T(8,128)S(1)}, u32[]{:S(2)}, u32[]{:S(2)}) collective-permute-start(f32[10,128,128]{2,1,0:T(8,128)S(1)} %collective-permute-done.14.refs_0_), channel_id=1, source_target_pairs={{0,1},{8,31},{1,2},{9,8},{2,3},{10,9},{3,4},{11,10},{4,5},{12,11},... | collective-permute-start | bytes 1966088 | tf_op jit(solution)/shard_map/ppermute | solution.py:216
  94.8 2.0 %collective-permute-done.5.refs_1_ = f32[10,128,128]{2,1,0:T(8,128)S(1)} collective-permute-done((f32[10,128,128]{2,1,0:T(8,128)S(1)}, f32[10,128,128]{2,1,0:T(8,128)S(1)}, u32[]{:S(2)}, u32[]{:S(2)}) %collective-permute-start.5) | collective-permute-done | bytes 655392 | tf_op jit(solution)/shard_map/ppermute | solution.py:216
  96.9 5.0 %collective-permute-start.6 = (f32[10,128,128]{2,1,0:T(8,128)S(1)}, f32[10,128,128]{2,1,0:T(8,128)S(1)}, u32[]{:S(2)}, u32[]{:S(2)}) collective-permute-start(f32[10,128,128]{2,1,0:T(8,128)S(1)} %collective-permute-done.5.refs_1_), channel_id=1, source_target_pairs={{0,1},{8,31},{1,2},{9,8},{2,3},{10,9},{3,4},{11,10},{4,5},{12,11},... | collective-permute-start | bytes 1966088 | tf_op jit(solution)/shard_map/ppermute | solution.py:216
  101.9 2.3 %products.13 = (f32[10,128,128]{2,1,0:T(8,128)S(1)}, f32[10,128,128]{2,1,0:T(8,128)S(1)}, f32[10,128,128]{2,1,0:T(8,128)S(1)}, f32[10,128,128]{2,1,0:T(8,128)S(1)}) custom-call(s32[962]{0:T(1024)S(1)} %pad_add_fusion.info, ...), custom_call_target="tpu_custom_call", output_to_operand_aliasing={{0}: (7, {}), {1}: (8, {}), {2}: (9, {}), {3}: (10, {})} | custom-call | flops 200000000 | bytes 8000000 | tf_op jit(solution)/shard_map/products/pallas_call | solution.py:162
  104.2 0.0 collective-permute-done.15.refs_0_
  104.2 4.7 %collective-permute-start.16 = (f32[10,128,128]{2,1,0:T(8,128)S(1)}, f32[10,128,128]{2,1,0:T(8,128)S(1)}, u32[]{:S(2)}, u32[]{:S(2)}) collective-permute-start(f32[10,128,128]{2,1,0:T(8,128)S(1)} %collective-permute-done.15.refs_0_), channel_id=1, source_target_pairs={{0,1},{8,31},{1,2},{9,8},{2,3},{10,9},{3,4},{11,10},{4,5},{12,11},... | collective-permute-start | bytes 1966088 | tf_op jit(solution)/shard_map/ppermute | solution.py:216
  108.9 2.0 %collective-permute-done.6.refs_1_ = f32[10,128,128]{2,1,0:T(8,128)S(1)} collective-permute-done((f32[10,128,128]{2,1,0:T(8,128)S(1)}, f32[10,128,128]{2,1,0:T(8,128)S(1)}, u32[]{:S(2)}, u32[]{:S(2)}) %collective-permute-start.6) | collective-permute-done | bytes 655392 | tf_op jit(solution)/shard_map/ppermute | solution.py:216
  110.9 5.0 %collective-permute-start.7 = (f32[10,128,128]{2,1,0:T(8,128)S(1)}, f32[10,128,128]{2,1,0:T(8,128)S(1)}, u32[]{:S(2)}, u32[]{:S(2)}) collective-permute-start(f32[10,128,128]{2,1,0:T(8,128)S(1)} %collective-permute-done.6.refs_1_), channel_id=1, source_target_pairs={{0,1},{8,31},{1,2},{9,8},{2,3},{10,9},{3,4},{11,10},{4,5},{12,11},... | collective-permute-start | bytes 1966088 | tf_op jit(solution)/shard_map/ppermute | solution.py:216
  115.9 2.3 %products.14 = (f32[10,128,128]{2,1,0:T(8,128)S(1)}, f32[10,128,128]{2,1,0:T(8,128)S(1)}, f32[10,128,128]{2,1,0:T(8,128)S(1)}, f32[10,128,128]{2,1,0:T(8,128)S(1)}) custom-call(s32[962]{0:T(1024)S(1)} %pad_add_fusion.info, ...), custom_call_target="tpu_custom_call", output_to_operand_aliasing={{0}: (7, {}), {1}: (8, {}), {2}: (9, {}), {3}: (10, {})} | custom-call | flops 200000000 | bytes 8000000 | tf_op jit(solution)/shard_map/products/pallas_call | solution.py:162
  118.2 0.0 collective-permute-done.16.refs_0_
  118.2 4.7 %collective-permute-start.17 = (f32[10,128,128]{2,1,0:T(8,128)S(1)}, f32[10,128,128]{2,1,0:T(8,128)S(1)}, u32[]{:S(2)}, u32[]{:S(2)}) collective-permute-start(f32[10,128,128]{2,1,0:T(8,128)S(1)} %collective-permute-done.16.refs_0_), channel_id=1, source_target_pairs={{0,1},{8,31},{1,2},{9,8},{2,3},{10,9},{3,4},{11,10},{4,5},{12,11},... | collective-permute-start | bytes 1966088 | tf_op jit(solution)/shard_map/ppermute | solution.py:216
  122.9 2.0 %collective-permute-done.7.refs_1_ = f32[10,128,128]{2,1,0:T(8,128)S(1)} collective-permute-done((f32[10,128,128]{2,1,0:T(8,128)S(1)}, f32[10,128,128]{2,1,0:T(8,128)S(1)}, u32[]{:S(2)}, u32[]{:S(2)}) %collective-permute-start.7) | collective-permute-done | bytes 655392 | tf_op jit(solution)/shard_map/ppermute | solution.py:216
  124.9 1.3 collective-permute-start.8
  126.2 2.3 %products.15 = (f32[10,128,128]{2,1,0:T(8,128)S(1)}, f32[10,128,128]{2,1,0:T(8,128)S(1)}, f32[10,128,128]{2,1,0:T(8,128)S(1)}, f32[10,128,128]{2,1,0:T(8,128)S(1)}) custom-call(s32[962]{0:T(1024)S(1)} %pad_add_fusion.info, ...), custom_call_target="tpu_custom_call", output_to_operand_aliasing={{0}: (7, {}), {1}: (8, {}), {2}: (9, {}), {3}: (10, {})} | custom-call | flops 200000000 | bytes 8000000 | tf_op jit(solution)/shard_map/products/pallas_call | solution.py:162
  128.5 3.4 %collective-permute-done.17.refs_0_ = f32[10,128,128]{2,1,0:T(8,128)S(1)} collective-permute-done((f32[10,128,128]{2,1,0:T(8,128)S(1)}, f32[10,128,128]{2,1,0:T(8,128)S(1)}, u32[]{:S(2)}, u32[]{:S(2)}) %collective-permute-start.17) | collective-permute-done | bytes 655392 | tf_op jit(solution)/shard_map/ppermute | solution.py:216
  132.0 3.3 %products.16 = (f32[10,128,128]{2,1,0:T(8,128)S(1)}, f32[10,128,128]{2,1,0:T(8,128)S(1)}, f32[10,128,128]{2,1,0:T(8,128)S(1)}, f32[10,128,128]{2,1,0:T(8,128)S(1)}) custom-call(s32[962]{0:T(1024)S(1)} %pad_add_fusion.info, ...), custom_call_target="tpu_custom_call", output_to_operand_aliasing={{0}: (7, {}), {1}: (8, {}), {2}: (9, {}), {3}: (10, {})} | custom-call | flops 200000000 | bytes 8000000 | tf_op jit(solution)/shard_map/products/pallas_call | solution.py:162
  135.2 3.9 %collective-permute-start.18 = (f32[10,128,128]{2,1,0:T(8,128)S(1)}, f32[10,128,128]{2,1,0:T(8,128)S(1)}, u32[]{:S(2)}, u32[]{:S(2)}) collective-permute-start(f32[10,128,128]{2,1,0:T(8,128)S(1)} %get-tuple-element.132), channel_id=1, source_target_pairs={{0,8},{1,9},{2,10},{3,11},{4,12},{5,13},{6,14},{7,15},{8,0},{9,1},... | collective-permute-start | bytes 1966088 | tf_op jit(solution)/shard_map/ppermute | solution.py:224
  139.1 1.9 %collective-permute-start.20 = (f32[10,128,128]{2,1,0:T(8,128)S(1)}, f32[10,128,128]{2,1,0:T(8,128)S(1)}, u32[]{:S(2)}, u32[]{:S(2)}) collective-permute-start(f32[10,128,128]{2,1,0:T(8,128)S(1)} %get-tuple-element.134), channel_id=1, source_target_pairs={{1000,0},{1001,1},{1002,2},{1003,3},{1004,4},{1005,5},{1006,6},{10... | collective-permute-start | bytes 1966088 | tf_op jit(solution)/shard_map/ppermute | solution.py:226
  141.0 0.0 collective-permute-done.8.refs_0_
  141.0 1.9 %products.17 = (f32[10,128,128]{2,1,0:T(8,128)S(1)}, f32[10,128,128]{2,1,0:T(8,128)S(1)}) custom-call(s32[962]{0:T(1024)S(1)} %pad_add_fusion.info, f32[10,128,128]{2,1,0:T(8,128)S(1)} %collective-permute-done.8.refs_0_, f32[10,128,128]{2,1,0:T(8,128)S(1)} %bitcast.20, ...), custom_call_target="tpu_custom_call", output_to_operand_aliasing={{0}: (4, {}), {1}: (5, {})} | custom-call | flops 200000000 | bytes 8000000 | tf_op jit(solution)/shard_map/products/pallas_call | solution.py:162
  142.9 1.9 %collective-permute-start.19 = (f32[10,128,128]{2,1,0:T(8,128)S(1)}, f32[10,128,128]{2,1,0:T(8,128)S(1)}, u32[]{:S(2)}, u32[]{:S(2)}) collective-permute-start(f32[10,128,128]{2,1,0:T(8,128)S(1)} %get-tuple-element.133), channel_id=1, source_target_pairs={{992,0},{993,1},{994,2},{995,3},{996,4},{997,5},{998,6},{999,7},{1... | collective-permute-start | bytes 1966088 | tf_op jit(solution)/shard_map/ppermute | solution.py:225
  144.8 0.0 collective-permute-done.18
  144.8 16.4 %collective-permute-done.20 = f32[10,128,128]{2,1,0:T(8,128)S(1)} collective-permute-done((f32[10,128,128]{2,1,0:T(8,128)S(1)}, f32[10,128,128]{2,1,0:T(8,128)S(1)}, u32[]{:S(2)}, u32[]{:S(2)}) %collective-permute-start.20) | collective-permute-done | bytes 655392 | tf_op jit(solution)/shard_map/ppermute | solution.py:226
  161.3 13.1 %collective-permute-done.19 = f32[10,128,128]{2,1,0:T(8,128)S(1)} collective-permute-done((f32[10,128,128]{2,1,0:T(8,128)S(1)}, f32[10,128,128]{2,1,0:T(8,128)S(1)}, u32[]{:S(2)}, u32[]{:S(2)}) %collective-permute-start.19) | collective-permute-done | bytes 655392 | tf_op jit(solution)/shard_map/ppermute | solution.py:225
  174.4 1.0 add_bitcast_fusion
  (7 shorter events, 0.2 us)
Async XLA Ops:
  0.0 40.7 %copy-start = (f32[1,10,128,128]{3,2,1,0:T(8,128)S(1)}, f32[1,10,128,128]{3,2,1,0:T(8,128)}, u32[]{:S(2)}) copy-start(f32[1,10,128,128]{3,2,1,0:T(8,128)} %param.2) | copy-start | bytes 1966084
  0.0 18.1 %collective-permute-start = (f32[10,128,128]{2,1,0:T(8,128)}, f32[10,128,128]{2,1,0:T(8,128)S(1)}, u32[]{:S(2)}, u32[]{:S(2)}) collective-permute-start(f32[10,128,128]{2,1,0:T(8,128)} %bitcast.7), channel_id=1, source_target_pairs={{0,8},{1,9},{2,10},{3,11},{4,12},{5,13},{6,14},{7,15},{8,0},{9,1},... | collective-permute-start | bytes 1966088 | tf_op jit(solution)/shard_map/ppermute | solution.py:206
  18.1 16.7 %collective-permute-start.1 = (f32[10,128,128]{2,1,0:T(8,128)S(1)}, f32[10,128,128]{2,1,0:T(8,128)}, u32[]{:S(2)}, u32[]{:S(2)}) collective-permute-start(f32[10,128,128]{2,1,0:T(8,128)S(1)} %collective-permute-done.refs_1_.refs_3_), channel_id=1, source_target_pairs={{0,1},{8,31},{1,2},{9,8},{2,3},{10,9},{3,4},{11,10},{4,5},{12,11},... | collective-permute-start | bytes 1966088 | tf_op jit(solution)/shard_map/ppermute | solution.py:212
  23.4 19.0 %collective-permute-start.10 = (f32[10,128,128]{2,1,0:T(8,128)}, f32[10,128,128]{2,1,0:T(8,128)S(1)}, u32[]{:S(2)}, u32[]{:S(2)}) collective-permute-start(f32[10,128,128]{2,1,0:T(8,128)} %bitcast.8), channel_id=1, source_target_pairs={{0,1},{8,31},{1,2},{9,8},{2,3},{10,9},{3,4},{11,10},{4,5},{12,11},... | collective-permute-start | bytes 1966088 | tf_op jit(solution)/shard_map/ppermute | solution.py:212
  25.6 24.8 %collective-permute-start.9 = (f32[10,128,128]{2,1,0:T(8,128)}, f32[10,128,128]{2,1,0:T(8,128)S(1)}, u32[]{:S(2)}, u32[]{:S(2)}) collective-permute-start(f32[10,128,128]{2,1,0:T(8,128)} %bitcast.9), channel_id=1, source_target_pairs={{0,992},{1,993},{2,994},{3,995},{4,996},{5,997},{6,998},{7,999},{8... | collective-permute-start | bytes 1966088 | tf_op jit(solution)/shard_map/ppermute | solution.py:207
  32.9 21.9 %collective-permute-start.12 = (f32[10,128,128]{2,1,0:T(8,128)}, f32[10,128,128]{2,1,0:T(8,128)S(1)}, u32[]{:S(2)}, u32[]{:S(2)}) collective-permute-start(f32[10,128,128]{2,1,0:T(8,128)} %bitcast.10), channel_id=1, source_target_pairs={{0,1000},{1,1001},{2,1002},{3,1003},{4,1004},{5,1005},{6,1006},{7,... | collective-permute-start | bytes 1966088 | tf_op jit(solution)/shard_map/ppermute | solution.py:208
  34.9 11.9 %collective-permute-start.2 = (f32[10,128,128]{2,1,0:T(8,128)}, f32[10,128,128]{2,1,0:T(8,128)}, u32[]{:S(2)}, u32[]{:S(2)}) collective-permute-start(f32[10,128,128]{2,1,0:T(8,128)} %collective-permute-done.1.refs_1_), channel_id=1, source_target_pairs={{0,1},{8,31},{1,2},{9,8},{2,3},{10,9},{3,4},{11,10},{4,5},{12,11},... | collective-permute-start | bytes 1966088 | tf_op jit(solution)/shard_map/ppermute | solution.py:216
  42.4 15.0 %collective-permute-start.11 = (f32[10,128,128]{2,1,0:T(8,128)S(1)}, f32[10,128,128]{2,1,0:T(8,128)S(1)}, u32[]{:S(2)}, u32[]{:S(2)}) collective-permute-start(f32[10,128,128]{2,1,0:T(8,128)S(1)} %collective-permute-done.10.refs_0_), channel_id=1, source_target_pairs={{0,1},{8,31},{1,2},{9,8},{2,3},{10,9},{3,4},{11,10},{4,5},{12,11},... | collective-permute-start | bytes 1966088 | tf_op jit(solution)/shard_map/ppermute | solution.py:216
  46.8 21.5 %collective-permute-start.3 = (f32[10,128,128]{2,1,0:T(8,128)}, f32[10,128,128]{2,1,0:T(8,128)S(1)}, u32[]{:S(2)}, u32[]{:S(2)}) collective-permute-start(f32[10,128,128]{2,1,0:T(8,128)} %collective-permute-done.2.refs_1_), channel_id=1, source_target_pairs={{0,1},{8,31},{1,2},{9,8},{2,3},{10,9},{3,4},{11,10},{4,5},{12,11},... | collective-permute-start | bytes 1966088 | tf_op jit(solution)/shard_map/ppermute | solution.py:216
  57.4 18.4 %collective-permute-start.13 = (f32[10,128,128]{2,1,0:T(8,128)S(1)}, f32[10,128,128]{2,1,0:T(8,128)S(1)}, u32[]{:S(2)}, u32[]{:S(2)}) collective-permute-start(f32[10,128,128]{2,1,0:T(8,128)S(1)} %collective-permute-done.11.refs_0_), channel_id=1, source_target_pairs={{0,1},{8,31},{1,2},{9,8},{2,3},{10,9},{3,4},{11,10},{4,5},{12,11},... | collective-permute-start | bytes 1966088 | tf_op jit(solution)/shard_map/ppermute | solution.py:216
  68.3 14.5 %collective-permute-start.4 = (f32[10,128,128]{2,1,0:T(8,128)S(1)}, f32[10,128,128]{2,1,0:T(8,128)S(1)}, u32[]{:S(2)}, u32[]{:S(2)}) collective-permute-start(f32[10,128,128]{2,1,0:T(8,128)S(1)} %collective-permute-done.3.refs_1_), channel_id=1, source_target_pairs={{0,1},{8,31},{1,2},{9,8},{2,3},{10,9},{3,4},{11,10},{4,5},{12,11},... | collective-permute-start | bytes 1966088 | tf_op jit(solution)/shard_map/ppermute | solution.py:216
  75.8 15.5 %collective-permute-start.14 = (f32[10,128,128]{2,1,0:T(8,128)S(1)}, f32[10,128,128]{2,1,0:T(8,128)S(1)}, u32[]{:S(2)}, u32[]{:S(2)}) collective-permute-start(f32[10,128,128]{2,1,0:T(8,128)S(1)} %collective-permute-done.13.refs_0_), channel_id=1, source_target_pairs={{0,1},{8,31},{1,2},{9,8},{2,3},{10,9},{3,4},{11,10},{4,5},{12,11},... | collective-permute-start | bytes 1966088 | tf_op jit(solution)/shard_map/ppermute | solution.py:216
  82.8 14.0 %collective-permute-start.5 = (f32[10,128,128]{2,1,0:T(8,128)S(1)}, f32[10,128,128]{2,1,0:T(8,128)S(1)}, u32[]{:S(2)}, u32[]{:S(2)}) collective-permute-start(f32[10,128,128]{2,1,0:T(8,128)S(1)} %collective-permute-done.4.refs_1_), channel_id=1, source_target_pairs={{0,1},{8,31},{1,2},{9,8},{2,3},{10,9},{3,4},{11,10},{4,5},{12,11},... | collective-permute-start | bytes 1966088 | tf_op jit(solution)/shard_map/ppermute | solution.py:216
  91.3 12.9 %collective-permute-start.15 = (f32[10,128,128]{2,1,0:T(8,128)S(1)}, f32[10,128,128]{2,1,0:T(8,128)S(1)}, u32[]{:S(2)}, u32[]{:S(2)}) collective-permute-start(f32[10,128,128]{2,1,0:T(8,128)S(1)} %collective-permute-done.14.refs_0_), channel_id=1, source_target_pairs={{0,1},{8,31},{1,2},{9,8},{2,3},{10,9},{3,4},{11,10},{4,5},{12,11},... | collective-permute-start | bytes 1966088 | tf_op jit(solution)/shard_map/ppermute | solution.py:216
  96.9 14.0 %collective-permute-start.6 = (f32[10,128,128]{2,1,0:T(8,128)S(1)}, f32[10,128,128]{2,1,0:T(8,128)S(1)}, u32[]{:S(2)}, u32[]{:S(2)}) collective-permute-start(f32[10,128,128]{2,1,0:T(8,128)S(1)} %collective-permute-done.5.refs_1_), channel_id=1, source_target_pairs={{0,1},{8,31},{1,2},{9,8},{2,3},{10,9},{3,4},{11,10},{4,5},{12,11},... | collective-permute-start | bytes 1966088 | tf_op jit(solution)/shard_map/ppermute | solution.py:216
  104.2 14.0 %collective-permute-start.16 = (f32[10,128,128]{2,1,0:T(8,128)S(1)}, f32[10,128,128]{2,1,0:T(8,128)S(1)}, u32[]{:S(2)}, u32[]{:S(2)}) collective-permute-start(f32[10,128,128]{2,1,0:T(8,128)S(1)} %collective-permute-done.15.refs_0_), channel_id=1, source_target_pairs={{0,1},{8,31},{1,2},{9,8},{2,3},{10,9},{3,4},{11,10},{4,5},{12,11},... | collective-permute-start | bytes 1966088 | tf_op jit(solution)/shard_map/ppermute | solution.py:216
  110.9 14.0 %collective-permute-start.7 = (f32[10,128,128]{2,1,0:T(8,128)S(1)}, f32[10,128,128]{2,1,0:T(8,128)S(1)}, u32[]{:S(2)}, u32[]{:S(2)}) collective-permute-start(f32[10,128,128]{2,1,0:T(8,128)S(1)} %collective-permute-done.6.refs_1_), channel_id=1, source_target_pairs={{0,1},{8,31},{1,2},{9,8},{2,3},{10,9},{3,4},{11,10},{4,5},{12,11},... | collective-permute-start | bytes 1966088 | tf_op jit(solution)/shard_map/ppermute | solution.py:216
  118.2 13.7 %collective-permute-start.17 = (f32[10,128,128]{2,1,0:T(8,128)S(1)}, f32[10,128,128]{2,1,0:T(8,128)S(1)}, u32[]{:S(2)}, u32[]{:S(2)}) collective-permute-start(f32[10,128,128]{2,1,0:T(8,128)S(1)} %collective-permute-done.16.refs_0_), channel_id=1, source_target_pairs={{0,1},{8,31},{1,2},{9,8},{2,3},{10,9},{3,4},{11,10},{4,5},{12,11},... | collective-permute-start | bytes 1966088 | tf_op jit(solution)/shard_map/ppermute | solution.py:216
  124.9 16.1 %collective-permute-start.8 = (f32[10,128,128]{2,1,0:T(8,128)S(1)}, f32[10,128,128]{2,1,0:T(8,128)S(1)}, u32[]{:S(2)}, u32[]{:S(2)}) collective-permute-start(f32[10,128,128]{2,1,0:T(8,128)S(1)} %collective-permute-done.7.refs_1_), channel_id=1, source_target_pairs={{0,1},{9,8},{10,9},{7,16},{16,17},{25,24},{26,25},{23,0},{32,33},{... | collective-permute-start | bytes 1966088 | tf_op jit(solution)/shard_map/ppermute | solution.py:218
  135.2 9.6 %collective-permute-start.18 = (f32[10,128,128]{2,1,0:T(8,128)S(1)}, f32[10,128,128]{2,1,0:T(8,128)S(1)}, u32[]{:S(2)}, u32[]{:S(2)}) collective-permute-start(f32[10,128,128]{2,1,0:T(8,128)S(1)} %get-tuple-element.132), channel_id=1, source_target_pairs={{0,8},{1,9},{2,10},{3,11},{4,12},{5,13},{6,14},{7,15},{8,0},{9,1},... | collective-permute-start | bytes 1966088 | tf_op jit(solution)/shard_map/ppermute | solution.py:224
  139.1 22.2 %collective-permute-start.20 = (f32[10,128,128]{2,1,0:T(8,128)S(1)}, f32[10,128,128]{2,1,0:T(8,128)S(1)}, u32[]{:S(2)}, u32[]{:S(2)}) collective-permute-start(f32[10,128,128]{2,1,0:T(8,128)S(1)} %get-tuple-element.134), channel_id=1, source_target_pairs={{1000,0},{1001,1},{1002,2},{1003,3},{1004,4},{1005,5},{1006,6},{10... | collective-permute-start | bytes 1966088 | tf_op jit(solution)/shard_map/ppermute | solution.py:226
  142.9 31.5 %collective-permute-start.19 = (f32[10,128,128]{2,1,0:T(8,128)S(1)}, f32[10,128,128]{2,1,0:T(8,128)S(1)}, u32[]{:S(2)}, u32[]{:S(2)}) collective-permute-start(f32[10,128,128]{2,1,0:T(8,128)S(1)} %get-tuple-element.133), channel_id=1, source_target_pairs={{992,0},{993,1},{994,2},{995,3},{996,4},{997,5},{998,6},{999,7},{1... | collective-permute-start | bytes 1966088 | tf_op jit(solution)/shard_map/ppermute | solution.py:225

commit v2 on v1

v2 whole, which is shorter than its diff:
```python
import functools

import jax
import jax.numpy as jnp
from jax import lax
from jax.experimental import pallas as pl
from jax.experimental.pallas import tpu as pltpu
from jax.sharding import PartitionSpec as P


def device(line, place, core, depth):
    return ((line * 2 + place // depth) * 2 + core) * depth + place % depth


def hop_pairs(lines, depth, step, which, across=False):
    pairs = []
    for line in range(lines):
        for place in range(2 * depth):
            for core in range(2):
                way = 1 - 2 * core
                origin = (place - way * (step - 1)) % (2 * depth)
                to = (place + way) % (2 * depth)
                crosses = place // depth - to // depth if origin // depth == core ^ which else 0
                pairs.append(
                    (
                        device(line, place, core, depth),
                        device((line + crosses) % lines, to, core ^ across, depth),
                    )
                )
    return pairs


def flip_pairs(depth):
    return [(n, n ^ depth) for n in range(4 * depth)]


def line_pairs(lines, depth):
    return [
        (device(line, place, core, depth), device((line - 1 + 2 * core) % lines, place, core, depth))
        for line in range(lines)
        for place in range(2 * depth)
        for core in range(2)
    ]


def split(value):
    high = value.astype(jnp.bfloat16)
    return high, (value - high.astype(jnp.float32)).astype(jnp.bfloat16)


def step_kernel(depth, slots, step, rows, targets, pairs, fresh, info, *refs):
    held, refs = refs[: len(rows)], refs[len(rows) :]
    factors, refs = refs[: len(targets)], refs[len(targets) :]
    if not fresh:
        refs = refs[len(targets) :]
    sums, refs = refs[: len(targets)], refs[len(targets) :]
    row_buf, factor_buf, sum_buf, row_sem, factor_sem, sum_sem = refs

    place, core = info[0], info[1]
    half, low = place // depth, place % depth
    there = (place + 2 * depth - step + 2 * step * core) % (2 * depth)
    origin, cls = there // depth, there % depth
    line_rows = 4 * depth

    def column(row, slot):
        return info[2 + row * slots + slot]

    def held_row(which):
        q = core + which * (1 - 2 * core)
        line = 1 + jnp.where(origin == q, half - origin, 0)
        return line_rows * line + 2 * depth * origin + depth * q + cls

    def target_row(which):
        q = core + (which == 1) * (1 - 2 * core)
        line = 1 + (which == 2) * (1 - 2 * core)
        return line_rows * line + 2 * depth * half + depth * q + low

    def find(k, i):
        more = jnp.minimum(cls + depth, slots - 1)
        first = column(i, cls) == k
        second = jnp.logical_and(cls + depth < slots, column(i, more) == k)
        return jnp.logical_or(first, second), jnp.where(first, cls, more)

    k_of = [held_row(r) for r in rows]
    i_of = [target_row(t) for t in targets]
    found = [find(k_of[r], i_of[t]) for r, t in pairs]

    def any_of(where):
        return functools.reduce(jnp.logical_or, [f[0] for f, p in zip(found, pairs) if where(p)])

    row_used = [any_of(lambda p, r=r: p[0] == r) for r in range(len(rows))]
    sum_used = [any_of(lambda p, t=t: p[1] == t) for t in range(len(targets))]

    def row_copy(r):
        return pltpu.make_async_copy(held[r], row_buf.at[r], row_sem.at[r])

    def factor_copy(n):
        t = pairs[n][1]
        return pltpu.make_async_copy(
            factors[t].at[found[n][1]], factor_buf.at[n], factor_sem.at[n]
        )

    def sum_load(t):
        return pltpu.make_async_copy(sums[t], sum_buf.at[t], sum_sem.at[t])

    def sum_store(t):
        return pltpu.make_async_copy(sum_buf.at[t], sums[t], sum_sem.at[t])

    for phase in ("start", "wait"):
        for r in range(len(rows)):
            pl.when(row_used[r])(getattr(row_copy(r), phase))
        for n in range(len(pairs)):
            pl.when(found[n][0])(getattr(factor_copy(n), phase))
        if not fresh:
            for t in range(len(targets)):
                pl.when(sum_used[t])(getattr(sum_load(t), phase))
        elif phase == "start":
            for t in range(len(targets)):
                sum_buf[t] = jnp.zeros(sum_buf.shape[1:], jnp.float32)

    def select(options, n):
        out = options[0]
        for m in range(1, len(options)):
            out = jnp.where(n == m, options[m], out)
        return out

    def product(n, carry):
        r = select([p[0] for p in pairs], n)
        t = select([p[1] for p in pairs], n)
        k, i = select(k_of, r), select(i_of, t)

        @pl.when(find(k, i)[0])
        def _():
            a_high, a_low = split(factor_buf[n])
            for pair in range(0, slots, 2):
                blocks = []
                for o in (pair, pair + 1):
                    goal = column(i, o)
                    match, where = column(k, o) == goal, o
                    twin = o + depth if o + depth < slots else o - depth
                    if twin >= 0:
                        second = column(k, twin) == goal
                        match, where = jnp.logical_or(match, second), jnp.where(second, twin, o)
                    block = row_buf[r, where]
                    blocks.append(jnp.where(match, block, jnp.zeros_like(block)))
                b_high, b_low = split(jnp.concatenate(blocks, axis=1))
                dot = functools.partial(jnp.dot, preferred_element_type=jnp.float32)
                part = dot(a_high, b_high) + (dot(a_high, b_low) + dot(a_low, b_high))
                edge = part.shape[0]
                sum_buf[t, pair] += part[:, :edge]
                sum_buf[t, pair + 1] += part[:, edge:]

        return carry

    lax.fori_loop(0, len(pairs), product, 0)

    for phase in ("start", "wait"):
        for t in range(len(targets)):
            if fresh:
                getattr(sum_store(t), phase)()
            else:
                pl.when(sum_used[t])(getattr(sum_store(t), phase))


def step_call(depth, step, rows, targets, pairs, info, held, factors, sums=None):
    slots, edge = held[0].shape[:2]
    fresh = sums is None
    shape = jax.ShapeDtypeStruct(held[0].shape, jnp.float32)
    hbm = pl.BlockSpec(memory_space=pl.ANY)
    operands = [info, *held, *factors] + ([] if fresh else list(sums))
    first = 1 + len(held) + len(factors)
    return list(
        pl.pallas_call(
            functools.partial(step_kernel, depth, slots, step, rows, targets, pairs, fresh),
            out_shape=[shape] * len(targets),
            in_specs=[pl.BlockSpec(memory_space=pltpu.SMEM)] + [hbm] * (len(operands) - 1),
            out_specs=[hbm] * len(targets),
            input_output_aliases={} if fresh else {first + t: t for t in range(len(targets))},
            scratch_shapes=[
                pltpu.VMEM((len(rows), *shape.shape), jnp.float32),
                pltpu.VMEM((len(pairs), edge, edge), jnp.float32),
                pltpu.VMEM((len(targets), *shape.shape), jnp.float32),
                pltpu.SemaphoreType.DMA((len(rows),)),
                pltpu.SemaphoreType.DMA((len(pairs),)),
                pltpu.SemaphoreType.DMA((len(targets),)),
            ],
            compiler_params=pltpu.CompilerParams(vmem_limit_bytes=24 << 20),
            cost_estimate=pl.CostEstimate(
                flops=200_000_000, bytes_accessed=8_000_000, transcendentals=0
            ),
            name="products",
        )(*operands)
    )


def body(blocks, columns):
    depth = lax.axis_size("depth")
    lines = lax.axis_size("row")
    block_rows, slots = columns.shape
    line_rows = 4 * depth
    ring, every = ("col", "depth"), ("row", "col", "depth")
    col = lax.axis_index("col")
    place = (col // 2) * depth + lax.axis_index("depth")
    base = (lax.axis_index("row") - 1) * line_rows + block_rows
    near = jnp.take(columns, (base + jnp.arange(3 * line_rows)) % block_rows, axis=0)
    near = (near - base + 2 * block_rows) % block_rows
    info = jnp.concatenate(
        [jnp.stack([place, col % 2]).astype(jnp.int32), near.reshape(-1)]
    )

    def hop(held, step, which):
        return lax.ppermute(held[which], every, hop_pairs(lines, depth, step, which))

    def flip(value):
        return lax.ppermute(value, ring, flip_pairs(depth))

    own = blocks[0]
    held = [own, flip(own)]
    away = line_pairs(lines, depth)
    ghost = lax.ppermute(own, every, away)
    factors = [held[0], held[1], ghost]
    sums = step_call(depth, 0, (0, 1), (0,), ((0, 0), (1, 0)), info, held, factors[:1])
    sums += [jnp.zeros_like(own) for _ in range(2)]
    held = [hop(held, 1, which) for which in range(2)]
    for step in range(1, depth - 1):
        held[0], sums = lax.optimization_barrier((held[0], sums))
        after = [hop(held, step + 1, which) for which in range(2)]
        pairs = ((0, 0), (0, 1), (0, 2), (1, 0), (1, 1))
        sums = step_call(depth, step, (0, 1), (0, 1, 2), pairs, info, held, factors, sums)
        held = after
    last = depth - 1
    held[0], sums = lax.optimization_barrier((held[0], sums))
    far = [
        p for p in hop_pairs(lines, depth, depth, 0, across=True) if p[1] % depth < slots - depth
    ]
    far = lax.ppermute(held[0], every, far)
    (foreign,) = step_call(
        depth, last, (0,), (2,), ((0, 0),), info, held[:1], factors[2:], sums[2:]
    )
    foreign = lax.ppermute(foreign, every, [(b, a) for a, b in away])
    mine, other = step_call(
        depth, last, (0, 1), (0, 1), ((0, 0), (0, 1), (1, 0), (1, 1)), info, held, factors[:2], sums[:2]
    )
    other = flip(other)
    (mine,) = step_call(depth, depth, (1,), (0,), ((0, 0),), info, [far], factors[:1], [mine])
    return (mine + other + foreign)[None]


def solution(mesh):
    placed = (P(("row", "col", "depth"), None, None, None), P())
    return jax.shard_map(
        body,
        mesh=mesh,
        in_specs=placed,
        out_specs=P(("row", "col", "depth"), None, None, None),
        check_vma=False,
    )
```

time: 176 us -> 158 us (0.90)
  waiting for transfers between devices: 51.6 us -> 15.8 us
  starting transfers between devices: 94.9 us -> 113 us
    ppermute x21 -> x19, waiting for transfers between devices: 51.6 us -> 15.8 us  [the longest x14 15.7 us: hop(): lax.ppermute(held[which], every, hop_pairs(lines, depth, step, which))]
    ppermute x21 -> x19, starting transfers between devices: 94.9 us -> 113 us  [the longest x14 78.3 us: hop(): lax.ppermute(held[which], every, hop_pairs(lines, depth, step, which))]
    pallas_call x9 -> x10, Pallas kernels: 23.5 us -> 22.6 us  [step_call(): pl.pallas_call(functools.partial(step_kernel, depth, slots, step, rows, t...]
  transfers between devices with their start and end apart: 21 -> 19, of which waited for: 11 -> 6; matrix products, arithmetic and copies ran while one was open for 2% -> 3% of each run, Pallas kernels for 13% -> 14%
where the time goes in v2:
time: 158 us; the launch traced here: 157 us
  starting transfers between devices  113 us (72%)
  Pallas kernels  22.6 us (14%)
  waiting for transfers between devices  15.8 us (10%)
  local copies, waits for them, and re-layouts  3.74 us (2%)
    ppermute x14, starting transfers between devices, hop(): lax.ppermute(held[which], every, hop_pairs(lines, depth, step, which))  78.3 us
    ppermute x2, starting transfers between devices, flip(): return lax.ppermute(value, ring, flip_pairs(depth))  28.5 us
    pallas_call x10, Pallas kernels, step_call(): pl.pallas_call(functools.partial(step_kernel, depth, slots, step, rows, t...  22.6 us
    ppermute x14, waiting for transfers between devices, hop(): lax.ppermute(held[which], every, hop_pairs(lines, depth, step, which))  15.7 us
  transfers between devices with their start and end apart: 19, of which 6 were waited for; matrix products, arithmetic and copies ran while one was open for 3% of the time, Pallas kernels for 14%

profile of v2, /device:TPU:1, one launch (start us, length us, event | category | flops | bytes accessed | tf_op | source)
XLA Modules:
  0.0 156.9 jit_solution(161873574882571840)
XLA Ops:
  0.0 0.0 copy-start
  0.0 16.2 %collective-permute-start.1 = (f32[10,128,128]{2,1,0:T(8,128)}, f32[10,128,128]{2,1,0:T(8,128)S(1)}, u32[]{:S(2)}, u32[]{:S(2)}) collective-permute-start(f32[10,128,128]{2,1,0:T(8,128)} %bitcast.7), channel_id=1, source_target_pairs={{0,8},{1,9},{2,10},{3,11},{4,12},{5,13},{6,14},{7,15},{8,0},{9,1},... | collective-permute-start | bytes 1966088 | tf_op jit(solution)/shard_map/ppermute | solution.py:215
  16.2 5.3 %collective-permute-start = (f32[10,128,128]{2,1,0:T(8,128)}, f32[10,128,128]{2,1,0:T(8,128)S(1)}, u32[]{:S(2)}, u32[]{:S(2)}) collective-permute-start(f32[10,128,128]{2,1,0:T(8,128)} %bitcast.8), channel_id=1, source_target_pairs={{0,1},{8,31},{1,2},{9,8},{2,3},{10,9},{3,4},{11,10},{4,5},{12,11},... | collective-permute-start | bytes 1966088 | tf_op jit(solution)/shard_map/ppermute | solution.py:212
  21.5 3.1 %collective-permute-start.4 = (f32[10,128,128]{2,1,0:T(8,128)}, f32[10,128,128]{2,1,0:T(8,128)S(1)}, u32[]{:S(2)}, u32[]{:S(2)}) collective-permute-start(f32[10,128,128]{2,1,0:T(8,128)} %bitcast.9), channel_id=1, source_target_pairs={{0,992},{8,40},{1,993},{9,41},{2,994},{10,42},{3,995},{11,43},{4,9... | collective-permute-start | bytes 1966088 | tf_op jit(solution)/shard_map/ppermute | solution.py:220
  24.7 0.0 collective-permute-done.1.refs_1_.refs_3_
  24.7 6.1 %collective-permute-start.3 = (f32[10,128,128]{2,1,0:T(8,128)S(1)}, f32[10,128,128]{2,1,0:T(8,128)S(1)}, u32[]{:S(2)}, u32[]{:S(2)}) collective-permute-start(f32[10,128,128]{2,1,0:T(8,128)S(1)} %collective-permute-done.1.refs_1_.refs_3_), channel_id=1, source_target_pairs={{0,1},{8,1023},{1,2},{9,8},{2,3},{10,9},{3,4},{11,10},{4,5},{12,11... | collective-permute-start | bytes 1966088 | tf_op jit(solution)/shard_map/ppermute | solution.py:212
  30.8 1.9 %copy.26 = s32[1024,10]{1,0:T(8,128)} copy(s32[1024,10]{0,1:T(8,128)} %param.3) | data formatting | bytes 81920 | tf_op args[1]
  32.7 1.7 %gather_fusion = s32[96,10]{1,0:T(8,128)S(1)} fusion(s32[1024,10]{1,0:T(8,128)} %copy.26, s32[1024]{0:T(1024)S(1)} %pad_clamp_fusion), kind=kCustom, calls=%fused_computation | custom fusion | bytes 8064 | tf_op jit(solution)/shard_map/jit(_take)/gather | solution.py:205
  34.3 0.1 subtract_add_fusion
  34.4 0.1 add.101
  34.6 0.1 pad_add_fusion.info
  34.7 0.0 copy-done
  34.7 1.7 %products.10.refs_5_ = f32[10,128,128]{2,1,0:T(8,128)S(1)} custom-call(s32[962]{0:T(1024)S(1)} %pad_add_fusion.info, f32[10,128,128]{2,1,0:T(8,128)S(1)} %bitcast.10, f32[10,128,128]{2,1,0:T(8,128)S(1)} %collective-permute-done.1.refs_1_.refs_3_, f32[10,128,128]{2,1,0:T(8,128)S(1)} %bitcast.11), custom_call_target="tpu_custom_call" | custom-call | flops 200000000 | bytes 8000000 | tf_op jit(solution)/shard_map/products/pallas_call | solution.py:173
  36.3 0.0 collective-permute-done.refs_0_
  36.4 1.9 %collective-permute-start.2 = (f32[10,128,128]{2,1,0:T(8,128)S(1)}, f32[10,128,128]{2,1,0:T(8,128)S(1)}, u32[]{:S(2)}, u32[]{:S(2)}) collective-permute-start(f32[10,128,128]{2,1,0:T(8,128)S(1)} %collective-permute-done.refs_0_), channel_id=1, source_target_pairs={{0,1},{8,31},{1,2},{9,8},{2,3},{10,9},{3,4},{11,10},{4,5},{12,11},... | collective-permute-start | bytes 1966088 | tf_op jit(solution)/shard_map/ppermute | solution.py:212
  38.3 0.0 collective-permute-done.3.refs_1_
  38.3 9.3 %collective-permute-start.6 = (f32[10,128,128]{2,1,0:T(8,128)S(1)}, f32[10,128,128]{2,1,0:T(8,128)S(1)}, u32[]{:S(2)}, u32[]{:S(2)}) collective-permute-start(f32[10,128,128]{2,1,0:T(8,128)S(1)} %collective-permute-done.3.refs_1_), channel_id=1, source_target_pairs={{0,1},{8,1023},{1,2},{9,8},{2,3},{10,9},{3,4},{11,10},{4,5},{12,11... | collective-permute-start | bytes 1966088 | tf_op jit(solution)/shard_map/ppermute | solution.py:212
  47.7 0.0 collective-permute-done.4.refs_4_.refs_1_
  47.7 3.2 %products.11 = (f32[10,128,128]{2,1,0:T(8,128)S(1)}, f32[10,128,128]{2,1,0:T(8,128)S(1)}, f32[10,128,128]{2,1,0:T(8,128)S(1)}) custom-call(s32[962]{0:T(1024)S(1)} %pad_add_fusion.info, f32[10,128,128]{2,1,0:T(8,128)S(1)} %collective-permute-done.refs_0_, ...), custom_call_target="tpu_custom_call", output_to_operand_aliasing={{0}: (6, {}), {1}: (7, {}), {2}: (8, {})} | custom-call | flops 200000000 | bytes 8000000 | tf_op jit(solution)/shard_map/products/pallas_call | solution.py:173
  50.9 0.0 collective-permute-done.2.refs_0_
  51.0 1.9 %collective-permute-start.5 = (f32[10,128,128]{2,1,0:T(8,128)S(1)}, f32[10,128,128]{2,1,0:T(8,128)S(1)}, u32[]{:S(2)}, u32[]{:S(2)}) collective-permute-start(f32[10,128,128]{2,1,0:T(8,128)S(1)} %collective-permute-done.2.refs_0_), channel_id=1, source_target_pairs={{0,1},{8,31},{1,2},{9,8},{2,3},{10,9},{3,4},{11,10},{4,5},{12,11},... | collective-permute-start | bytes 1966088 | tf_op jit(solution)/shard_map/ppermute | solution.py:212
  52.9 2.2 %collective-permute-done.6.refs_1_ = f32[10,128,128]{2,1,0:T(8,128)S(1)} collective-permute-done((f32[10,128,128]{2,1,0:T(8,128)S(1)}, f32[10,128,128]{2,1,0:T(8,128)S(1)}, u32[]{:S(2)}, u32[]{:S(2)}) %collective-permute-start.6) | collective-permute-done | bytes 655392 | tf_op jit(solution)/shard_map/ppermute | solution.py:212
  55.1 9.2 %collective-permute-start.8 = (f32[10,128,128]{2,1,0:T(8,128)S(1)}, f32[10,128,128]{2,1,0:T(8,128)S(1)}, u32[]{:S(2)}, u32[]{:S(2)}) collective-permute-start(f32[10,128,128]{2,1,0:T(8,128)S(1)} %collective-permute-done.6.refs_1_), channel_id=1, source_target_pairs={{0,1},{8,1023},{1,2},{9,8},{2,3},{10,9},{3,4},{11,10},{4,5},{12,11... | collective-permute-start | bytes 1966088 | tf_op jit(solution)/shard_map/ppermute | solution.py:212
  64.4 2.1 %products.12 = (f32[10,128,128]{2,1,0:T(8,128)S(1)}, f32[10,128,128]{2,1,0:T(8,128)S(1)}, f32[10,128,128]{2,1,0:T(8,128)S(1)}) custom-call(s32[962]{0:T(1024)S(1)} %pad_add_fusion.info, f32[10,128,128]{2,1,0:T(8,128)S(1)} %collective-permute-done.2.refs_0_, ...), custom_call_target="tpu_custom_call", output_to_operand_aliasing={{0}: (6, {}), {1}: (7, {}), {2}: (8, {})} | custom-call | flops 200000000 | bytes 8000000 | tf_op jit(solution)/shard_map/products/pallas_call | solution.py:173
  66.5 0.0 collective-permute-done.5.refs_0_
  66.5 1.9 %collective-permute-start.7 = (f32[10,128,128]{2,1,0:T(8,128)S(1)}, f32[10,128,128]{2,1,0:T(8,128)S(1)}, u32[]{:S(2)}, u32[]{:S(2)}) collective-permute-start(f32[10,128,128]{2,1,0:T(8,128)S(1)} %collective-permute-done.5.refs_0_), channel_id=1, source_target_pairs={{0,1},{8,31},{1,2},{9,8},{2,3},{10,9},{3,4},{11,10},{4,5},{12,11},... | collective-permute-start | bytes 1966088 | tf_op jit(solution)/shard_map/ppermute | solution.py:212
  68.4 3.5 %collective-permute-done.8.refs_1_ = f32[10,128,128]{2,1,0:T(8,128)S(1)} collective-permute-done((f32[10,128,128]{2,1,0:T(8,128)S(1)}, f32[10,128,128]{2,1,0:T(8,128)S(1)}, u32[]{:S(2)}, u32[]{:S(2)}) %collective-permute-start.8) | collective-permute-done | bytes 655392 | tf_op jit(solution)/shard_map/ppermute | solution.py:212
  71.9 9.2 %collective-permute-start.10 = (f32[10,128,128]{2,1,0:T(8,128)S(1)}, f32[10,128,128]{2,1,0:T(8,128)S(1)}, u32[]{:S(2)}, u32[]{:S(2)}) collective-permute-start(f32[10,128,128]{2,1,0:T(8,128)S(1)} %collective-permute-done.8.refs_1_), channel_id=1, source_target_pairs={{0,1},{8,1023},{1,2},{9,8},{2,3},{10,9},{3,4},{11,10},{4,5},{12,11... | collective-permute-start | bytes 1966088 | tf_op jit(solution)/shard_map/ppermute | solution.py:212
  81.1 3.0 %products.13 = (f32[10,128,128]{2,1,0:T(8,128)S(1)}, f32[10,128,128]{2,1,0:T(8,128)S(1)}, f32[10,128,128]{2,1,0:T(8,128)S(1)}) custom-call(s32[962]{0:T(1024)S(1)} %pad_add_fusion.info, f32[10,128,128]{2,1,0:T(8,128)S(1)} %collective-permute-done.5.refs_0_, ...), custom_call_target="tpu_custom_call", output_to_operand_aliasing={{0}: (6, {}), {1}: (7, {}), {2}: (8, {})} | custom-call | flops 200000000 | bytes 8000000 | tf_op jit(solution)/shard_map/products/pallas_call | solution.py:173
  84.1 0.0 collective-permute-done.7.refs_0_
  84.1 1.9 %collective-permute-start.9 = (f32[10,128,128]{2,1,0:T(8,128)S(1)}, f32[10,128,128]{2,1,0:T(8,128)S(1)}, u32[]{:S(2)}, u32[]{:S(2)}) collective-permute-start(f32[10,128,128]{2,1,0:T(8,128)S(1)} %collective-permute-done.7.refs_0_), channel_id=1, source_target_pairs={{0,1},{8,31},{1,2},{9,8},{2,3},{10,9},{3,4},{11,10},{4,5},{12,11},... | collective-permute-start | bytes 1966088 | tf_op jit(solution)/shard_map/ppermute | solution.py:212
  86.1 2.5 %collective-permute-done.10.refs_1_ = f32[10,128,128]{2,1,0:T(8,128)S(1)} collective-permute-done((f32[10,128,128]{2,1,0:T(8,128)S(1)}, f32[10,128,128]{2,1,0:T(8,128)S(1)}, u32[]{:S(2)}, u32[]{:S(2)}) %collective-permute-start.10) | collective-permute-done | bytes 655392 | tf_op jit(solution)/shard_map/ppermute | solution.py:212
  88.6 9.2 %collective-permute-start.12 = (f32[10,128,128]{2,1,0:T(8,128)S(1)}, f32[10,128,128]{2,1,0:T(8,128)S(1)}, u32[]{:S(2)}, u32[]{:S(2)}) collective-permute-start(f32[10,128,128]{2,1,0:T(8,128)S(1)} %collective-permute-done.10.refs_1_), channel_id=1, source_target_pairs={{0,1},{8,1023},{1,2},{9,8},{2,3},{10,9},{3,4},{11,10},{4,5},{12,11... | collective-permute-start | bytes 1966088 | tf_op jit(solution)/shard_map/ppermute | solution.py:212
  97.9 3.2 %products.14 = (f32[10,128,128]{2,1,0:T(8,128)S(1)}, f32[10,128,128]{2,1,0:T(8,128)S(1)}, f32[10,128,128]{2,1,0:T(8,128)S(1)}) custom-call(s32[962]{0:T(1024)S(1)} %pad_add_fusion.info, f32[10,128,128]{2,1,0:T(8,128)S(1)} %collective-permute-done.7.refs_0_, ...), custom_call_target="tpu_custom_call", output_to_operand_aliasing={{0}: (6, {}), {1}: (7, {}), {2}: (8, {})} | custom-call | flops 200000000 | bytes 8000000 | tf_op jit(solution)/shard_map/products/pallas_call | solution.py:173
  101.1 0.0 collective-permute-done.9.refs_0_
  101.1 1.9 %collective-permute-start.11 = (f32[10,128,128]{2,1,0:T(8,128)S(1)}, f32[10,128,128]{2,1,0:T(8,128)S(1)}, u32[]{:S(2)}, u32[]{:S(2)}) collective-permute-start(f32[10,128,128]{2,1,0:T(8,128)S(1)} %collective-permute-done.9.refs_0_), channel_id=1, source_target_pairs={{0,1},{8,31},{1,2},{9,8},{2,3},{10,9},{3,4},{11,10},{4,5},{12,11},... | collective-permute-start | bytes 1966088 | tf_op jit(solution)/shard_map/ppermute | solution.py:212
  103.0 2.4 %collective-permute-done.12.refs_1_ = f32[10,128,128]{2,1,0:T(8,128)S(1)} collective-permute-done((f32[10,128,128]{2,1,0:T(8,128)S(1)}, f32[10,128,128]{2,1,0:T(8,128)S(1)}, u32[]{:S(2)}, u32[]{:S(2)}) %collective-permute-start.12) | collective-permute-done | bytes 655392 | tf_op jit(solution)/shard_map/ppermute | solution.py:212
  105.4 9.2 %collective-permute-start.14 = (f32[10,128,128]{2,1,0:T(8,128)S(1)}, f32[10,128,128]{2,1,0:T(8,128)S(1)}, u32[]{:S(2)}, u32[]{:S(2)}) collective-permute-start(f32[10,128,128]{2,1,0:T(8,128)S(1)} %collective-permute-done.12.refs_1_), channel_id=1, source_target_pairs={{0,1},{8,1023},{1,2},{9,8},{2,3},{10,9},{3,4},{11,10},{4,5},{12,11... | collective-permute-start | bytes 1966088 | tf_op jit(solution)/shard_map/ppermute | solution.py:212
  114.6 2.0 %products.15 = (f32[10,128,128]{2,1,0:T(8,128)S(1)}, f32[10,128,128]{2,1,0:T(8,128)S(1)}, f32[10,128,128]{2,1,0:T(8,128)S(1)}) custom-call(s32[962]{0:T(1024)S(1)} %pad_add_fusion.info, f32[10,128,128]{2,1,0:T(8,128)S(1)} %collective-permute-done.9.refs_0_, ...), custom_call_target="tpu_custom_call", output_to_operand_aliasing={{0}: (6, {}), {1}: (7, {}), {2}: (8, {})} | custom-call | flops 200000000 | bytes 8000000 | tf_op jit(solution)/shard_map/products/pallas_call | solution.py:173
  116.6 0.0 collective-permute-done.11.refs_0_
  116.7 1.9 %collective-permute-start.13 = (f32[10,128,128]{2,1,0:T(8,128)S(1)}, f32[10,128,128]{2,1,0:T(8,128)S(1)}, u32[]{:S(2)}, u32[]{:S(2)}) collective-permute-start(f32[10,128,128]{2,1,0:T(8,128)S(1)} %collective-permute-done.11.refs_0_), channel_id=1, source_target_pairs={{0,1},{8,31},{1,2},{9,8},{2,3},{10,9},{3,4},{11,10},{4,5},{12,11},... | collective-permute-start | bytes 1966088 | tf_op jit(solution)/shard_map/ppermute | solution.py:212
  118.6 3.5 %collective-permute-done.14.refs_1_ = f32[10,128,128]{2,1,0:T(8,128)S(1)} collective-permute-done((f32[10,128,128]{2,1,0:T(8,128)S(1)}, f32[10,128,128]{2,1,0:T(8,128)S(1)}, u32[]{:S(2)}, u32[]{:S(2)}) %collective-permute-start.14) | collective-permute-done | bytes 655392 | tf_op jit(solution)/shard_map/ppermute | solution.py:212
  122.1 9.2 %collective-permute-start.16 = (f32[10,128,128]{2,1,0:T(8,128)S(1)}, f32[10,128,128]{2,1,0:T(8,128)S(1)}, u32[]{:S(2)}, u32[]{:S(2)}) collective-permute-start(f32[10,128,128]{2,1,0:T(8,128)S(1)} %collective-permute-done.14.refs_1_), channel_id=1, source_target_pairs={{0,1},{8,1023},{1,2},{9,8},{2,3},{10,9},{3,4},{11,10},{4,5},{12,11... | collective-permute-start | bytes 1966088 | tf_op jit(solution)/shard_map/ppermute | solution.py:212
  131.3 2.0 %products.16 = (f32[10,128,128]{2,1,0:T(8,128)S(1)}, f32[10,128,128]{2,1,0:T(8,128)S(1)}, f32[10,128,128]{2,1,0:T(8,128)S(1)}) custom-call(s32[962]{0:T(1024)S(1)} %pad_add_fusion.info, f32[10,128,128]{2,1,0:T(8,128)S(1)} %collective-permute-done.11.refs_0_, ...), custom_call_target="tpu_custom_call", output_to_operand_aliasing={{0}: (6, {}), {1}: (7, {}), {2}: (8, {})} | custom-call | flops 200000000 | bytes 8000000 | tf_op jit(solution)/shard_map/products/pallas_call | solution.py:173
  133.4 0.0 collective-permute-done.13.refs_0_
  133.4 1.3 collective-permute-start.15
  134.7 0.7 products.19
  135.4 1.9 %collective-permute-start.18 = (f32[10,128,128]{2,1,0:T(8,128)S(1)}, f32[10,128,128]{2,1,0:T(8,128)S(1)}, u32[]{:S(2)}, u32[]{:S(2)}) collective-permute-start(f32[10,128,128]{2,1,0:T(8,128)S(1)} %products.19), channel_id=1, source_target_pairs={{992,0},{40,8},{993,1},{41,9},{994,2},{42,10},{995,3},{43,11},{996... | collective-permute-start | bytes 1966088 | tf_op jit(solution)/shard_map/ppermute | solution.py:240
  137.3 1.6 %collective-permute-done.16.refs_1_ = f32[10,128,128]{2,1,0:T(8,128)S(1)} collective-permute-done((f32[10,128,128]{2,1,0:T(8,128)S(1)}, f32[10,128,128]{2,1,0:T(8,128)S(1)}, u32[]{:S(2)}, u32[]{:S(2)}) %collective-permute-start.16) | collective-permute-done | bytes 655392 | tf_op jit(solution)/shard_map/ppermute | solution.py:212
  138.9 2.9 %products.17 = (f32[10,128,128]{2,1,0:T(8,128)S(1)}, f32[10,128,128]{2,1,0:T(8,128)S(1)}) custom-call(s32[962]{0:T(1024)S(1)} %pad_add_fusion.info, f32[10,128,128]{2,1,0:T(8,128)S(1)} %collective-permute-done.13.refs_0_, f32[10,128,128]{2,1,0:T(8,128)S(1)} %collective-permute-done.16.refs_1_, ...), custom_call_target="tpu_custom_call", output_to_operand_aliasing={{0}: (5, {}), {1}: (6, {})} | custom-call | flops 200000000 | bytes 8000000 | tf_op jit(solution)/shard_map/products/pallas_call | solution.py:173
  141.8 12.4 %collective-permute-start.17 = (f32[10,128,128]{2,1,0:T(8,128)S(1)}, f32[10,128,128]{2,1,0:T(8,128)S(1)}, u32[]{:S(2)}, u32[]{:S(2)}) collective-permute-start(f32[10,128,128]{2,1,0:T(8,128)S(1)} %get-tuple-element.99), channel_id=1, source_target_pairs={{0,8},{1,9},{2,10},{3,11},{4,12},{5,13},{6,14},{7,15},{8,0},{9,1},... | collective-permute-start | bytes 1966088 | tf_op jit(solution)/shard_map/ppermute | solution.py:215
  154.1 0.0 collective-permute-done.15.refs_0_
  154.2 1.8 %products.18 = f32[10,128,128]{2,1,0:T(8,128)S(1)} custom-call(s32[962]{0:T(1024)S(1)} %pad_add_fusion.info, f32[10,128,128]{2,1,0:T(8,128)S(1)} %collective-permute-done.15.refs_0_, f32[10,128,128]{2,1,0:T(8,128)S(1)} %bitcast.19, f32[10,128,128]{2,1,0:T(8,128)S(1)} %get-tuple-element.98.refs_2_), custom_call_target="tpu_custom_call", output_to_operand_aliasing={{}: (3, {})} | custom-call | flops 200000000 | bytes 8000000 | tf_op jit(solution)/shard_map/products/pallas_call | solution.py:173
  156.0 0.0 collective-permute-done.18
  156.0 0.0 collective-permute-done.17
  156.0 0.9 add_bitcast_fusion
  (6 shorter events, 0.1 us)
Async XLA Ops:
  0.0 34.7 %copy-start = (f32[1,10,128,128]{3,2,1,0:T(8,128)S(1)}, f32[1,10,128,128]{3,2,1,0:T(8,128)}, u32[]{:S(2)}) copy-start(f32[1,10,128,128]{3,2,1,0:T(8,128)} %param.2) | copy-start | bytes 1966084
  0.0 24.7 %collective-permute-start.1 = (f32[10,128,128]{2,1,0:T(8,128)}, f32[10,128,128]{2,1,0:T(8,128)S(1)}, u32[]{:S(2)}, u32[]{:S(2)}) collective-permute-start(f32[10,128,128]{2,1,0:T(8,128)} %bitcast.7), channel_id=1, source_target_pairs={{0,8},{1,9},{2,10},{3,11},{4,12},{5,13},{6,14},{7,15},{8,0},{9,1},... | collective-permute-start | bytes 1966088 | tf_op jit(solution)/shard_map/ppermute | solution.py:215
  16.2 20.2 %collective-permute-start = (f32[10,128,128]{2,1,0:T(8,128)}, f32[10,128,128]{2,1,0:T(8,128)S(1)}, u32[]{:S(2)}, u32[]{:S(2)}) collective-permute-start(f32[10,128,128]{2,1,0:T(8,128)} %bitcast.8), channel_id=1, source_target_pairs={{0,1},{8,31},{1,2},{9,8},{2,3},{10,9},{3,4},{11,10},{4,5},{12,11},... | collective-permute-start | bytes 1966088 | tf_op jit(solution)/shard_map/ppermute | solution.py:212
  21.5 26.2 %collective-permute-start.4 = (f32[10,128,128]{2,1,0:T(8,128)}, f32[10,128,128]{2,1,0:T(8,128)S(1)}, u32[]{:S(2)}, u32[]{:S(2)}) collective-permute-start(f32[10,128,128]{2,1,0:T(8,128)} %bitcast.9), channel_id=1, source_target_pairs={{0,992},{8,40},{1,993},{9,41},{2,994},{10,42},{3,995},{11,43},{4,9... | collective-permute-start | bytes 1966088 | tf_op jit(solution)/shard_map/ppermute | solution.py:220
  24.7 13.6 %collective-permute-start.3 = (f32[10,128,128]{2,1,0:T(8,128)S(1)}, f32[10,128,128]{2,1,0:T(8,128)S(1)}, u32[]{:S(2)}, u32[]{:S(2)}) collective-permute-start(f32[10,128,128]{2,1,0:T(8,128)S(1)} %collective-permute-done.1.refs_1_.refs_3_), channel_id=1, source_target_pairs={{0,1},{8,1023},{1,2},{9,8},{2,3},{10,9},{3,4},{11,10},{4,5},{12,11... | collective-permute-start | bytes 1966088 | tf_op jit(solution)/shard_map/ppermute | solution.py:212
  36.4 14.6 %collective-permute-start.2 = (f32[10,128,128]{2,1,0:T(8,128)S(1)}, f32[10,128,128]{2,1,0:T(8,128)S(1)}, u32[]{:S(2)}, u32[]{:S(2)}) collective-permute-start(f32[10,128,128]{2,1,0:T(8,128)S(1)} %collective-permute-done.refs_0_), channel_id=1, source_target_pairs={{0,1},{8,31},{1,2},{9,8},{2,3},{10,9},{3,4},{11,10},{4,5},{12,11},... | collective-permute-start | bytes 1966088 | tf_op jit(solution)/shard_map/ppermute | solution.py:212
  38.3 16.8 %collective-permute-start.6 = (f32[10,128,128]{2,1,0:T(8,128)S(1)}, f32[10,128,128]{2,1,0:T(8,128)S(1)}, u32[]{:S(2)}, u32[]{:S(2)}) collective-permute-start(f32[10,128,128]{2,1,0:T(8,128)S(1)} %collective-permute-done.3.refs_1_), channel_id=1, source_target_pairs={{0,1},{8,1023},{1,2},{9,8},{2,3},{10,9},{3,4},{11,10},{4,5},{12,11... | collective-permute-start | bytes 1966088 | tf_op jit(solution)/shard_map/ppermute | solution.py:212
  51.0 15.5 %collective-permute-start.5 = (f32[10,128,128]{2,1,0:T(8,128)S(1)}, f32[10,128,128]{2,1,0:T(8,128)S(1)}, u32[]{:S(2)}, u32[]{:S(2)}) collective-permute-start(f32[10,128,128]{2,1,0:T(8,128)S(1)} %collective-permute-done.2.refs_0_), channel_id=1, source_target_pairs={{0,1},{8,31},{1,2},{9,8},{2,3},{10,9},{3,4},{11,10},{4,5},{12,11},... | collective-permute-start | bytes 1966088 | tf_op jit(solution)/shard_map/ppermute | solution.py:212
  55.1 16.7 %collective-permute-start.8 = (f32[10,128,128]{2,1,0:T(8,128)S(1)}, f32[10,128,128]{2,1,0:T(8,128)S(1)}, u32[]{:S(2)}, u32[]{:S(2)}) collective-permute-start(f32[10,128,128]{2,1,0:T(8,128)S(1)} %collective-permute-done.6.refs_1_), channel_id=1, source_target_pairs={{0,1},{8,1023},{1,2},{9,8},{2,3},{10,9},{3,4},{11,10},{4,5},{12,11... | collective-permute-start | bytes 1966088 | tf_op jit(solution)/shard_map/ppermute | solution.py:212
  66.5 17.7 %collective-permute-start.7 = (f32[10,128,128]{2,1,0:T(8,128)S(1)}, f32[10,128,128]{2,1,0:T(8,128)S(1)}, u32[]{:S(2)}, u32[]{:S(2)}) collective-permute-start(f32[10,128,128]{2,1,0:T(8,128)S(1)} %collective-permute-done.5.refs_0_), channel_id=1, source_target_pairs={{0,1},{8,31},{1,2},{9,8},{2,3},{10,9},{3,4},{11,10},{4,5},{12,11},... | collective-permute-start | bytes 1966088 | tf_op jit(solution)/shard_map/ppermute | solution.py:212
  71.9 16.7 %collective-permute-start.10 = (f32[10,128,128]{2,1,0:T(8,128)S(1)}, f32[10,128,128]{2,1,0:T(8,128)S(1)}, u32[]{:S(2)}, u32[]{:S(2)}) collective-permute-start(f32[10,128,128]{2,1,0:T(8,128)S(1)} %collective-permute-done.8.refs_1_), channel_id=1, source_target_pairs={{0,1},{8,1023},{1,2},{9,8},{2,3},{10,9},{3,4},{11,10},{4,5},{12,11... | collective-permute-start | bytes 1966088 | tf_op jit(solution)/shard_map/ppermute | solution.py:212
  84.1 16.9 %collective-permute-start.9 = (f32[10,128,128]{2,1,0:T(8,128)S(1)}, f32[10,128,128]{2,1,0:T(8,128)S(1)}, u32[]{:S(2)}, u32[]{:S(2)}) collective-permute-start(f32[10,128,128]{2,1,0:T(8,128)S(1)} %collective-permute-done.7.refs_0_), channel_id=1, source_target_pairs={{0,1},{8,31},{1,2},{9,8},{2,3},{10,9},{3,4},{11,10},{4,5},{12,11},... | collective-permute-start | bytes 1966088 | tf_op jit(solution)/shard_map/ppermute | solution.py:212
  88.6 16.7 %collective-permute-start.12 = (f32[10,128,128]{2,1,0:T(8,128)S(1)}, f32[10,128,128]{2,1,0:T(8,128)S(1)}, u32[]{:S(2)}, u32[]{:S(2)}) collective-permute-start(f32[10,128,128]{2,1,0:T(8,128)S(1)} %collective-permute-done.10.refs_1_), channel_id=1, source_target_pairs={{0,1},{8,1023},{1,2},{9,8},{2,3},{10,9},{3,4},{11,10},{4,5},{12,11... | collective-permute-start | bytes 1966088 | tf_op jit(solution)/shard_map/ppermute | solution.py:212
  101.1 15.6 %collective-permute-start.11 = (f32[10,128,128]{2,1,0:T(8,128)S(1)}, f32[10,128,128]{2,1,0:T(8,128)S(1)}, u32[]{:S(2)}, u32[]{:S(2)}) collective-permute-start(f32[10,128,128]{2,1,0:T(8,128)S(1)} %collective-permute-done.9.refs_0_), channel_id=1, source_target_pairs={{0,1},{8,31},{1,2},{9,8},{2,3},{10,9},{3,4},{11,10},{4,5},{12,11},... | collective-permute-start | bytes 1966088 | tf_op jit(solution)/shard_map/ppermute | solution.py:212
  105.4 16.7 %collective-permute-start.14 = (f32[10,128,128]{2,1,0:T(8,128)S(1)}, f32[10,128,128]{2,1,0:T(8,128)S(1)}, u32[]{:S(2)}, u32[]{:S(2)}) collective-permute-start(f32[10,128,128]{2,1,0:T(8,128)S(1)} %collective-permute-done.12.refs_1_), channel_id=1, source_target_pairs={{0,1},{8,1023},{1,2},{9,8},{2,3},{10,9},{3,4},{11,10},{4,5},{12,11... | collective-permute-start | bytes 1966088 | tf_op jit(solution)/shard_map/ppermute | solution.py:212
  116.7 16.7 %collective-permute-start.13 = (f32[10,128,128]{2,1,0:T(8,128)S(1)}, f32[10,128,128]{2,1,0:T(8,128)S(1)}, u32[]{:S(2)}, u32[]{:S(2)}) collective-permute-start(f32[10,128,128]{2,1,0:T(8,128)S(1)} %collective-permute-done.11.refs_0_), channel_id=1, source_target_pairs={{0,1},{8,31},{1,2},{9,8},{2,3},{10,9},{3,4},{11,10},{4,5},{12,11},... | collective-permute-start | bytes 1966088 | tf_op jit(solution)/shard_map/ppermute | solution.py:212
  122.1 16.8 %collective-permute-start.16 = (f32[10,128,128]{2,1,0:T(8,128)S(1)}, f32[10,128,128]{2,1,0:T(8,128)S(1)}, u32[]{:S(2)}, u32[]{:S(2)}) collective-permute-start(f32[10,128,128]{2,1,0:T(8,128)S(1)} %collective-permute-done.14.refs_1_), channel_id=1, source_target_pairs={{0,1},{8,1023},{1,2},{9,8},{2,3},{10,9},{3,4},{11,10},{4,5},{12,11... | collective-permute-start | bytes 1966088 | tf_op jit(solution)/shard_map/ppermute | solution.py:212
  133.4 20.7 %collective-permute-start.15 = (f32[10,128,128]{2,1,0:T(8,128)S(1)}, f32[10,128,128]{2,1,0:T(8,128)S(1)}, u32[]{:S(2)}, u32[]{:S(2)}) collective-permute-start(f32[10,128,128]{2,1,0:T(8,128)S(1)} %collective-permute-done.13.refs_0_), channel_id=1, source_target_pairs={{0,9},{9,0},{10,1},{7,1016},{16,25},{25,16},{26,17},{23,8},{32,41}... | collective-permute-start | bytes 1966088 | tf_op jit(solution)/shard_map/ppermute | solution.py:236
  135.4 20.6 %collective-permute-start.18 = (f32[10,128,128]{2,1,0:T(8,128)S(1)}, f32[10,128,128]{2,1,0:T(8,128)S(1)}, u32[]{:S(2)}, u32[]{:S(2)}) collective-permute-start(f32[10,128,128]{2,1,0:T(8,128)S(1)} %products.19), channel_id=1, source_target_pairs={{992,0},{40,8},{993,1},{41,9},{994,2},{42,10},{995,3},{43,11},{996... | collective-permute-start | bytes 1966088 | tf_op jit(solution)/shard_map/ppermute | solution.py:240
  141.8 14.2 %collective-permute-start.17 = (f32[10,128,128]{2,1,0:T(8,128)S(1)}, f32[10,128,128]{2,1,0:T(8,128)S(1)}, u32[]{:S(2)}, u32[]{:S(2)}) collective-permute-start(f32[10,128,128]{2,1,0:T(8,128)S(1)} %get-tuple-element.99), channel_id=1, source_target_pairs={{0,8},{1,9},{2,10},{3,11},{4,12},{5,13},{6,14},{7,15},{8,0},{9,1},... | collective-permute-start | bytes 1966088 | tf_op jit(solution)/shard_map/ppermute | solution.py:215

commit v3 on v2

--- a/solution.py
+++ b/solution.py
@@ -215,7 +215,8 @@
         return lax.ppermute(value, ring, flip_pairs(depth))
 
     own = blocks[0]
-    held = [own, flip(own)]
+    other, info = lax.optimization_barrier((flip(own), info))
+    held = [own, other]
     away = line_pairs(lines, depth)
     ghost = lax.ppermute(own, every, away)
     factors = [held[0], held[1], ghost]

time: 158 us -> 157 us (level)
  local copies, waits for them, and re-layouts: 3.74 us -> 1.9 us
    ppermute x14, waiting for transfers between devices: 15.7 us -> 13.2 us  [hop(): lax.ppermute(held[which], every, hop_pairs(lines, depth, step, which))]
  transfers between devices with their start and end apart: 19 -> 19, of which waited for: 6 -> 9; matrix products, arithmetic and copies ran while one was open for 3% -> 1% of each run, Pallas kernels for 14% -> 15%
where the time goes in v3:
time: 157 us
  starting transfers between devices  114 us (73%)
  Pallas kernels  24 us (15%)
  waiting for transfers between devices  15.4 us (10%)
  local copies, waits for them, and re-layouts  1.9 us (1%)
    ppermute x14, starting transfers between devices, hop(): lax.ppermute(held[which], every, hop_pairs(lines, depth, step, which))  79.5 us
    ppermute x2, starting transfers between devices, flip(): return lax.ppermute(value, ring, flip_pairs(depth))  29.3 us
    pallas_call x10, Pallas kernels, step_call(): pl.pallas_call(functools.partial(step_kernel, depth, slots, step, rows, t...  24 us
    ppermute x14, waiting for transfers between devices, hop(): lax.ppermute(held[which], every, hop_pairs(lines, depth, step, which))  13.2 us
  transfers between devices with their start and end apart: 19, of which 9 were waited for; matrix products, arithmetic and copies ran while one was open for 1% of the time, Pallas kernels for 15%

profile of v3, /device:TPU:1, one launch (start us, length us, event | category | flops | bytes accessed | tf_op | source)
XLA Modules:
  0.0 156.8 jit_solution(9964418421526973710)
XLA Ops:
  0.0 0.0 copy-start
  0.0 16.2 %collective-permute-start = (f32[10,128,128]{2,1,0:T(8,128)}, f32[10,128,128]{2,1,0:T(8,128)S(1)}, u32[]{:S(2)}, u32[]{:S(2)}) collective-permute-start(f32[10,128,128]{2,1,0:T(8,128)} %bitcast.7), channel_id=1, source_target_pairs={{0,8},{1,9},{2,10},{3,11},{4,12},{5,13},{6,14},{7,15},{8,0},{9,1},... | collective-permute-start | bytes 1966088 | tf_op jit(solution)/shard_map/ppermute | solution.py:215
  16.2 5.3 %collective-permute-start.1 = (f32[10,128,128]{2,1,0:T(8,128)}, f32[10,128,128]{2,1,0:T(8,128)S(1)}, u32[]{:S(2)}, u32[]{:S(2)}) collective-permute-start(f32[10,128,128]{2,1,0:T(8,128)} %bitcast.8), channel_id=1, source_target_pairs={{0,1},{8,31},{1,2},{9,8},{2,3},{10,9},{3,4},{11,10},{4,5},{12,11},... | collective-permute-start | bytes 1966088 | tf_op jit(solution)/shard_map/ppermute | solution.py:212
  21.5 1.1 copy.26
  22.6 0.6 gather_fusion
  23.2 0.1 subtract_add_fusion
  23.3 0.1 add.101
  23.5 0.1 pad_add_fusion.info
  23.6 0.0 collective-permute-done.refs_1_.refs_3_
  23.6 7.3 %collective-permute-start.3 = (f32[10,128,128]{2,1,0:T(8,128)S(1)}, f32[10,128,128]{2,1,0:T(8,128)S(1)}, u32[]{:S(2)}, u32[]{:S(2)}) collective-permute-start(f32[10,128,128]{2,1,0:T(8,128)S(1)} %collective-permute-done.refs_1_.refs_3_), channel_id=1, source_target_pairs={{0,1},{8,1023},{1,2},{9,8},{2,3},{10,9},{3,4},{11,10},{4,5},{12,11... | collective-permute-start | bytes 1966088 | tf_op jit(solution)/shard_map/ppermute | solution.py:212
  30.9 0.0 copy-done
  30.9 1.9 %collective-permute-start.4 = (f32[10,128,128]{2,1,0:T(8,128)S(1)}, f32[10,128,128]{2,1,0:T(8,128)S(1)}, u32[]{:S(2)}, u32[]{:S(2)}) collective-permute-start(f32[10,128,128]{2,1,0:T(8,128)S(1)} %bitcast.9), channel_id=1, source_target_pairs={{0,992},{8,40},{1,993},{9,41},{2,994},{10,42},{3,995},{11,43},{4,9... | collective-permute-start | bytes 1966088 | tf_op jit(solution)/shard_map/ppermute | solution.py:221
  32.8 2.4 %products.10.refs_5_ = f32[10,128,128]{2,1,0:T(8,128)S(1)} custom-call(s32[962]{0:T(1024)S(1)} %pad_add_fusion.info, f32[10,128,128]{2,1,0:T(8,128)S(1)} %bitcast.10, f32[10,128,128]{2,1,0:T(8,128)S(1)} %collective-permute-done.refs_1_.refs_3_, f32[10,128,128]{2,1,0:T(8,128)S(1)} %bitcast.11), custom_call_target="tpu_custom_call" | custom-call | flops 200000000 | bytes 8000000 | tf_op jit(solution)/shard_map/products/pallas_call | solution.py:173
  35.2 0.0 collective-permute-done.1.refs_0_
  35.2 1.9 %collective-permute-start.2 = (f32[10,128,128]{2,1,0:T(8,128)S(1)}, f32[10,128,128]{2,1,0:T(8,128)S(1)}, u32[]{:S(2)}, u32[]{:S(2)}) collective-permute-start(f32[10,128,128]{2,1,0:T(8,128)S(1)} %collective-permute-done.1.refs_0_), channel_id=1, source_target_pairs={{0,1},{8,31},{1,2},{9,8},{2,3},{10,9},{3,4},{11,10},{4,5},{12,11},... | collective-permute-start | bytes 1966088 | tf_op jit(solution)/shard_map/ppermute | solution.py:212
  37.1 1.3 collective-permute-done.3.refs_1_
  38.4 9.3 %collective-permute-start.6 = (f32[10,128,128]{2,1,0:T(8,128)S(1)}, f32[10,128,128]{2,1,0:T(8,128)S(1)}, u32[]{:S(2)}, u32[]{:S(2)}) collective-permute-start(f32[10,128,128]{2,1,0:T(8,128)S(1)} %collective-permute-done.3.refs_1_), channel_id=1, source_target_pairs={{0,1},{8,1023},{1,2},{9,8},{2,3},{10,9},{3,4},{11,10},{4,5},{12,11... | collective-permute-start | bytes 1966088 | tf_op jit(solution)/shard_map/ppermute | solution.py:212
  47.8 1.2 collective-permute-done.4.refs_4_.refs_1_
  49.0 3.7 %products.11 = (f32[10,128,128]{2,1,0:T(8,128)S(1)}, f32[10,128,128]{2,1,0:T(8,128)S(1)}, f32[10,128,128]{2,1,0:T(8,128)S(1)}) custom-call(s32[962]{0:T(1024)S(1)} %pad_add_fusion.info, f32[10,128,128]{2,1,0:T(8,128)S(1)} %collective-permute-done.1.refs_0_, ...), custom_call_target="tpu_custom_call", output_to_operand_aliasing={{0}: (6, {}), {1}: (7, {}), {2}: (8, {})} | custom-call | flops 200000000 | bytes 8000000 | tf_op jit(solution)/shard_map/products/pallas_call | solution.py:173
  52.7 0.0 collective-permute-done.2.refs_0_
  52.7 1.9 %collective-permute-start.5 = (f32[10,128,128]{2,1,0:T(8,128)S(1)}, f32[10,128,128]{2,1,0:T(8,128)S(1)}, u32[]{:S(2)}, u32[]{:S(2)}) collective-permute-start(f32[10,128,128]{2,1,0:T(8,128)S(1)} %collective-permute-done.2.refs_0_), channel_id=1, source_target_pairs={{0,1},{8,31},{1,2},{9,8},{2,3},{10,9},{3,4},{11,10},{4,5},{12,11},... | collective-permute-start | bytes 1966088 | tf_op jit(solution)/shard_map/ppermute | solution.py:212
  54.7 0.6 collective-permute-done.6.refs_1_
  55.2 9.2 %collective-permute-start.8 = (f32[10,128,128]{2,1,0:T(8,128)S(1)}, f32[10,128,128]{2,1,0:T(8,128)S(1)}, u32[]{:S(2)}, u32[]{:S(2)}) collective-permute-start(f32[10,128,128]{2,1,0:T(8,128)S(1)} %collective-permute-done.6.refs_1_), channel_id=1, source_target_pairs={{0,1},{8,1023},{1,2},{9,8},{2,3},{10,9},{3,4},{11,10},{4,5},{12,11... | collective-permute-start | bytes 1966088 | tf_op jit(solution)/shard_map/ppermute | solution.py:212
  64.5 3.3 %products.12 = (f32[10,128,128]{2,1,0:T(8,128)S(1)}, f32[10,128,128]{2,1,0:T(8,128)S(1)}, f32[10,128,128]{2,1,0:T(8,128)S(1)}) custom-call(s32[962]{0:T(1024)S(1)} %pad_add_fusion.info, f32[10,128,128]{2,1,0:T(8,128)S(1)} %collective-permute-done.2.refs_0_, ...), custom_call_target="tpu_custom_call", output_to_operand_aliasing={{0}: (6, {}), {1}: (7, {}), {2}: (8, {})} | custom-call | flops 200000000 | bytes 8000000 | tf_op jit(solution)/shard_map/products/pallas_call | solution.py:173
  67.8 0.0 collective-permute-done.5.refs_0_
  67.8 1.9 %collective-permute-start.7 = (f32[10,128,128]{2,1,0:T(8,128)S(1)}, f32[10,128,128]{2,1,0:T(8,128)S(1)}, u32[]{:S(2)}, u32[]{:S(2)}) collective-permute-start(f32[10,128,128]{2,1,0:T(8,128)S(1)} %collective-permute-done.5.refs_0_), channel_id=1, source_target_pairs={{0,1},{8,31},{1,2},{9,8},{2,3},{10,9},{3,4},{11,10},{4,5},{12,11},... | collective-permute-start | bytes 1966088 | tf_op jit(solution)/shard_map/ppermute | solution.py:212
  69.7 2.3 %collective-permute-done.8.refs_1_ = f32[10,128,128]{2,1,0:T(8,128)S(1)} collective-permute-done((f32[10,128,128]{2,1,0:T(8,128)S(1)}, f32[10,128,128]{2,1,0:T(8,128)S(1)}, u32[]{:S(2)}, u32[]{:S(2)}) %collective-permute-start.8) | collective-permute-done | bytes 655392 | tf_op jit(solution)/shard_map/ppermute | solution.py:212
  72.0 9.2 %collective-permute-start.10 = (f32[10,128,128]{2,1,0:T(8,128)S(1)}, f32[10,128,128]{2,1,0:T(8,128)S(1)}, u32[]{:S(2)}, u32[]{:S(2)}) collective-permute-start(f32[10,128,128]{2,1,0:T(8,128)S(1)} %collective-permute-done.8.refs_1_), channel_id=1, source_target_pairs={{0,1},{8,1023},{1,2},{9,8},{2,3},{10,9},{3,4},{11,10},{4,5},{12,11... | collective-permute-start | bytes 1966088 | tf_op jit(solution)/shard_map/ppermute | solution.py:212
  81.2 2.0 %products.13 = (f32[10,128,128]{2,1,0:T(8,128)S(1)}, f32[10,128,128]{2,1,0:T(8,128)S(1)}, f32[10,128,128]{2,1,0:T(8,128)S(1)}) custom-call(s32[962]{0:T(1024)S(1)} %pad_add_fusion.info, f32[10,128,128]{2,1,0:T(8,128)S(1)} %collective-permute-done.5.refs_0_, ...), custom_call_target="tpu_custom_call", output_to_operand_aliasing={{0}: (6, {}), {1}: (7, {}), {2}: (8, {})} | custom-call | flops 200000000 | bytes 8000000 | tf_op jit(solution)/shard_map/products/pallas_call | solution.py:173
  83.3 0.0 collective-permute-done.7.refs_0_
  83.3 1.9 %collective-permute-start.9 = (f32[10,128,128]{2,1,0:T(8,128)S(1)}, f32[10,128,128]{2,1,0:T(8,128)S(1)}, u32[]{:S(2)}, u32[]{:S(2)}) collective-permute-start(f32[10,128,128]{2,1,0:T(8,128)S(1)} %collective-permute-done.7.refs_0_), channel_id=1, source_target_pairs={{0,1},{8,31},{1,2},{9,8},{2,3},{10,9},{3,4},{11,10},{4,5},{12,11},... | collective-permute-start | bytes 1966088 | tf_op jit(solution)/shard_map/ppermute | solution.py:212
  85.2 3.5 %collective-permute-done.10.refs_1_ = f32[10,128,128]{2,1,0:T(8,128)S(1)} collective-permute-done((f32[10,128,128]{2,1,0:T(8,128)S(1)}, f32[10,128,128]{2,1,0:T(8,128)S(1)}, u32[]{:S(2)}, u32[]{:S(2)}) %collective-permute-start.10) | collective-permute-done | bytes 655392 | tf_op jit(solution)/shard_map/ppermute | solution.py:212
  88.7 9.2 %collective-permute-start.12 = (f32[10,128,128]{2,1,0:T(8,128)S(1)}, f32[10,128,128]{2,1,0:T(8,128)S(1)}, u32[]{:S(2)}, u32[]{:S(2)}) collective-permute-start(f32[10,128,128]{2,1,0:T(8,128)S(1)} %collective-permute-done.10.refs_1_), channel_id=1, source_target_pairs={{0,1},{8,1023},{1,2},{9,8},{2,3},{10,9},{3,4},{11,10},{4,5},{12,11... | collective-permute-start | bytes 1966088 | tf_op jit(solution)/shard_map/ppermute | solution.py:212
  98.0 3.0 %products.14 = (f32[10,128,128]{2,1,0:T(8,128)S(1)}, f32[10,128,128]{2,1,0:T(8,128)S(1)}, f32[10,128,128]{2,1,0:T(8,128)S(1)}) custom-call(s32[962]{0:T(1024)S(1)} %pad_add_fusion.info, f32[10,128,128]{2,1,0:T(8,128)S(1)} %collective-permute-done.7.refs_0_, ...), custom_call_target="tpu_custom_call", output_to_operand_aliasing={{0}: (6, {}), {1}: (7, {}), {2}: (8, {})} | custom-call | flops 200000000 | bytes 8000000 | tf_op jit(solution)/shard_map/products/pallas_call | solution.py:173
  101.0 0.0 collective-permute-done.9.refs_0_
  101.0 1.9 %collective-permute-start.11 = (f32[10,128,128]{2,1,0:T(8,128)S(1)}, f32[10,128,128]{2,1,0:T(8,128)S(1)}, u32[]{:S(2)}, u32[]{:S(2)}) collective-permute-start(f32[10,128,128]{2,1,0:T(8,128)S(1)} %collective-permute-done.9.refs_0_), channel_id=1, source_target_pairs={{0,1},{8,31},{1,2},{9,8},{2,3},{10,9},{3,4},{11,10},{4,5},{12,11},... | collective-permute-start | bytes 1966088 | tf_op jit(solution)/shard_map/ppermute | solution.py:212
  102.9 2.6 %collective-permute-done.12.refs_1_ = f32[10,128,128]{2,1,0:T(8,128)S(1)} collective-permute-done((f32[10,128,128]{2,1,0:T(8,128)S(1)}, f32[10,128,128]{2,1,0:T(8,128)S(1)}, u32[]{:S(2)}, u32[]{:S(2)}) %collective-permute-start.12) | collective-permute-done | bytes 655392 | tf_op jit(solution)/shard_map/ppermute | solution.py:212
  105.5 9.2 %collective-permute-start.14 = (f32[10,128,128]{2,1,0:T(8,128)S(1)}, f32[10,128,128]{2,1,0:T(8,128)S(1)}, u32[]{:S(2)}, u32[]{:S(2)}) collective-permute-start(f32[10,128,128]{2,1,0:T(8,128)S(1)} %collective-permute-done.12.refs_1_), channel_id=1, source_target_pairs={{0,1},{8,1023},{1,2},{9,8},{2,3},{10,9},{3,4},{11,10},{4,5},{12,11... | collective-permute-start | bytes 1966088 | tf_op jit(solution)/shard_map/ppermute | solution.py:212
  114.7 3.2 %products.15 = (f32[10,128,128]{2,1,0:T(8,128)S(1)}, f32[10,128,128]{2,1,0:T(8,128)S(1)}, f32[10,128,128]{2,1,0:T(8,128)S(1)}) custom-call(s32[962]{0:T(1024)S(1)} %pad_add_fusion.info, f32[10,128,128]{2,1,0:T(8,128)S(1)} %collective-permute-done.9.refs_0_, ...), custom_call_target="tpu_custom_call", output_to_operand_aliasing={{0}: (6, {}), {1}: (7, {}), {2}: (8, {})} | custom-call | flops 200000000 | bytes 8000000 | tf_op jit(solution)/shard_map/products/pallas_call | solution.py:173
  117.9 0.0 collective-permute-done.11.refs_0_
  117.9 1.9 %collective-permute-start.13 = (f32[10,128,128]{2,1,0:T(8,128)S(1)}, f32[10,128,128]{2,1,0:T(8,128)S(1)}, u32[]{:S(2)}, u32[]{:S(2)}) collective-permute-start(f32[10,128,128]{2,1,0:T(8,128)S(1)} %collective-permute-done.11.refs_0_), channel_id=1, source_target_pairs={{0,1},{8,31},{1,2},{9,8},{2,3},{10,9},{3,4},{11,10},{4,5},{12,11},... | collective-permute-start | bytes 1966088 | tf_op jit(solution)/shard_map/ppermute | solution.py:212
  119.9 2.3 %collective-permute-done.14.refs_1_ = f32[10,128,128]{2,1,0:T(8,128)S(1)} collective-permute-done((f32[10,128,128]{2,1,0:T(8,128)S(1)}, f32[10,128,128]{2,1,0:T(8,128)S(1)}, u32[]{:S(2)}, u32[]{:S(2)}) %collective-permute-start.14) | collective-permute-done | bytes 655392 | tf_op jit(solution)/shard_map/ppermute | solution.py:212
  122.2 9.2 %collective-permute-start.16 = (f32[10,128,128]{2,1,0:T(8,128)S(1)}, f32[10,128,128]{2,1,0:T(8,128)S(1)}, u32[]{:S(2)}, u32[]{:S(2)}) collective-permute-start(f32[10,128,128]{2,1,0:T(8,128)S(1)} %collective-permute-done.14.refs_1_), channel_id=1, source_target_pairs={{0,1},{8,1023},{1,2},{9,8},{2,3},{10,9},{3,4},{11,10},{4,5},{12,11... | collective-permute-start | bytes 1966088 | tf_op jit(solution)/shard_map/ppermute | solution.py:212
  131.5 3.0 %products.16 = (f32[10,128,128]{2,1,0:T(8,128)S(1)}, f32[10,128,128]{2,1,0:T(8,128)S(1)}, f32[10,128,128]{2,1,0:T(8,128)S(1)}) custom-call(s32[962]{0:T(1024)S(1)} %pad_add_fusion.info, f32[10,128,128]{2,1,0:T(8,128)S(1)} %collective-permute-done.11.refs_0_, ...), custom_call_target="tpu_custom_call", output_to_operand_aliasing={{0}: (6, {}), {1}: (7, {}), {2}: (8, {})} | custom-call | flops 200000000 | bytes 8000000 | tf_op jit(solution)/shard_map/products/pallas_call | solution.py:173
  134.5 0.0 collective-permute-done.13.refs_0_
  134.5 1.3 collective-permute-start.15
  135.8 0.7 products.19
  136.5 1.9 %collective-permute-start.18 = (f32[10,128,128]{2,1,0:T(8,128)S(1)}, f32[10,128,128]{2,1,0:T(8,128)S(1)}, u32[]{:S(2)}, u32[]{:S(2)}) collective-permute-start(f32[10,128,128]{2,1,0:T(8,128)S(1)} %products.19), channel_id=1, source_target_pairs={{992,0},{40,8},{993,1},{41,9},{994,2},{42,10},{995,3},{43,11},{996... | collective-permute-start | bytes 1966088 | tf_op jit(solution)/shard_map/ppermute | solution.py:241
  138.4 0.6 collective-permute-done.16.refs_1_
  139.0 2.0 %products.17 = (f32[10,128,128]{2,1,0:T(8,128)S(1)}, f32[10,128,128]{2,1,0:T(8,128)S(1)}) custom-call(s32[962]{0:T(1024)S(1)} %pad_add_fusion.info, f32[10,128,128]{2,1,0:T(8,128)S(1)} %collective-permute-done.13.refs_0_, f32[10,128,128]{2,1,0:T(8,128)S(1)} %collective-permute-done.16.refs_1_, ...), custom_call_target="tpu_custom_call", output_to_operand_aliasing={{0}: (5, {}), {1}: (6, {})} | custom-call | flops 200000000 | bytes 8000000 | tf_op jit(solution)/shard_map/products/pallas_call | solution.py:173
  141.0 13.2 %collective-permute-start.17 = (f32[10,128,128]{2,1,0:T(8,128)S(1)}, f32[10,128,128]{2,1,0:T(8,128)S(1)}, u32[]{:S(2)}, u32[]{:S(2)}) collective-permute-start(f32[10,128,128]{2,1,0:T(8,128)S(1)} %get-tuple-element.103), channel_id=1, source_target_pairs={{0,8},{1,9},{2,10},{3,11},{4,12},{5,13},{6,14},{7,15},{8,0},{9,1},... | collective-permute-start | bytes 1966088 | tf_op jit(solution)/shard_map/ppermute | solution.py:215
  154.1 0.0 collective-permute-done.15.refs_0_
  154.1 0.7 products.18
  154.8 0.0 collective-permute-done.18
  154.8 1.0 collective-permute-done.17
  155.8 0.9 add_bitcast_fusion
  (6 shorter events, 0.1 us)
Async XLA Ops:
  0.0 30.9 %copy-start = (f32[1,10,128,128]{3,2,1,0:T(8,128)S(1)}, f32[1,10,128,128]{3,2,1,0:T(8,128)}, u32[]{:S(2)}) copy-start(f32[1,10,128,128]{3,2,1,0:T(8,128)} %param.2) | copy-start | bytes 1966084
  0.0 23.6 %collective-permute-start = (f32[10,128,128]{2,1,0:T(8,128)}, f32[10,128,128]{2,1,0:T(8,128)S(1)}, u32[]{:S(2)}, u32[]{:S(2)}) collective-permute-start(f32[10,128,128]{2,1,0:T(8,128)} %bitcast.7), channel_id=1, source_target_pairs={{0,8},{1,9},{2,10},{3,11},{4,12},{5,13},{6,14},{7,15},{8,0},{9,1},... | collective-permute-start | bytes 1966088 | tf_op jit(solution)/shard_map/ppermute | solution.py:215
  16.2 19.0 %collective-permute-start.1 = (f32[10,128,128]{2,1,0:T(8,128)}, f32[10,128,128]{2,1,0:T(8,128)S(1)}, u32[]{:S(2)}, u32[]{:S(2)}) collective-permute-start(f32[10,128,128]{2,1,0:T(8,128)} %bitcast.8), channel_id=1, source_target_pairs={{0,1},{8,31},{1,2},{9,8},{2,3},{10,9},{3,4},{11,10},{4,5},{12,11},... | collective-permute-start | bytes 1966088 | tf_op jit(solution)/shard_map/ppermute | solution.py:212
  23.6 14.8 %collective-permute-start.3 = (f32[10,128,128]{2,1,0:T(8,128)S(1)}, f32[10,128,128]{2,1,0:T(8,128)S(1)}, u32[]{:S(2)}, u32[]{:S(2)}) collective-permute-start(f32[10,128,128]{2,1,0:T(8,128)S(1)} %collective-permute-done.refs_1_.refs_3_), channel_id=1, source_target_pairs={{0,1},{8,1023},{1,2},{9,8},{2,3},{10,9},{3,4},{11,10},{4,5},{12,11... | collective-permute-start | bytes 1966088 | tf_op jit(solution)/shard_map/ppermute | solution.py:212
  30.9 18.1 %collective-permute-start.4 = (f32[10,128,128]{2,1,0:T(8,128)S(1)}, f32[10,128,128]{2,1,0:T(8,128)S(1)}, u32[]{:S(2)}, u32[]{:S(2)}) collective-permute-start(f32[10,128,128]{2,1,0:T(8,128)S(1)} %bitcast.9), channel_id=1, source_target_pairs={{0,992},{8,40},{1,993},{9,41},{2,994},{10,42},{3,995},{11,43},{4,9... | collective-permute-start | bytes 1966088 | tf_op jit(solution)/shard_map/ppermute | solution.py:221
  35.2 17.5 %collective-permute-start.2 = (f32[10,128,128]{2,1,0:T(8,128)S(1)}, f32[10,128,128]{2,1,0:T(8,128)S(1)}, u32[]{:S(2)}, u32[]{:S(2)}) collective-permute-start(f32[10,128,128]{2,1,0:T(8,128)S(1)} %collective-permute-done.1.refs_0_), channel_id=1, source_target_pairs={{0,1},{8,31},{1,2},{9,8},{2,3},{10,9},{3,4},{11,10},{4,5},{12,11},... | collective-permute-start | bytes 1966088 | tf_op jit(solution)/shard_map/ppermute | solution.py:212
  38.4 16.8 %collective-permute-start.6 = (f32[10,128,128]{2,1,0:T(8,128)S(1)}, f32[10,128,128]{2,1,0:T(8,128)S(1)}, u32[]{:S(2)}, u32[]{:S(2)}) collective-permute-start(f32[10,128,128]{2,1,0:T(8,128)S(1)} %collective-permute-done.3.refs_1_), channel_id=1, source_target_pairs={{0,1},{8,1023},{1,2},{9,8},{2,3},{10,9},{3,4},{11,10},{4,5},{12,11... | collective-permute-start | bytes 1966088 | tf_op jit(solution)/shard_map/ppermute | solution.py:212
  52.7 15.0 %collective-permute-start.5 = (f32[10,128,128]{2,1,0:T(8,128)S(1)}, f32[10,128,128]{2,1,0:T(8,128)S(1)}, u32[]{:S(2)}, u32[]{:S(2)}) collective-permute-start(f32[10,128,128]{2,1,0:T(8,128)S(1)} %collective-permute-done.2.refs_0_), channel_id=1, source_target_pairs={{0,1},{8,31},{1,2},{9,8},{2,3},{10,9},{3,4},{11,10},{4,5},{12,11},... | collective-permute-start | bytes 1966088 | tf_op jit(solution)/shard_map/ppermute | solution.py:212
  55.2 16.7 %collective-permute-start.8 = (f32[10,128,128]{2,1,0:T(8,128)S(1)}, f32[10,128,128]{2,1,0:T(8,128)S(1)}, u32[]{:S(2)}, u32[]{:S(2)}) collective-permute-start(f32[10,128,128]{2,1,0:T(8,128)S(1)} %collective-permute-done.6.refs_1_), channel_id=1, source_target_pairs={{0,1},{8,1023},{1,2},{9,8},{2,3},{10,9},{3,4},{11,10},{4,5},{12,11... | collective-permute-start | bytes 1966088 | tf_op jit(solution)/shard_map/ppermute | solution.py:212
  67.8 15.5 %collective-permute-start.7 = (f32[10,128,128]{2,1,0:T(8,128)S(1)}, f32[10,128,128]{2,1,0:T(8,128)S(1)}, u32[]{:S(2)}, u32[]{:S(2)}) collective-permute-start(f32[10,128,128]{2,1,0:T(8,128)S(1)} %collective-permute-done.5.refs_0_), channel_id=1, source_target_pairs={{0,1},{8,31},{1,2},{9,8},{2,3},{10,9},{3,4},{11,10},{4,5},{12,11},... | collective-permute-start | bytes 1966088 | tf_op jit(solution)/shard_map/ppermute | solution.py:212
  72.0 16.7 %collective-permute-start.10 = (f32[10,128,128]{2,1,0:T(8,128)S(1)}, f32[10,128,128]{2,1,0:T(8,128)S(1)}, u32[]{:S(2)}, u32[]{:S(2)}) collective-permute-start(f32[10,128,128]{2,1,0:T(8,128)S(1)} %collective-permute-done.8.refs_1_), channel_id=1, source_target_pairs={{0,1},{8,1023},{1,2},{9,8},{2,3},{10,9},{3,4},{11,10},{4,5},{12,11... | collective-permute-start | bytes 1966088 | tf_op jit(solution)/shard_map/ppermute | solution.py:212
  83.3 17.7 %collective-permute-start.9 = (f32[10,128,128]{2,1,0:T(8,128)S(1)}, f32[10,128,128]{2,1,0:T(8,128)S(1)}, u32[]{:S(2)}, u32[]{:S(2)}) collective-permute-start(f32[10,128,128]{2,1,0:T(8,128)S(1)} %collective-permute-done.7.refs_0_), channel_id=1, source_target_pairs={{0,1},{8,31},{1,2},{9,8},{2,3},{10,9},{3,4},{11,10},{4,5},{12,11},... | collective-permute-start | bytes 1966088 | tf_op jit(solution)/shard_map/ppermute | solution.py:212
  88.7 16.7 %collective-permute-start.12 = (f32[10,128,128]{2,1,0:T(8,128)S(1)}, f32[10,128,128]{2,1,0:T(8,128)S(1)}, u32[]{:S(2)}, u32[]{:S(2)}) collective-permute-start(f32[10,128,128]{2,1,0:T(8,128)S(1)} %collective-permute-done.10.refs_1_), channel_id=1, source_target_pairs={{0,1},{8,1023},{1,2},{9,8},{2,3},{10,9},{3,4},{11,10},{4,5},{12,11... | collective-permute-start | bytes 1966088 | tf_op jit(solution)/shard_map/ppermute | solution.py:212
  101.0 16.9 %collective-permute-start.11 = (f32[10,128,128]{2,1,0:T(8,128)S(1)}, f32[10,128,128]{2,1,0:T(8,128)S(1)}, u32[]{:S(2)}, u32[]{:S(2)}) collective-permute-start(f32[10,128,128]{2,1,0:T(8,128)S(1)} %collective-permute-done.9.refs_0_), channel_id=1, source_target_pairs={{0,1},{8,31},{1,2},{9,8},{2,3},{10,9},{3,4},{11,10},{4,5},{12,11},... | collective-permute-start | bytes 1966088 | tf_op jit(solution)/shard_map/ppermute | solution.py:212
  105.5 16.7 %collective-permute-start.14 = (f32[10,128,128]{2,1,0:T(8,128)S(1)}, f32[10,128,128]{2,1,0:T(8,128)S(1)}, u32[]{:S(2)}, u32[]{:S(2)}) collective-permute-start(f32[10,128,128]{2,1,0:T(8,128)S(1)} %collective-permute-done.12.refs_1_), channel_id=1, source_target_pairs={{0,1},{8,1023},{1,2},{9,8},{2,3},{10,9},{3,4},{11,10},{4,5},{12,11... | collective-permute-start | bytes 1966088 | tf_op jit(solution)/shard_map/ppermute | solution.py:212
  117.9 16.5 %collective-permute-start.13 = (f32[10,128,128]{2,1,0:T(8,128)S(1)}, f32[10,128,128]{2,1,0:T(8,128)S(1)}, u32[]{:S(2)}, u32[]{:S(2)}) collective-permute-start(f32[10,128,128]{2,1,0:T(8,128)S(1)} %collective-permute-done.11.refs_0_), channel_id=1, source_target_pairs={{0,1},{8,31},{1,2},{9,8},{2,3},{10,9},{3,4},{11,10},{4,5},{12,11},... | collective-permute-start | bytes 1966088 | tf_op jit(solution)/shard_map/ppermute | solution.py:212
  122.2 16.8 %collective-permute-start.16 = (f32[10,128,128]{2,1,0:T(8,128)S(1)}, f32[10,128,128]{2,1,0:T(8,128)S(1)}, u32[]{:S(2)}, u32[]{:S(2)}) collective-permute-start(f32[10,128,128]{2,1,0:T(8,128)S(1)} %collective-permute-done.14.refs_1_), channel_id=1, source_target_pairs={{0,1},{8,1023},{1,2},{9,8},{2,3},{10,9},{3,4},{11,10},{4,5},{12,11... | collective-permute-start | bytes 1966088 | tf_op jit(solution)/shard_map/ppermute | solution.py:212
  134.5 19.7 %collective-permute-start.15 = (f32[10,128,128]{2,1,0:T(8,128)S(1)}, f32[10,128,128]{2,1,0:T(8,128)S(1)}, u32[]{:S(2)}, u32[]{:S(2)}) collective-permute-start(f32[10,128,128]{2,1,0:T(8,128)S(1)} %collective-permute-done.13.refs_0_), channel_id=1, source_target_pairs={{0,9},{9,0},{10,1},{7,1016},{16,25},{25,16},{26,17},{23,8},{32,41}... | collective-permute-start | bytes 1966088 | tf_op jit(solution)/shard_map/ppermute | solution.py:237
  136.5 18.4 %collective-permute-start.18 = (f32[10,128,128]{2,1,0:T(8,128)S(1)}, f32[10,128,128]{2,1,0:T(8,128)S(1)}, u32[]{:S(2)}, u32[]{:S(2)}) collective-permute-start(f32[10,128,128]{2,1,0:T(8,128)S(1)} %products.19), channel_id=1, source_target_pairs={{992,0},{40,8},{993,1},{41,9},{994,2},{42,10},{995,3},{43,11},{996... | collective-permute-start | bytes 1966088 | tf_op jit(solution)/shard_map/ppermute | solution.py:241
  141.0 14.9 %collective-permute-start.17 = (f32[10,128,128]{2,1,0:T(8,128)S(1)}, f32[10,128,128]{2,1,0:T(8,128)S(1)}, u32[]{:S(2)}, u32[]{:S(2)}) collective-permute-start(f32[10,128,128]{2,1,0:T(8,128)S(1)} %get-tuple-element.103), channel_id=1, source_target_pairs={{0,8},{1,9},{2,10},{3,11},{4,12},{5,13},{6,14},{7,15},{8,0},{9,1},... | collective-permute-start | bytes 1966088 | tf_op jit(solution)/shard_map/ppermute | solution.py:215

commit v4 on v3

--- a/solution.py
+++ b/solution.py
@@ -6,6 +6,9 @@
 from jax.experimental import pallas as pl
 from jax.experimental.pallas import tpu as pltpu
 from jax.sharding import PartitionSpec as P
+
+
+CUTS = ((5,), (5,))
 
 
 def device(line, place, core, depth):
@@ -40,6 +43,7 @@
         for line in range(lines)
         for place in range(2 * depth)
         for core in range(2)
+        if place % depth != (depth - 1 if core == 0 else 0)
     ]
 
 
@@ -48,13 +52,17 @@
     return high, (value - high.astype(jnp.float32)).astype(jnp.bfloat16)
 
 
-def step_kernel(depth, slots, step, rows, targets, pairs, fresh, info, *refs):
-    held, refs = refs[: len(rows)], refs[len(rows) :]
+def step_kernel(depth, slots, step, rows, targets, pairs, fresh, pieces, info, *refs):
+    held = []
+    for count in pieces:
+        held.append(refs[:count])
+        refs = refs[count:]
     factors, refs = refs[: len(targets)], refs[len(targets) :]
     if not fresh:
         refs = refs[len(targets) :]
     sums, refs = refs[: len(targets)], refs[len(targets) :]
     row_buf, factor_buf, sum_buf, row_sem, factor_sem, sum_sem = refs
+    width = max(pieces)
 
     place, core = info[0], info[1]
     half, low = place // depth, place % depth
@@ -91,8 +99,13 @@
     row_used = [any_of(lambda p, r=r: p[0] == r) for r in range(len(rows))]
     sum_used = [any_of(lambda p, t=t: p[1] == t) for t in range(len(targets))]
 
-    def row_copy(r):
-        return pltpu.make_async_copy(held[r], row_buf.at[r], row_sem.at[r])
+    def row_copies(r):
+        out, at = [], 0
+        for n, piece in enumerate(held[r]):
+            here = row_buf.at[r, pl.ds(at, piece.shape[0])]
+            out.append(pltpu.make_async_copy(piece, here, row_sem.at[r * width + n]))
+            at += piece.shape[0]
+        return out
 
     def factor_copy(n):
         t = pairs[n][1]
@@ -108,7 +121,8 @@
 
     for phase in ("start", "wait"):
         for r in range(len(rows)):
-            pl.when(row_used[r])(getattr(row_copy(r), phase))
+            for copy in row_copies(r):
+                pl.when(row_used[r])(getattr(copy, phase))
         for n in range(len(pairs)):
             pl.when(found[n][0])(getattr(factor_copy(n), phase))
         if not fresh:
@@ -163,15 +177,16 @@
 
 
 def step_call(depth, step, rows, targets, pairs, info, held, factors, sums=None):
-    slots, edge = held[0].shape[:2]
+    slots, edge = factors[0].shape[:2]
     fresh = sums is None
-    shape = jax.ShapeDtypeStruct(held[0].shape, jnp.float32)
+    shape = jax.ShapeDtypeStruct(factors[0].shape, jnp.float32)
     hbm = pl.BlockSpec(memory_space=pl.ANY)
-    operands = [info, *held, *factors] + ([] if fresh else list(sums))
-    first = 1 + len(held) + len(factors)
+    pieces = tuple(len(row) for row in held)
+    operands = [info, *sum(held, []), *factors] + ([] if fresh else list(sums))
+    first = 1 + sum(pieces) + len(factors)
     return list(
         pl.pallas_call(
-            functools.partial(step_kernel, depth, slots, step, rows, targets, pairs, fresh),
+            functools.partial(step_kernel, depth, slots, step, rows, targets, pairs, fresh, pieces),
             out_shape=[shape] * len(targets),
             in_specs=[pl.BlockSpec(memory_space=pltpu.SMEM)] + [hbm] * (len(operands) - 1),
             out_specs=[hbm] * len(targets),
@@ -180,7 +195,7 @@
                 pltpu.VMEM((len(rows), *shape.shape), jnp.float32),
                 pltpu.VMEM((len(pairs), edge, edge), jnp.float32),
                 pltpu.VMEM((len(targets), *shape.shape), jnp.float32),
-                pltpu.SemaphoreType.DMA((len(rows),)),
+                pltpu.SemaphoreType.DMA((len(rows) * max(pieces),)),
                 pltpu.SemaphoreType.DMA((len(pairs),)),
                 pltpu.SemaphoreType.DMA((len(targets),)),
             ],
@@ -209,32 +224,39 @@
     )
 
     def hop(held, step, which):
-        return lax.ppermute(held[which], every, hop_pairs(lines, depth, step, which))
+        pairs = hop_pairs(lines, depth, step, which)
+        return [lax.ppermute(piece, every, pairs) for piece in held[which]]
 
     def flip(value):
         return lax.ppermute(value, ring, flip_pairs(depth))
 
     own = blocks[0]
     other, info = lax.optimization_barrier((flip(own), info))
-    held = [own, other]
     away = line_pairs(lines, depth)
     ghost = lax.ppermute(own, every, away)
-    factors = [held[0], held[1], ghost]
-    sums = step_call(depth, 0, (0, 1), (0,), ((0, 0), (1, 0)), info, held, factors[:1])
+    factors = [own, other, ghost]
+    sums = step_call(
+        depth, 0, (0, 1), (0,), ((0, 0), (1, 0)), info, [[own], [other]], factors[:1]
+    )
     sums += [jnp.zeros_like(own) for _ in range(2)]
+    held = [
+        [value[a:b] for a, b in zip((0, *cuts), (*cuts, slots))]
+        for value, cuts in zip((own, other), CUTS)
+    ]
     held = [hop(held, 1, which) for which in range(2)]
     for step in range(1, depth - 1):
-        held[0], sums = lax.optimization_barrier((held[0], sums))
-        after = [hop(held, step + 1, which) for which in range(2)]
+        held[0][0], sums = lax.optimization_barrier((held[0][0], sums))
+        going = [held[0], held[1] if step < depth - 2 else [jnp.concatenate(held[1])]]
+        after = [hop(going, step + 1, which) for which in range(2)]
         pairs = ((0, 0), (0, 1), (0, 2), (1, 0), (1, 1))
         sums = step_call(depth, step, (0, 1), (0, 1, 2), pairs, info, held, factors, sums)
         held = after
     last = depth - 1
-    held[0], sums = lax.optimization_barrier((held[0], sums))
+    held[0][0], sums = lax.optimization_barrier((held[0][0], sums))
     far = [
         p for p in hop_pairs(lines, depth, depth, 0, across=True) if p[1] % depth < slots - depth
     ]
-    far = lax.ppermute(held[0], every, far)
+    far = [lax.ppermute(jnp.concatenate(held[0]), every, far)]
     (foreign,) = step_call(
         depth, last, (0,), (2,), ((0, 0),), info, held[:1], factors[2:], sums[2:]
     )

time: 157 us -> 156 us (level)
  the two profiles are of different devices: /device:TPU:1 before, /device:TPU:65 now
where the time goes in v4:
time: 156 us; the launch traced here: 155 us
  starting transfers between devices  122 us (78%)
  Pallas kernels  22.8 us (15%)
  waiting for transfers between devices  5.84 us (4%)
  local copies, waits for them, and re-layouts  1.99 us (1%)
    ppermute x27, starting transfers between devices, hop(): return [lax.ppermute(piece, every, pairs) for piece in held[which]]  101 us
    pallas_call x10, Pallas kernels, step_call(): pl.pallas_call(functools.partial(step_kernel, depth, slots, step, rows, t...  22.8 us
    ppermute x1, starting transfers between devices, body(): foreign = lax.ppermute(foreign, every, [(b, a) for a, b in away])  9.83 us
    ppermute x1, starting transfers between devices, body(): far = [lax.ppermute(jnp.concatenate(held[0]), every, far)]  4.75 us
    ppermute x2, starting transfers between devices, flip(): return lax.ppermute(value, ring, flip_pairs(depth))  4.49 us
    ppermute x27, waiting for transfers between devices, hop(): return [lax.ppermute(piece, every, pairs) for piece in held[which]]  4.12 us
  transfers between devices with their start and end apart: 32, of which 3 were waited for; matrix products, arithmetic and copies ran while one was open for 1% of the time, Pallas kernels for 15%

profile of v4, /device:TPU:65, one launch (start us, length us, event | category | flops | bytes accessed | tf_op | source)
XLA Modules:
  0.0 154.7 jit_solution(7567238986568343146)
XLA Ops:
  0.0 2.6 %collective-permute-start = (f32[10,128,128]{2,1,0:T(8,128)}, f32[10,128,128]{2,1,0:T(8,128)S(1)}, u32[]{:S(2)}, u32[]{:S(2)}) collective-permute-start(f32[10,128,128]{2,1,0:T(8,128)} %bitcast.11), channel_id=1, source_target_pairs={{0,8},{1,9},{2,10},{3,11},{4,12},{5,13},{6,14},{7,15},{8,0},{9,1},... | collective-permute-start | bytes 1966088 | tf_op jit(solution)/shard_map/ppermute | solution.py:231
  2.6 1.1 copy.26
  3.7 0.6 gather_fusion
  4.3 0.1 subtract_add_fusion
  4.4 0.1 add.101
  4.6 0.1 pad_add_fusion.info
  4.7 0.0 collective-permute-done.refs_1_.refs_5_.refs_4_
  4.7 14.1 %collective-permute-start.4 = (f32[5,128,128]{2,1,0:T(8,128)S(1)}, f32[5,128,128]{2,1,0:T(8,128)S(1)}, u32[]{:S(2)}, u32[]{:S(2)}) collective-permute-start(f32[5,128,128]{2,1,0:T(8,128)S(1)} %get-tuple-element.106), channel_id=1, source_target_pairs={{0,1},{8,1023},{1,2},{9,8},{2,3},{10,9},{3,4},{11,10},{4,5},{12,11... | collective-permute-start | bytes 983048 | tf_op jit(solution)/shard_map/ppermute | solution.py:228
  18.8 10.4 %collective-permute-start.5 = (f32[5,128,128]{2,1,0:T(8,128)S(1)}, f32[5,128,128]{2,1,0:T(8,128)S(1)}, u32[]{:S(2)}, u32[]{:S(2)}) collective-permute-start(f32[5,128,128]{2,1,0:T(8,128)S(1)} %get-tuple-element.105), channel_id=1, source_target_pairs={{0,1},{8,1023},{1,2},{9,8},{2,3},{10,9},{3,4},{11,10},{4,5},{12,11... | collective-permute-start | bytes 983048 | tf_op jit(solution)/shard_map/ppermute | solution.py:228
  29.2 1.9 %collective-permute-start.6 = (f32[10,128,128]{2,1,0:T(8,128)S(1)}, f32[10,128,128]{2,1,0:T(8,128)S(1)}, u32[]{:S(2)}, u32[]{:S(2)}) collective-permute-start(f32[10,128,128]{2,1,0:T(8,128)S(1)} %bitcast.12), channel_id=1, source_target_pairs={{0,992},{1,993},{9,41},{2,994},{10,42},{3,995},{11,43},{4,996},{12... | collective-permute-start | bytes 1966088 | tf_op jit(solution)/shard_map/ppermute | solution.py:236
  31.2 1.9 %collective-permute-start.1 = (f32[5,128,128]{2,1,0:T(8,128)S(1)}, f32[5,128,128]{2,1,0:T(8,128)S(1)}, u32[]{:S(2)}, u32[]{:S(2)}) collective-permute-start(f32[5,128,128]{2,1,0:T(8,128)S(1)} %get-tuple-element.108), channel_id=1, source_target_pairs={{0,1},{8,31},{1,2},{9,8},{2,3},{10,9},{3,4},{11,10},{4,5},{12,11},... | collective-permute-start | bytes 983048 | tf_op jit(solution)/shard_map/ppermute | solution.py:228
  33.1 1.9 %collective-permute-start.3 = (f32[5,128,128]{2,1,0:T(8,128)S(1)}, f32[5,128,128]{2,1,0:T(8,128)S(1)}, u32[]{:S(2)}, u32[]{:S(2)}) collective-permute-start(f32[5,128,128]{2,1,0:T(8,128)S(1)} %get-tuple-element.107), channel_id=1, source_target_pairs={{0,1},{8,31},{1,2},{9,8},{2,3},{10,9},{3,4},{11,10},{4,5},{12,11},... | collective-permute-start | bytes 983048 | tf_op jit(solution)/shard_map/ppermute | solution.py:228
  35.1 1.9 %collective-permute-start.9 = (f32[5,128,128]{2,1,0:T(8,128)S(1)}, f32[5,128,128]{2,1,0:T(8,128)S(1)}, u32[]{:S(2)}, u32[]{:S(2)}) collective-permute-start(f32[5,128,128]{2,1,0:T(8,128)S(1)} %collective-permute-done.4.refs_2_), channel_id=1, source_target_pairs={{0,1},{8,1023},{1,2},{9,8},{2,3},{10,9},{3,4},{11,10},{4,5},{12,11... | collective-permute-start | bytes 983048 | tf_op jit(solution)/shard_map/ppermute | solution.py:228
  37.0 0.0 collective-permute-done.5.refs_3_
  37.0 5.4 %collective-permute-start.10 = (f32[5,128,128]{2,1,0:T(8,128)S(1)}, f32[5,128,128]{2,1,0:T(8,128)S(1)}, u32[]{:S(2)}, u32[]{:S(2)}) collective-permute-start(f32[5,128,128]{2,1,0:T(8,128)S(1)} %collective-permute-done.5.refs_3_), channel_id=1, source_target_pairs={{0,1},{8,1023},{1,2},{9,8},{2,3},{10,9},{3,4},{11,10},{4,5},{12,11... | collective-permute-start | bytes 983048 | tf_op jit(solution)/shard_map/ppermute | solution.py:228
  42.5 2.4 %products.10.refs_7_ = f32[10,128,128]{2,1,0:T(8,128)S(1)} custom-call(s32[962]{0:T(1024)S(1)} %pad_add_fusion.info, f32[10,128,128]{2,1,0:T(8,128)S(1)} %bitcast.13, f32[10,128,128]{2,1,0:T(8,128)S(1)} %collective-permute-done.refs_1_.refs_5_.refs_4_, f32[10,128,128]{2,1,0:T(8,128)S(1)} %bitcast.14), custom_call_target="tpu_custom_call" | custom-call | flops 200000000 | bytes 8000000 | tf_op jit(solution)/shard_map/products/pallas_call | solution.py:188
  44.8 0.0 collective-permute-done.1.refs_0_
  44.9 2.8 %collective-permute-start.2 = (f32[5,128,128]{2,1,0:T(8,128)S(1)}, f32[5,128,128]{2,1,0:T(8,128)S(1)}, u32[]{:S(2)}, u32[]{:S(2)}) collective-permute-start(f32[5,128,128]{2,1,0:T(8,128)S(1)} %collective-permute-done.1.refs_0_), channel_id=1, source_target_pairs={{0,1},{8,31},{1,2},{9,8},{2,3},{10,9},{3,4},{11,10},{4,5},{12,11},... | collective-permute-start | bytes 983048 | tf_op jit(solution)/shard_map/ppermute | solution.py:228
  47.7 0.0 collective-permute-done.3.refs_1_
  47.7 1.9 %collective-permute-start.8 = (f32[5,128,128]{2,1,0:T(8,128)S(1)}, f32[5,128,128]{2,1,0:T(8,128)S(1)}, u32[]{:S(2)}, u32[]{:S(2)}) collective-permute-start(f32[5,128,128]{2,1,0:T(8,128)S(1)} %collective-permute-done.3.refs_1_), channel_id=1, source_target_pairs={{0,1},{8,31},{1,2},{9,8},{2,3},{10,9},{3,4},{11,10},{4,5},{12,11},... | collective-permute-start | bytes 983048 | tf_op jit(solution)/shard_map/ppermute | solution.py:228
  49.6 1.9 %collective-permute-start.13 = (f32[5,128,128]{2,1,0:T(8,128)S(1)}, f32[5,128,128]{2,1,0:T(8,128)S(1)}, u32[]{:S(2)}, u32[]{:S(2)}) collective-permute-start(f32[5,128,128]{2,1,0:T(8,128)S(1)} %collective-permute-done.9.refs_2_), channel_id=1, source_target_pairs={{0,1},{8,1023},{1,2},{9,8},{2,3},{10,9},{3,4},{11,10},{4,5},{12,11... | collective-permute-start | bytes 983048 | tf_op jit(solution)/shard_map/ppermute | solution.py:228
  51.5 0.0 collective-permute-done.10.refs_3_
  51.5 4.9 %collective-permute-start.14 = (f32[5,128,128]{2,1,0:T(8,128)S(1)}, f32[5,128,128]{2,1,0:T(8,128)S(1)}, u32[]{:S(2)}, u32[]{:S(2)}) collective-permute-start(f32[5,128,128]{2,1,0:T(8,128)S(1)} %collective-permute-done.10.refs_3_), channel_id=1, source_target_pairs={{0,1},{8,1023},{1,2},{9,8},{2,3},{10,9},{3,4},{11,10},{4,5},{12,11... | collective-permute-start | bytes 983048 | tf_op jit(solution)/shard_map/ppermute | solution.py:228
  56.6 0.0 collective-permute-done.6.refs_6_.refs_2_
  56.6 3.1 %products.11 = (f32[10,128,128]{2,1,0:T(8,128)S(1)}, f32[10,128,128]{2,1,0:T(8,128)S(1)}, f32[10,128,128]{2,1,0:T(8,128)S(1)}) custom-call(s32[962]{0:T(1024)S(1)} %pad_add_fusion.info, f32[5,128,128]{2,1,0:T(8,128)S(1)} %collective-permute-done.1.refs_0_, ...), custom_call_target="tpu_custom_call", output_to_operand_aliasing={{0}: (8, {}), {1}: (9, {}), {2}: (10, {})} | custom-call | flops 200000000 | bytes 8000000 | tf_op jit(solution)/shard_map/products/pallas_call | solution.py:188
  59.7 0.0 collective-permute-done.2.refs_0_
  59.7 2.5 %collective-permute-start.7 = (f32[5,128,128]{2,1,0:T(8,128)S(1)}, f32[5,128,128]{2,1,0:T(8,128)S(1)}, u32[]{:S(2)}, u32[]{:S(2)}) collective-permute-start(f32[5,128,128]{2,1,0:T(8,128)S(1)} %collective-permute-done.2.refs_0_), channel_id=1, source_target_pairs={{0,1},{8,31},{1,2},{9,8},{2,3},{10,9},{3,4},{11,10},{4,5},{12,11},... | collective-permute-start | bytes 983048 | tf_op jit(solution)/shard_map/ppermute | solution.py:228
  62.3 1.9 %collective-permute-start.12 = (f32[5,128,128]{2,1,0:T(8,128)S(1)}, f32[5,128,128]{2,1,0:T(8,128)S(1)}, u32[]{:S(2)}, u32[]{:S(2)}) collective-permute-start(f32[5,128,128]{2,1,0:T(8,128)S(1)} %collective-permute-done.8.refs_1_), channel_id=1, source_target_pairs={{0,1},{8,31},{1,2},{9,8},{2,3},{10,9},{3,4},{11,10},{4,5},{12,11},... | collective-permute-start | bytes 983048 | tf_op jit(solution)/shard_map/ppermute | solution.py:228
  64.2 0.0 collective-permute-done.13.refs_2_
  64.2 1.9 %collective-permute-start.17 = (f32[5,128,128]{2,1,0:T(8,128)S(1)}, f32[5,128,128]{2,1,0:T(8,128)S(1)}, u32[]{:S(2)}, u32[]{:S(2)}) collective-permute-start(f32[5,128,128]{2,1,0:T(8,128)S(1)} %collective-permute-done.13.refs_2_), channel_id=1, source_target_pairs={{0,1},{8,1023},{1,2},{9,8},{2,3},{10,9},{3,4},{11,10},{4,5},{12,11... | collective-permute-start | bytes 983048 | tf_op jit(solution)/shard_map/ppermute | solution.py:228
  66.1 4.4 %collective-permute-start.18 = (f32[5,128,128]{2,1,0:T(8,128)S(1)}, f32[5,128,128]{2,1,0:T(8,128)S(1)}, u32[]{:S(2)}, u32[]{:S(2)}) collective-permute-start(f32[5,128,128]{2,1,0:T(8,128)S(1)} %collective-permute-done.14.refs_3_), channel_id=1, source_target_pairs={{0,1},{8,1023},{1,2},{9,8},{2,3},{10,9},{3,4},{11,10},{4,5},{12,11... | collective-permute-start | bytes 983048 | tf_op jit(solution)/shard_map/ppermute | solution.py:228
  70.5 3.3 %products.12 = (f32[10,128,128]{2,1,0:T(8,128)S(1)}, f32[10,128,128]{2,1,0:T(8,128)S(1)}, f32[10,128,128]{2,1,0:T(8,128)S(1)}) custom-call(s32[962]{0:T(1024)S(1)} %pad_add_fusion.info, f32[5,128,128]{2,1,0:T(8,128)S(1)} %collective-permute-done.2.refs_0_, ...), custom_call_target="tpu_custom_call", output_to_operand_aliasing={{0}: (8, {}), {1}: (9, {}), {2}: (10, {})} | custom-call | flops 200000000 | bytes 8000000 | tf_op jit(solution)/shard_map/products/pallas_call | solution.py:188
  73.9 3.3 %collective-permute-start.11 = (f32[5,128,128]{2,1,0:T(8,128)S(1)}, f32[5,128,128]{2,1,0:T(8,128)S(1)}, u32[]{:S(2)}, u32[]{:S(2)}) collective-permute-start(f32[5,128,128]{2,1,0:T(8,128)S(1)} %collective-permute-done.7.refs_0_), channel_id=1, source_target_pairs={{0,1},{8,31},{1,2},{9,8},{2,3},{10,9},{3,4},{11,10},{4,5},{12,11},... | collective-permute-start | bytes 983048 | tf_op jit(solution)/shard_map/ppermute | solution.py:228
  77.2 0.0 collective-permute-done.12.refs_1_
  77.2 1.9 %collective-permute-start.16 = (f32[5,128,128]{2,1,0:T(8,128)S(1)}, f32[5,128,128]{2,1,0:T(8,128)S(1)}, u32[]{:S(2)}, u32[]{:S(2)}) collective-permute-start(f32[5,128,128]{2,1,0:T(8,128)S(1)} %collective-permute-done.12.refs_1_), channel_id=1, source_target_pairs={{0,1},{8,31},{1,2},{9,8},{2,3},{10,9},{3,4},{11,10},{4,5},{12,11},... | collective-permute-start | bytes 983048 | tf_op jit(solution)/shard_map/ppermute | solution.py:228
  79.1 0.0 collective-permute-done.17.refs_2_
  79.1 1.9 %collective-permute-start.21 = (f32[5,128,128]{2,1,0:T(8,128)S(1)}, f32[5,128,128]{2,1,0:T(8,128)S(1)}, u32[]{:S(2)}, u32[]{:S(2)}) collective-permute-start(f32[5,128,128]{2,1,0:T(8,128)S(1)} %collective-permute-done.17.refs_2_), channel_id=1, source_target_pairs={{0,1},{8,1023},{1,2},{9,8},{2,3},{10,9},{3,4},{11,10},{4,5},{12,11... | collective-permute-start | bytes 983048 | tf_op jit(solution)/shard_map/ppermute | solution.py:228
  81.0 6.6 %collective-permute-start.22 = (f32[5,128,128]{2,1,0:T(8,128)S(1)}, f32[5,128,128]{2,1,0:T(8,128)S(1)}, u32[]{:S(2)}, u32[]{:S(2)}) collective-permute-start(f32[5,128,128]{2,1,0:T(8,128)S(1)} %collective-permute-done.18.refs_3_), channel_id=1, source_target_pairs={{0,1},{8,1023},{1,2},{9,8},{2,3},{10,9},{3,4},{11,10},{4,5},{12,11... | collective-permute-start | bytes 983048 | tf_op jit(solution)/shard_map/ppermute | solution.py:228
  87.7 2.1 %products.13 = (f32[10,128,128]{2,1,0:T(8,128)S(1)}, f32[10,128,128]{2,1,0:T(8,128)S(1)}, f32[10,128,128]{2,1,0:T(8,128)S(1)}) custom-call(s32[962]{0:T(1024)S(1)} %pad_add_fusion.info, f32[5,128,128]{2,1,0:T(8,128)S(1)} %collective-permute-done.7.refs_0_, ...), custom_call_target="tpu_custom_call", output_to_operand_aliasing={{0}: (8, {}), {1}: (9, {}), {2}: (10, {})} | custom-call | flops 200000000 | bytes 8000000 | tf_op jit(solution)/shard_map/products/pallas_call | solution.py:188
  89.8 3.9 %collective-permute-start.15 = (f32[5,128,128]{2,1,0:T(8,128)S(1)}, f32[5,128,128]{2,1,0:T(8,128)S(1)}, u32[]{:S(2)}, u32[]{:S(2)}) collective-permute-start(f32[5,128,128]{2,1,0:T(8,128)S(1)} %collective-permute-done.11.refs_0_), channel_id=1, source_target_pairs={{0,1},{8,31},{1,2},{9,8},{2,3},{10,9},{3,4},{11,10},{4,5},{12,11},... | collective-permute-start | bytes 983048 | tf_op jit(solution)/shard_map/ppermute | solution.py:228
  93.7 0.0 collective-permute-done.16.refs_1_
  93.7 1.9 %collective-permute-start.20 = (f32[5,128,128]{2,1,0:T(8,128)S(1)}, f32[5,128,128]{2,1,0:T(8,128)S(1)}, u32[]{:S(2)}, u32[]{:S(2)}) collective-permute-start(f32[5,128,128]{2,1,0:T(8,128)S(1)} %collective-permute-done.16.refs_1_), channel_id=1, source_target_pairs={{0,1},{8,31},{1,2},{9,8},{2,3},{10,9},{3,4},{11,10},{4,5},{12,11},... | collective-permute-start | bytes 983048 | tf_op jit(solution)/shard_map/ppermute | solution.py:228
  95.7 1.9 %collective-permute-start.25 = (f32[5,128,128]{2,1,0:T(8,128)S(1)}, f32[5,128,128]{2,1,0:T(8,128)S(1)}, u32[]{:S(2)}, u32[]{:S(2)}) collective-permute-start(f32[5,128,128]{2,1,0:T(8,128)S(1)} %collective-permute-done.21.refs_2_), channel_id=1, source_target_pairs={{0,1},{8,1023},{1,2},{9,8},{2,3},{10,9},{3,4},{11,10},{4,5},{12,11... | collective-permute-start | bytes 983048 | tf_op jit(solution)/shard_map/ppermute | solution.py:228
  97.6 0.0 collective-permute-done.22.refs_3_
  97.6 4.3 %collective-permute-start.26 = (f32[5,128,128]{2,1,0:T(8,128)S(1)}, f32[5,128,128]{2,1,0:T(8,128)S(1)}, u32[]{:S(2)}, u32[]{:S(2)}) collective-permute-start(f32[5,128,128]{2,1,0:T(8,128)S(1)} %collective-permute-done.22.refs_3_), channel_id=1, source_target_pairs={{0,1},{8,1023},{1,2},{9,8},{2,3},{10,9},{3,4},{11,10},{4,5},{12,11... | collective-permute-start | bytes 983048 | tf_op jit(solution)/shard_map/ppermute | solution.py:228
  101.9 3.1 %products.14 = (f32[10,128,128]{2,1,0:T(8,128)S(1)}, f32[10,128,128]{2,1,0:T(8,128)S(1)}, f32[10,128,128]{2,1,0:T(8,128)S(1)}) custom-call(s32[962]{0:T(1024)S(1)} %pad_add_fusion.info, f32[5,128,128]{2,1,0:T(8,128)S(1)} %collective-permute-done.11.refs_0_, ...), custom_call_target="tpu_custom_call", output_to_operand_aliasing={{0}: (8, {}), {1}: (9, {}), {2}: (10, {})} | custom-call | flops 200000000 | bytes 8000000 | tf_op jit(solution)/shard_map/products/pallas_call | solution.py:188
  105.0 2.5 %collective-permute-start.19 = (f32[5,128,128]{2,1,0:T(8,128)S(1)}, f32[5,128,128]{2,1,0:T(8,128)S(1)}, u32[]{:S(2)}, u32[]{:S(2)}) collective-permute-start(f32[5,128,128]{2,1,0:T(8,128)S(1)} %collective-permute-done.15.refs_0_), channel_id=1, source_target_pairs={{0,1},{8,31},{1,2},{9,8},{2,3},{10,9},{3,4},{11,10},{4,5},{12,11},... | collective-permute-start | bytes 983048 | tf_op jit(solution)/shard_map/ppermute | solution.py:228
  107.5 1.9 %collective-permute-start.24 = (f32[5,128,128]{2,1,0:T(8,128)S(1)}, f32[5,128,128]{2,1,0:T(8,128)S(1)}, u32[]{:S(2)}, u32[]{:S(2)}) collective-permute-start(f32[5,128,128]{2,1,0:T(8,128)S(1)} %collective-permute-done.20.refs_1_), channel_id=1, source_target_pairs={{0,1},{8,31},{1,2},{9,8},{2,3},{10,9},{3,4},{11,10},{4,5},{12,11},... | collective-permute-start | bytes 983048 | tf_op jit(solution)/shard_map/ppermute | solution.py:228
  109.5 0.0 collective-permute-done.25.refs_2_
  109.6 2.8 %collective-permute-start.29 = (f32[10,128,128]{2,1,0:T(8,128)S(1)}, f32[10,128,128]{2,1,0:T(8,128)S(1)}, u32[]{:S(2)}, u32[]{:S(2)}) collective-permute-start(f32[10,128,128]{2,1,0:T(8,128)S(1)} %pad_maximum_fusion.1), channel_id=1, source_target_pairs={{0,1},{8,1023},{1,2},{9,8},{2,3},{10,9},{3,4},{11,10},{4,5},{12,11... | collective-permute-start | bytes 1966088 | tf_op jit(solution)/shard_map/ppermute | solution.py:228
  112.4 2.1 %products.15 = (f32[10,128,128]{2,1,0:T(8,128)S(1)}, f32[10,128,128]{2,1,0:T(8,128)S(1)}, f32[10,128,128]{2,1,0:T(8,128)S(1)}) custom-call(s32[962]{0:T(1024)S(1)} %pad_add_fusion.info, f32[5,128,128]{2,1,0:T(8,128)S(1)} %collective-permute-done.15.refs_0_, ...), custom_call_target="tpu_custom_call", output_to_operand_aliasing={{0}: (8, {}), {1}: (9, {}), {2}: (10, {})} | custom-call | flops 200000000 | bytes 8000000 | tf_op jit(solution)/shard_map/products/pallas_call | solution.py:188
  114.5 8.2 %collective-permute-start.23 = (f32[5,128,128]{2,1,0:T(8,128)S(1)}, f32[5,128,128]{2,1,0:T(8,128)S(1)}, u32[]{:S(2)}, u32[]{:S(2)}) collective-permute-start(f32[5,128,128]{2,1,0:T(8,128)S(1)} %collective-permute-done.19.refs_0_), channel_id=1, source_target_pairs={{0,1},{8,31},{1,2},{9,8},{2,3},{10,9},{3,4},{11,10},{4,5},{12,11},... | collective-permute-start | bytes 983048 | tf_op jit(solution)/shard_map/ppermute | solution.py:228
  122.8 1.9 %collective-permute-start.27 = (f32[5,128,128]{2,1,0:T(8,128)S(1)}, f32[5,128,128]{2,1,0:T(8,128)S(1)}, u32[]{:S(2)}, u32[]{:S(2)}) collective-permute-start(f32[5,128,128]{2,1,0:T(8,128)S(1)} %collective-permute-done.24.refs_1_), channel_id=1, source_target_pairs={{0,1},{8,31},{1,2},{9,8},{2,3},{10,9},{3,4},{11,10},{4,5},{12,11},... | collective-permute-start | bytes 983048 | tf_op jit(solution)/shard_map/ppermute | solution.py:228
  124.7 2.1 %products.16 = (f32[10,128,128]{2,1,0:T(8,128)S(1)}, f32[10,128,128]{2,1,0:T(8,128)S(1)}, f32[10,128,128]{2,1,0:T(8,128)S(1)}) custom-call(s32[962]{0:T(1024)S(1)} %pad_add_fusion.info, f32[5,128,128]{2,1,0:T(8,128)S(1)} %collective-permute-done.19.refs_0_, ...), custom_call_target="tpu_custom_call", output_to_operand_aliasing={{0}: (8, {}), {1}: (9, {}), {2}: (10, {})} | custom-call | flops 200000000 | bytes 8000000 | tf_op jit(solution)/shard_map/products/pallas_call | solution.py:188
  126.9 0.3 collective-permute-done.23.refs_0_
  127.2 3.8 %collective-permute-done.27.refs_1_ = f32[5,128,128]{2,1,0:T(8,128)S(1)} collective-permute-done((f32[5,128,128]{2,1,0:T(8,128)S(1)}, f32[5,128,128]{2,1,0:T(8,128)S(1)}, u32[]{:S(2)}, u32[]{:S(2)}) %collective-permute-start.27) | collective-permute-done | bytes 327712 | tf_op jit(solution)/shard_map/ppermute | solution.py:228
  131.0 4.8 %collective-permute-start.28 = (f32[10,128,128]{2,1,0:T(8,128)S(1)}, f32[10,128,128]{2,1,0:T(8,128)S(1)}, u32[]{:S(2)}, u32[]{:S(2)}) collective-permute-start(f32[10,128,128]{2,1,0:T(8,128)S(1)} %pad_maximum_fusion), channel_id=1, source_target_pairs={{0,9},{9,0},{10,1},{7,1016},{16,25},{25,16},{26,17},{23,8},{32,41}... | collective-permute-start | bytes 1966088 | tf_op jit(solution)/shard_map/ppermute | solution.py:259
  135.7 0.7 products.19
  136.4 9.8 %collective-permute-start.31 = (f32[10,128,128]{2,1,0:T(8,128)S(1)}, f32[10,128,128]{2,1,0:T(8,128)S(1)}, u32[]{:S(2)}, u32[]{:S(2)}) collective-permute-start(f32[10,128,128]{2,1,0:T(8,128)S(1)} %products.19), channel_id=1, source_target_pairs={{992,0},{993,1},{41,9},{994,2},{42,10},{995,3},{43,11},{996,4},{44... | collective-permute-start | bytes 1966088 | tf_op jit(solution)/shard_map/ppermute | solution.py:263
  146.3 3.2 %products.17 = (f32[10,128,128]{2,1,0:T(8,128)S(1)}, f32[10,128,128]{2,1,0:T(8,128)S(1)}) custom-call(s32[962]{0:T(1024)S(1)} %pad_add_fusion.info, f32[5,128,128]{2,1,0:T(8,128)S(1)} %collective-permute-done.23.refs_0_, f32[5,128,128]{2,1,0:T(8,128)S(1)} %collective-permute-done.27.refs_1_, ...), custom_call_target="tpu_custom_call", output_to_operand_aliasing={{0}: (6, {}), {1}: (7, {})} | custom-call | flops 200000000 | bytes 8000000 | tf_op jit(solution)/shard_map/products/pallas_call | solution.py:188
  149.4 1.9 %collective-permute-start.30 = (f32[10,128,128]{2,1,0:T(8,128)S(1)}, f32[10,128,128]{2,1,0:T(8,128)S(1)}, u32[]{:S(2)}, u32[]{:S(2)}) collective-permute-start(f32[10,128,128]{2,1,0:T(8,128)S(1)} %get-tuple-element.103), channel_id=1, source_target_pairs={{0,8},{1,9},{2,10},{3,11},{4,12},{5,13},{6,14},{7,15},{8,0},{9,1},... | collective-permute-start | bytes 1966088 | tf_op jit(solution)/shard_map/ppermute | solution.py:231
  151.4 0.7 products.18
  152.1 1.7 %collective-permute-done.31 = f32[10,128,128]{2,1,0:T(8,128)S(1)} collective-permute-done((f32[10,128,128]{2,1,0:T(8,128)S(1)}, f32[10,128,128]{2,1,0:T(8,128)S(1)}, u32[]{:S(2)}, u32[]{:S(2)}) %collective-permute-start.31) | collective-permute-done | bytes 655392 | tf_op jit(solution)/shard_map/ppermute | solution.py:263
  153.8 0.9 add_bitcast_fusion
  (28 shorter events, 0.4 us)
Async XLA Ops:
  0.0 4.7 %collective-permute-start = (f32[10,128,128]{2,1,0:T(8,128)}, f32[10,128,128]{2,1,0:T(8,128)S(1)}, u32[]{:S(2)}, u32[]{:S(2)}) collective-permute-start(f32[10,128,128]{2,1,0:T(8,128)} %bitcast.11), channel_id=1, source_target_pairs={{0,8},{1,9},{2,10},{3,11},{4,12},{5,13},{6,14},{7,15},{8,0},{9,1},... | collective-permute-start | bytes 1966088 | tf_op jit(solution)/shard_map/ppermute | solution.py:231
  4.7 24.5 %copy-start = (f32[1,10,128,128]{3,2,1,0:T(8,128)S(1)}, f32[1,10,128,128]{3,2,1,0:T(8,128)}, u32[]{:S(2)}) copy-start(f32[1,10,128,128]{3,2,1,0:T(8,128)} %param.2) | copy-start | bytes 1966084
  4.7 30.3 %collective-permute-start.4 = (f32[5,128,128]{2,1,0:T(8,128)S(1)}, f32[5,128,128]{2,1,0:T(8,128)S(1)}, u32[]{:S(2)}, u32[]{:S(2)}) collective-permute-start(f32[5,128,128]{2,1,0:T(8,128)S(1)} %get-tuple-element.106), channel_id=1, source_target_pairs={{0,1},{8,1023},{1,2},{9,8},{2,3},{10,9},{3,4},{11,10},{4,5},{12,11... | collective-permute-start | bytes 983048 | tf_op jit(solution)/shard_map/ppermute | solution.py:228
  18.8 18.2 %collective-permute-start.5 = (f32[5,128,128]{2,1,0:T(8,128)S(1)}, f32[5,128,128]{2,1,0:T(8,128)S(1)}, u32[]{:S(2)}, u32[]{:S(2)}) collective-permute-start(f32[5,128,128]{2,1,0:T(8,128)S(1)} %get-tuple-element.105), channel_id=1, source_target_pairs={{0,1},{8,1023},{1,2},{9,8},{2,3},{10,9},{3,4},{11,10},{4,5},{12,11... | collective-permute-start | bytes 983048 | tf_op jit(solution)/shard_map/ppermute | solution.py:228
  29.2 27.4 %collective-permute-start.6 = (f32[10,128,128]{2,1,0:T(8,128)S(1)}, f32[10,128,128]{2,1,0:T(8,128)S(1)}, u32[]{:S(2)}, u32[]{:S(2)}) collective-permute-start(f32[10,128,128]{2,1,0:T(8,128)S(1)} %bitcast.12), channel_id=1, source_target_pairs={{0,992},{1,993},{9,41},{2,994},{10,42},{3,995},{11,43},{4,996},{12... | collective-permute-start | bytes 1966088 | tf_op jit(solution)/shard_map/ppermute | solution.py:236
  31.2 13.7 %collective-permute-start.1 = (f32[5,128,128]{2,1,0:T(8,128)S(1)}, f32[5,128,128]{2,1,0:T(8,128)S(1)}, u32[]{:S(2)}, u32[]{:S(2)}) collective-permute-start(f32[5,128,128]{2,1,0:T(8,128)S(1)} %get-tuple-element.108), channel_id=1, source_target_pairs={{0,1},{8,31},{1,2},{9,8},{2,3},{10,9},{3,4},{11,10},{4,5},{12,11},... | collective-permute-start | bytes 983048 | tf_op jit(solution)/shard_map/ppermute | solution.py:228
  33.1 14.5 %collective-permute-start.3 = (f32[5,128,128]{2,1,0:T(8,128)S(1)}, f32[5,128,128]{2,1,0:T(8,128)S(1)}, u32[]{:S(2)}, u32[]{:S(2)}) collective-permute-start(f32[5,128,128]{2,1,0:T(8,128)S(1)} %get-tuple-element.107), channel_id=1, source_target_pairs={{0,1},{8,31},{1,2},{9,8},{2,3},{10,9},{3,4},{11,10},{4,5},{12,11},... | collective-permute-start | bytes 983048 | tf_op jit(solution)/shard_map/ppermute | solution.py:228
  35.1 14.5 %collective-permute-start.9 = (f32[5,128,128]{2,1,0:T(8,128)S(1)}, f32[5,128,128]{2,1,0:T(8,128)S(1)}, u32[]{:S(2)}, u32[]{:S(2)}) collective-permute-start(f32[5,128,128]{2,1,0:T(8,128)S(1)} %collective-permute-done.4.refs_2_), channel_id=1, source_target_pairs={{0,1},{8,1023},{1,2},{9,8},{2,3},{10,9},{3,4},{11,10},{4,5},{12,11... | collective-permute-start | bytes 983048 | tf_op jit(solution)/shard_map/ppermute | solution.py:228
  37.0 14.5 %collective-permute-start.10 = (f32[5,128,128]{2,1,0:T(8,128)S(1)}, f32[5,128,128]{2,1,0:T(8,128)S(1)}, u32[]{:S(2)}, u32[]{:S(2)}) collective-permute-start(f32[5,128,128]{2,1,0:T(8,128)S(1)} %collective-permute-done.5.refs_3_), channel_id=1, source_target_pairs={{0,1},{8,1023},{1,2},{9,8},{2,3},{10,9},{3,4},{11,10},{4,5},{12,11... | collective-permute-start | bytes 983048 | tf_op jit(solution)/shard_map/ppermute | solution.py:228
  44.9 14.9 %collective-permute-start.2 = (f32[5,128,128]{2,1,0:T(8,128)S(1)}, f32[5,128,128]{2,1,0:T(8,128)S(1)}, u32[]{:S(2)}, u32[]{:S(2)}) collective-permute-start(f32[5,128,128]{2,1,0:T(8,128)S(1)} %collective-permute-done.1.refs_0_), channel_id=1, source_target_pairs={{0,1},{8,31},{1,2},{9,8},{2,3},{10,9},{3,4},{11,10},{4,5},{12,11},... | collective-permute-start | bytes 983048 | tf_op jit(solution)/shard_map/ppermute | solution.py:228
  47.7 14.6 %collective-permute-start.8 = (f32[5,128,128]{2,1,0:T(8,128)S(1)}, f32[5,128,128]{2,1,0:T(8,128)S(1)}, u32[]{:S(2)}, u32[]{:S(2)}) collective-permute-start(f32[5,128,128]{2,1,0:T(8,128)S(1)} %collective-permute-done.3.refs_1_), channel_id=1, source_target_pairs={{0,1},{8,31},{1,2},{9,8},{2,3},{10,9},{3,4},{11,10},{4,5},{12,11},... | collective-permute-start | bytes 983048 | tf_op jit(solution)/shard_map/ppermute | solution.py:228
  49.6 14.6 %collective-permute-start.13 = (f32[5,128,128]{2,1,0:T(8,128)S(1)}, f32[5,128,128]{2,1,0:T(8,128)S(1)}, u32[]{:S(2)}, u32[]{:S(2)}) collective-permute-start(f32[5,128,128]{2,1,0:T(8,128)S(1)} %collective-permute-done.9.refs_2_), channel_id=1, source_target_pairs={{0,1},{8,1023},{1,2},{9,8},{2,3},{10,9},{3,4},{11,10},{4,5},{12,11... | collective-permute-start | bytes 983048 | tf_op jit(solution)/shard_map/ppermute | solution.py:228
  51.5 14.6 %collective-permute-start.14 = (f32[5,128,128]{2,1,0:T(8,128)S(1)}, f32[5,128,128]{2,1,0:T(8,128)S(1)}, u32[]{:S(2)}, u32[]{:S(2)}) collective-permute-start(f32[5,128,128]{2,1,0:T(8,128)S(1)} %collective-permute-done.10.refs_3_), channel_id=1, source_target_pairs={{0,1},{8,1023},{1,2},{9,8},{2,3},{10,9},{3,4},{11,10},{4,5},{12,11... | collective-permute-start | bytes 983048 | tf_op jit(solution)/shard_map/ppermute | solution.py:228
  59.7 14.1 %collective-permute-start.7 = (f32[5,128,128]{2,1,0:T(8,128)S(1)}, f32[5,128,128]{2,1,0:T(8,128)S(1)}, u32[]{:S(2)}, u32[]{:S(2)}) collective-permute-start(f32[5,128,128]{2,1,0:T(8,128)S(1)} %collective-permute-done.2.refs_0_), channel_id=1, source_target_pairs={{0,1},{8,31},{1,2},{9,8},{2,3},{10,9},{3,4},{11,10},{4,5},{12,11},... | collective-permute-start | bytes 983048 | tf_op jit(solution)/shard_map/ppermute | solution.py:228
  62.3 14.9 %collective-permute-start.12 = (f32[5,128,128]{2,1,0:T(8,128)S(1)}, f32[5,128,128]{2,1,0:T(8,128)S(1)}, u32[]{:S(2)}, u32[]{:S(2)}) collective-permute-start(f32[5,128,128]{2,1,0:T(8,128)S(1)} %collective-permute-done.8.refs_1_), channel_id=1, source_target_pairs={{0,1},{8,31},{1,2},{9,8},{2,3},{10,9},{3,4},{11,10},{4,5},{12,11},... | collective-permute-start | bytes 983048 | tf_op jit(solution)/shard_map/ppermute | solution.py:228
  64.2 14.9 %collective-permute-start.17 = (f32[5,128,128]{2,1,0:T(8,128)S(1)}, f32[5,128,128]{2,1,0:T(8,128)S(1)}, u32[]{:S(2)}, u32[]{:S(2)}) collective-permute-start(f32[5,128,128]{2,1,0:T(8,128)S(1)} %collective-permute-done.13.refs_2_), channel_id=1, source_target_pairs={{0,1},{8,1023},{1,2},{9,8},{2,3},{10,9},{3,4},{11,10},{4,5},{12,11... | collective-permute-start | bytes 983048 | tf_op jit(solution)/shard_map/ppermute | solution.py:228
  66.1 14.9 %collective-permute-start.18 = (f32[5,128,128]{2,1,0:T(8,128)S(1)}, f32[5,128,128]{2,1,0:T(8,128)S(1)}, u32[]{:S(2)}, u32[]{:S(2)}) collective-permute-start(f32[5,128,128]{2,1,0:T(8,128)S(1)} %collective-permute-done.14.refs_3_), channel_id=1, source_target_pairs={{0,1},{8,1023},{1,2},{9,8},{2,3},{10,9},{3,4},{11,10},{4,5},{12,11... | collective-permute-start | bytes 983048 | tf_op jit(solution)/shard_map/ppermute | solution.py:228
  73.9 16.0 %collective-permute-start.11 = (f32[5,128,128]{2,1,0:T(8,128)S(1)}, f32[5,128,128]{2,1,0:T(8,128)S(1)}, u32[]{:S(2)}, u32[]{:S(2)}) collective-permute-start(f32[5,128,128]{2,1,0:T(8,128)S(1)} %collective-permute-done.7.refs_0_), channel_id=1, source_target_pairs={{0,1},{8,31},{1,2},{9,8},{2,3},{10,9},{3,4},{11,10},{4,5},{12,11},... | collective-permute-start | bytes 983048 | tf_op jit(solution)/shard_map/ppermute | solution.py:228
  77.2 16.5 %collective-permute-start.16 = (f32[5,128,128]{2,1,0:T(8,128)S(1)}, f32[5,128,128]{2,1,0:T(8,128)S(1)}, u32[]{:S(2)}, u32[]{:S(2)}) collective-permute-start(f32[5,128,128]{2,1,0:T(8,128)S(1)} %collective-permute-done.12.refs_1_), channel_id=1, source_target_pairs={{0,1},{8,31},{1,2},{9,8},{2,3},{10,9},{3,4},{11,10},{4,5},{12,11},... | collective-permute-start | bytes 983048 | tf_op jit(solution)/shard_map/ppermute | solution.py:228
  79.1 16.5 %collective-permute-start.21 = (f32[5,128,128]{2,1,0:T(8,128)S(1)}, f32[5,128,128]{2,1,0:T(8,128)S(1)}, u32[]{:S(2)}, u32[]{:S(2)}) collective-permute-start(f32[5,128,128]{2,1,0:T(8,128)S(1)} %collective-permute-done.17.refs_2_), channel_id=1, source_target_pairs={{0,1},{8,1023},{1,2},{9,8},{2,3},{10,9},{3,4},{11,10},{4,5},{12,11... | collective-permute-start | bytes 983048 | tf_op jit(solution)/shard_map/ppermute | solution.py:228
  81.0 16.5 %collective-permute-start.22 = (f32[5,128,128]{2,1,0:T(8,128)S(1)}, f32[5,128,128]{2,1,0:T(8,128)S(1)}, u32[]{:S(2)}, u32[]{:S(2)}) collective-permute-start(f32[5,128,128]{2,1,0:T(8,128)S(1)} %collective-permute-done.18.refs_3_), channel_id=1, source_target_pairs={{0,1},{8,1023},{1,2},{9,8},{2,3},{10,9},{3,4},{11,10},{4,5},{12,11... | collective-permute-start | bytes 983048 | tf_op jit(solution)/shard_map/ppermute | solution.py:228
  89.8 15.2 %collective-permute-start.15 = (f32[5,128,128]{2,1,0:T(8,128)S(1)}, f32[5,128,128]{2,1,0:T(8,128)S(1)}, u32[]{:S(2)}, u32[]{:S(2)}) collective-permute-start(f32[5,128,128]{2,1,0:T(8,128)S(1)} %collective-permute-done.11.refs_0_), channel_id=1, source_target_pairs={{0,1},{8,31},{1,2},{9,8},{2,3},{10,9},{3,4},{11,10},{4,5},{12,11},... | collective-permute-start | bytes 983048 | tf_op jit(solution)/shard_map/ppermute | solution.py:228
  93.7 13.8 %collective-permute-start.20 = (f32[5,128,128]{2,1,0:T(8,128)S(1)}, f32[5,128,128]{2,1,0:T(8,128)S(1)}, u32[]{:S(2)}, u32[]{:S(2)}) collective-permute-start(f32[5,128,128]{2,1,0:T(8,128)S(1)} %collective-permute-done.16.refs_1_), channel_id=1, source_target_pairs={{0,1},{8,31},{1,2},{9,8},{2,3},{10,9},{3,4},{11,10},{4,5},{12,11},... | collective-permute-start | bytes 983048 | tf_op jit(solution)/shard_map/ppermute | solution.py:228
  95.7 13.8 %collective-permute-start.25 = (f32[5,128,128]{2,1,0:T(8,128)S(1)}, f32[5,128,128]{2,1,0:T(8,128)S(1)}, u32[]{:S(2)}, u32[]{:S(2)}) collective-permute-start(f32[5,128,128]{2,1,0:T(8,128)S(1)} %collective-permute-done.21.refs_2_), channel_id=1, source_target_pairs={{0,1},{8,1023},{1,2},{9,8},{2,3},{10,9},{3,4},{11,10},{4,5},{12,11... | collective-permute-start | bytes 983048 | tf_op jit(solution)/shard_map/ppermute | solution.py:228
  97.6 11.9 %collective-permute-start.26 = (f32[5,128,128]{2,1,0:T(8,128)S(1)}, f32[5,128,128]{2,1,0:T(8,128)S(1)}, u32[]{:S(2)}, u32[]{:S(2)}) collective-permute-start(f32[5,128,128]{2,1,0:T(8,128)S(1)} %collective-permute-done.22.refs_3_), channel_id=1, source_target_pairs={{0,1},{8,1023},{1,2},{9,8},{2,3},{10,9},{3,4},{11,10},{4,5},{12,11... | collective-permute-start | bytes 983048 | tf_op jit(solution)/shard_map/ppermute | solution.py:228
  105.0 9.5 %collective-permute-start.19 = (f32[5,128,128]{2,1,0:T(8,128)S(1)}, f32[5,128,128]{2,1,0:T(8,128)S(1)}, u32[]{:S(2)}, u32[]{:S(2)}) collective-permute-start(f32[5,128,128]{2,1,0:T(8,128)S(1)} %collective-permute-done.15.refs_0_), channel_id=1, source_target_pairs={{0,1},{8,31},{1,2},{9,8},{2,3},{10,9},{3,4},{11,10},{4,5},{12,11},... | collective-permute-start | bytes 983048 | tf_op jit(solution)/shard_map/ppermute | solution.py:228
  107.5 15.2 %collective-permute-start.24 = (f32[5,128,128]{2,1,0:T(8,128)S(1)}, f32[5,128,128]{2,1,0:T(8,128)S(1)}, u32[]{:S(2)}, u32[]{:S(2)}) collective-permute-start(f32[5,128,128]{2,1,0:T(8,128)S(1)} %collective-permute-done.20.refs_1_), channel_id=1, source_target_pairs={{0,1},{8,31},{1,2},{9,8},{2,3},{10,9},{3,4},{11,10},{4,5},{12,11},... | collective-permute-start | bytes 983048 | tf_op jit(solution)/shard_map/ppermute | solution.py:228
  109.6 36.7 %collective-permute-start.29 = (f32[10,128,128]{2,1,0:T(8,128)S(1)}, f32[10,128,128]{2,1,0:T(8,128)S(1)}, u32[]{:S(2)}, u32[]{:S(2)}) collective-permute-start(f32[10,128,128]{2,1,0:T(8,128)S(1)} %pad_maximum_fusion.1), channel_id=1, source_target_pairs={{0,1},{8,1023},{1,2},{9,8},{2,3},{10,9},{3,4},{11,10},{4,5},{12,11... | collective-permute-start | bytes 1966088 | tf_op jit(solution)/shard_map/ppermute | solution.py:228
  114.5 12.6 %collective-permute-start.23 = (f32[5,128,128]{2,1,0:T(8,128)S(1)}, f32[5,128,128]{2,1,0:T(8,128)S(1)}, u32[]{:S(2)}, u32[]{:S(2)}) collective-permute-start(f32[5,128,128]{2,1,0:T(8,128)S(1)} %collective-permute-done.19.refs_0_), channel_id=1, source_target_pairs={{0,1},{8,31},{1,2},{9,8},{2,3},{10,9},{3,4},{11,10},{4,5},{12,11},... | collective-permute-start | bytes 983048 | tf_op jit(solution)/shard_map/ppermute | solution.py:228
  122.8 8.1 %collective-permute-start.27 = (f32[5,128,128]{2,1,0:T(8,128)S(1)}, f32[5,128,128]{2,1,0:T(8,128)S(1)}, u32[]{:S(2)}, u32[]{:S(2)}) collective-permute-start(f32[5,128,128]{2,1,0:T(8,128)S(1)} %collective-permute-done.24.refs_1_), channel_id=1, source_target_pairs={{0,1},{8,31},{1,2},{9,8},{2,3},{10,9},{3,4},{11,10},{4,5},{12,11},... | collective-permute-start | bytes 983048 | tf_op jit(solution)/shard_map/ppermute | solution.py:228
  131.0 20.4 %collective-permute-start.28 = (f32[10,128,128]{2,1,0:T(8,128)S(1)}, f32[10,128,128]{2,1,0:T(8,128)S(1)}, u32[]{:S(2)}, u32[]{:S(2)}) collective-permute-start(f32[10,128,128]{2,1,0:T(8,128)S(1)} %pad_maximum_fusion), channel_id=1, source_target_pairs={{0,9},{9,0},{10,1},{7,1016},{16,25},{25,16},{26,17},{23,8},{32,41}... | collective-permute-start | bytes 1966088 | tf_op jit(solution)/shard_map/ppermute | solution.py:259
  136.4 17.3 %collective-permute-start.31 = (f32[10,128,128]{2,1,0:T(8,128)S(1)}, f32[10,128,128]{2,1,0:T(8,128)S(1)}, u32[]{:S(2)}, u32[]{:S(2)}) collective-permute-start(f32[10,128,128]{2,1,0:T(8,128)S(1)} %products.19), channel_id=1, source_target_pairs={{992,0},{993,1},{41,9},{994,2},{42,10},{995,3},{43,11},{996,4},{44... | collective-permute-start | bytes 1966088 | tf_op jit(solution)/shard_map/ppermute | solution.py:263
  149.4 4.3 %collective-permute-start.30 = (f32[10,128,128]{2,1,0:T(8,128)S(1)}, f32[10,128,128]{2,1,0:T(8,128)S(1)}, u32[]{:S(2)}, u32[]{:S(2)}) collective-permute-start(f32[10,128,128]{2,1,0:T(8,128)S(1)} %get-tuple-element.103), channel_id=1, source_target_pairs={{0,8},{1,9},{2,10},{3,11},{4,12},{5,13},{6,14},{7,15},{8,0},{9,1},... | collective-permute-start | bytes 1966088 | tf_op jit(solution)/shard_map/ppermute | solution.py:231

commit v5 on v4

--- a/solution.py
+++ b/solution.py
@@ -231,10 +231,9 @@
         return lax.ppermute(value, ring, flip_pairs(depth))
 
     own = blocks[0]
-    other, info = lax.optimization_barrier((flip(own), info))
+    other = flip(own)
     away = line_pairs(lines, depth)
-    ghost = lax.ppermute(own, every, away)
-    factors = [own, other, ghost]
+    factors = [own]
     sums = step_call(
         depth, 0, (0, 1), (0,), ((0, 0), (1, 0)), info, [[own], [other]], factors[:1]
     )
@@ -244,6 +243,8 @@
         for value, cuts in zip((own, other), CUTS)
     ]
     held = [hop(held, 1, which) for which in range(2)]
+    later, held[0][0] = lax.optimization_barrier((own, held[0][0]))
+    factors = [own, other, lax.ppermute(later, every, away)]
     for step in range(1, depth - 1):
         held[0][0], sums = lax.optimization_barrier((held[0][0], sums))
         going = [held[0], held[1] if step < depth - 2 else [jnp.concatenate(held[1])]]

time: 156 us -> 163 us (1.045)
  the two profiles are of different devices: /device:TPU:65 before, /device:TPU:95 now
where the time goes in v5:
time: 163 us; the launch traced here: 162 us
  starting transfers between devices  121 us (74%)
  Pallas kernels  23.4 us (14%)
  waiting for transfers between devices  12.5 us (8%)
  local copies, waits for them, and re-layouts  3.12 us (2%)
    ppermute x27, starting transfers between devices, hop(): return [lax.ppermute(piece, every, pairs) for piece in held[which]]  95.7 us
    pallas_call x10, Pallas kernels, step_call(): pl.pallas_call(functools.partial(step_kernel, depth, slots, step, rows, t...  23.4 us
    ppermute x1, starting transfers between devices, body(): far = [lax.ppermute(jnp.concatenate(held[0]), every, far)]  12.4 us
    ppermute x1, starting transfers between devices, body(): factors = [own, other, lax.ppermute(later, every, away)]  6.15 us
    ppermute x1, waiting for transfers between devices, body(): foreign = lax.ppermute(foreign, every, [(b, a) for a, b in away])  6.11 us
    ppermute x27, waiting for transfers between devices, hop(): return [lax.ppermute(piece, every, pairs) for piece in held[which]]  5.57 us
    ppermute x2, starting transfers between devices, flip(): return lax.ppermute(value, ring, flip_pairs(depth))  4.49 us
  transfers between devices with their start and end apart: 32, of which 5 were waited for; matrix products, arithmetic and copies ran while one was open for 2% of the time, Pallas kernels for 14%

profile of v5, /device:TPU:95, one launch (start us, length us, event | category | flops | bytes accessed | tf_op | source)
XLA Modules:
  0.0 161.5 jit_solution(15648524860771896284)
XLA Ops:
  0.0 2.6 %collective-permute-start.1 = (f32[10,128,128]{2,1,0:T(8,128)}, f32[10,128,128]{2,1,0:T(8,128)S(1)}, u32[]{:S(2)}, u32[]{:S(2)}) collective-permute-start(f32[10,128,128]{2,1,0:T(8,128)} %bitcast.11), channel_id=1, source_target_pairs={{0,8},{1,9},{2,10},{3,11},{4,12},{5,13},{6,14},{7,15},{8,0},{9,1},... | collective-permute-start | bytes 1966088 | tf_op jit(solution)/shard_map/ppermute | solution.py:231
  2.6 1.2 slice_bitcast_fusion
  3.8 1.9 %collective-permute-start = (f32[5,128,128]{2,1,0:T(8,128)S(1)}, f32[5,128,128]{2,1,0:T(8,128)S(1)}, u32[]{:S(2)}, u32[]{:S(2)}) collective-permute-start(f32[5,128,128]{2,1,0:T(8,128)S(1)} %get-tuple-element.108), channel_id=1, source_target_pairs={{0,1},{8,31},{1,2},{9,8},{2,3},{10,9},{3,4},{11,10},{4,5},{12,11},... | collective-permute-start | bytes 983048 | tf_op jit(solution)/shard_map/ppermute | solution.py:228
  5.7 17.3 %collective-permute-start.3 = (f32[5,128,128]{2,1,0:T(8,128)S(1)}, f32[5,128,128]{2,1,0:T(8,128)S(1)}, u32[]{:S(2)}, u32[]{:S(2)}) collective-permute-start(f32[5,128,128]{2,1,0:T(8,128)S(1)} %get-tuple-element.107), channel_id=1, source_target_pairs={{0,1},{8,31},{1,2},{9,8},{2,3},{10,9},{3,4},{11,10},{4,5},{12,11},... | collective-permute-start | bytes 983048 | tf_op jit(solution)/shard_map/ppermute | solution.py:228
  23.0 0.2 copy.26
  23.3 0.6 gather_fusion
  23.9 0.9 fusion.4
  24.8 2.2 %collective-permute-start.4 = (f32[5,128,128]{2,1,0:T(8,128)}, f32[5,128,128]{2,1,0:T(8,128)S(1)}, u32[]{:S(2)}, u32[]{:S(2)}) collective-permute-start(f32[5,128,128]{2,1,0:T(8,128)} %get-tuple-element.106), channel_id=1, source_target_pairs={{0,1},{8,1023},{1,2},{9,8},{2,3},{10,9},{3,4},{11,10},{4,5},{12,11... | collective-permute-start | bytes 983048 | tf_op jit(solution)/shard_map/ppermute | solution.py:228
  27.0 2.4 %collective-permute-start.5 = (f32[5,128,128]{2,1,0:T(8,128)}, f32[5,128,128]{2,1,0:T(8,128)S(1)}, u32[]{:S(2)}, u32[]{:S(2)}) collective-permute-start(f32[5,128,128]{2,1,0:T(8,128)} %get-tuple-element.105), channel_id=1, source_target_pairs={{0,1},{8,1023},{1,2},{9,8},{2,3},{10,9},{3,4},{11,10},{4,5},{12,11... | collective-permute-start | bytes 983048 | tf_op jit(solution)/shard_map/ppermute | solution.py:228
  29.5 0.1 subtract_add_fusion
  29.6 0.1 add.101
  29.7 6.1 %collective-permute-start.6 = (f32[10,128,128]{2,1,0:T(8,128)S(1)}, f32[10,128,128]{2,1,0:T(8,128)S(1)}, u32[]{:S(2)}, u32[]{:S(2)}) collective-permute-start(f32[10,128,128]{2,1,0:T(8,128)S(1)} %bitcast.12), channel_id=1, source_target_pairs={{0,992},{1,993},{9,41},{2,994},{10,42},{3,995},{11,43},{4,996},{12... | collective-permute-start | bytes 1966088 | tf_op jit(solution)/shard_map/ppermute | solution.py:247
  35.9 0.8 collective-permute-done.5.refs_3_
  36.6 2.2 %collective-permute-start.10 = (f32[5,128,128]{2,1,0:T(8,128)S(1)}, f32[5,128,128]{2,1,0:T(8,128)S(1)}, u32[]{:S(2)}, u32[]{:S(2)}) collective-permute-start(f32[5,128,128]{2,1,0:T(8,128)S(1)} %collective-permute-done.5.refs_3_), channel_id=1, source_target_pairs={{0,1},{8,1023},{1,2},{9,8},{2,3},{10,9},{3,4},{11,10},{4,5},{12,11... | collective-permute-start | bytes 983048 | tf_op jit(solution)/shard_map/ppermute | solution.py:228
  38.8 4.6 %collective-permute-start.9 = (f32[5,128,128]{2,1,0:T(8,128)S(1)}, f32[5,128,128]{2,1,0:T(8,128)S(1)}, u32[]{:S(2)}, u32[]{:S(2)}) collective-permute-start(f32[5,128,128]{2,1,0:T(8,128)S(1)} %collective-permute-done.4.refs_2_), channel_id=1, source_target_pairs={{0,1},{8,1023},{1,2},{9,8},{2,3},{10,9},{3,4},{11,10},{4,5},{12,11... | collective-permute-start | bytes 983048 | tf_op jit(solution)/shard_map/ppermute | solution.py:228
  43.5 0.1 pad_add_fusion.info
  43.5 1.7 %products.10.refs_7_ = f32[10,128,128]{2,1,0:T(8,128)S(1)} custom-call(s32[962]{0:T(1024)S(1)} %pad_add_fusion.info, f32[10,128,128]{2,1,0:T(8,128)S(1)} %bitcast.13, f32[10,128,128]{2,1,0:T(8,128)S(1)} %collective-permute-done.1.refs_1_.refs_5_.refs_4_, f32[10,128,128]{2,1,0:T(8,128)S(1)} %bitcast.14), custom_call_target="tpu_custom_call" | custom-call | flops 200000000 | bytes 8000000 | tf_op jit(solution)/shard_map/products/pallas_call | solution.py:188
  45.2 1.9 %collective-permute-start.2 = (f32[5,128,128]{2,1,0:T(8,128)S(1)}, f32[5,128,128]{2,1,0:T(8,128)S(1)}, u32[]{:S(2)}, u32[]{:S(2)}) collective-permute-start(f32[5,128,128]{2,1,0:T(8,128)S(1)} %collective-permute-done.refs_0_), channel_id=1, source_target_pairs={{0,1},{8,31},{1,2},{9,8},{2,3},{10,9},{3,4},{11,10},{4,5},{12,11},... | collective-permute-start | bytes 983048 | tf_op jit(solution)/shard_map/ppermute | solution.py:228
  47.2 4.6 %collective-permute-start.8 = (f32[5,128,128]{2,1,0:T(8,128)S(1)}, f32[5,128,128]{2,1,0:T(8,128)S(1)}, u32[]{:S(2)}, u32[]{:S(2)}) collective-permute-start(f32[5,128,128]{2,1,0:T(8,128)S(1)} %collective-permute-done.3.refs_1_), channel_id=1, source_target_pairs={{0,1},{8,31},{1,2},{9,8},{2,3},{10,9},{3,4},{11,10},{4,5},{12,11},... | collective-permute-start | bytes 983048 | tf_op jit(solution)/shard_map/ppermute | solution.py:228
  51.8 0.0 collective-permute-done.9.refs_2_
  51.8 1.9 %collective-permute-start.13 = (f32[5,128,128]{2,1,0:T(8,128)S(1)}, f32[5,128,128]{2,1,0:T(8,128)S(1)}, u32[]{:S(2)}, u32[]{:S(2)}) collective-permute-start(f32[5,128,128]{2,1,0:T(8,128)S(1)} %collective-permute-done.9.refs_2_), channel_id=1, source_target_pairs={{0,1},{8,1023},{1,2},{9,8},{2,3},{10,9},{3,4},{11,10},{4,5},{12,11... | collective-permute-start | bytes 983048 | tf_op jit(solution)/shard_map/ppermute | solution.py:228
  53.8 3.1 %collective-permute-start.14 = (f32[5,128,128]{2,1,0:T(8,128)S(1)}, f32[5,128,128]{2,1,0:T(8,128)S(1)}, u32[]{:S(2)}, u32[]{:S(2)}) collective-permute-start(f32[5,128,128]{2,1,0:T(8,128)S(1)} %collective-permute-done.10.refs_3_), channel_id=1, source_target_pairs={{0,1},{8,1023},{1,2},{9,8},{2,3},{10,9},{3,4},{11,10},{4,5},{12,11... | collective-permute-start | bytes 983048 | tf_op jit(solution)/shard_map/ppermute | solution.py:228
  57.0 0.0 collective-permute-done.6.refs_6_.refs_2_
  57.0 2.1 %products.11 = (f32[10,128,128]{2,1,0:T(8,128)S(1)}, f32[10,128,128]{2,1,0:T(8,128)S(1)}, f32[10,128,128]{2,1,0:T(8,128)S(1)}) custom-call(s32[962]{0:T(1024)S(1)} %pad_add_fusion.info, f32[5,128,128]{2,1,0:T(8,128)S(1)} %collective-permute-done.refs_0_, ...), custom_call_target="tpu_custom_call", output_to_operand_aliasing={{0}: (8, {}), {1}: (9, {}), {2}: (10, {})} | custom-call | flops 200000000 | bytes 8000000 | tf_op jit(solution)/shard_map/products/pallas_call | solution.py:188
  59.1 0.0 collective-permute-done.2.refs_0_
  59.1 3.1 %collective-permute-start.7 = (f32[5,128,128]{2,1,0:T(8,128)S(1)}, f32[5,128,128]{2,1,0:T(8,128)S(1)}, u32[]{:S(2)}, u32[]{:S(2)}) collective-permute-start(f32[5,128,128]{2,1,0:T(8,128)S(1)} %collective-permute-done.2.refs_0_), channel_id=1, source_target_pairs={{0,1},{8,31},{1,2},{9,8},{2,3},{10,9},{3,4},{11,10},{4,5},{12,11},... | collective-permute-start | bytes 983048 | tf_op jit(solution)/shard_map/ppermute | solution.py:228
  62.2 0.0 collective-permute-done.8.refs_1_
  62.3 6.8 %collective-permute-start.12 = (f32[5,128,128]{2,1,0:T(8,128)S(1)}, f32[5,128,128]{2,1,0:T(8,128)S(1)}, u32[]{:S(2)}, u32[]{:S(2)}) collective-permute-start(f32[5,128,128]{2,1,0:T(8,128)S(1)} %collective-permute-done.8.refs_1_), channel_id=1, source_target_pairs={{0,1},{8,31},{1,2},{9,8},{2,3},{10,9},{3,4},{11,10},{4,5},{12,11},... | collective-permute-start | bytes 983048 | tf_op jit(solution)/shard_map/ppermute | solution.py:228
  69.0 0.0 collective-permute-done.13.refs_2_
  69.0 1.9 %collective-permute-start.17 = (f32[5,128,128]{2,1,0:T(8,128)S(1)}, f32[5,128,128]{2,1,0:T(8,128)S(1)}, u32[]{:S(2)}, u32[]{:S(2)}) collective-permute-start(f32[5,128,128]{2,1,0:T(8,128)S(1)} %collective-permute-done.13.refs_2_), channel_id=1, source_target_pairs={{0,1},{8,1023},{1,2},{9,8},{2,3},{10,9},{3,4},{11,10},{4,5},{12,11... | collective-permute-start | bytes 983048 | tf_op jit(solution)/shard_map/ppermute | solution.py:228
  71.0 1.9 %collective-permute-start.18 = (f32[5,128,128]{2,1,0:T(8,128)S(1)}, f32[5,128,128]{2,1,0:T(8,128)S(1)}, u32[]{:S(2)}, u32[]{:S(2)}) collective-permute-start(f32[5,128,128]{2,1,0:T(8,128)S(1)} %collective-permute-done.14.refs_3_), channel_id=1, source_target_pairs={{0,1},{8,1023},{1,2},{9,8},{2,3},{10,9},{3,4},{11,10},{4,5},{12,11... | collective-permute-start | bytes 983048 | tf_op jit(solution)/shard_map/ppermute | solution.py:228
  72.9 2.1 %products.12 = (f32[10,128,128]{2,1,0:T(8,128)S(1)}, f32[10,128,128]{2,1,0:T(8,128)S(1)}, f32[10,128,128]{2,1,0:T(8,128)S(1)}) custom-call(s32[962]{0:T(1024)S(1)} %pad_add_fusion.info, f32[5,128,128]{2,1,0:T(8,128)S(1)} %collective-permute-done.2.refs_0_, ...), custom_call_target="tpu_custom_call", output_to_operand_aliasing={{0}: (8, {}), {1}: (9, {}), {2}: (10, {})} | custom-call | flops 200000000 | bytes 8000000 | tf_op jit(solution)/shard_map/products/pallas_call | solution.py:188
  75.0 0.0 collective-permute-done.7.refs_0_
  75.1 2.9 %collective-permute-start.11 = (f32[5,128,128]{2,1,0:T(8,128)S(1)}, f32[5,128,128]{2,1,0:T(8,128)S(1)}, u32[]{:S(2)}, u32[]{:S(2)}) collective-permute-start(f32[5,128,128]{2,1,0:T(8,128)S(1)} %collective-permute-done.7.refs_0_), channel_id=1, source_target_pairs={{0,1},{8,31},{1,2},{9,8},{2,3},{10,9},{3,4},{11,10},{4,5},{12,11},... | collective-permute-start | bytes 983048 | tf_op jit(solution)/shard_map/ppermute | solution.py:228
  78.0 0.0 collective-permute-done.12.refs_1_
  78.0 5.8 %collective-permute-start.16 = (f32[5,128,128]{2,1,0:T(8,128)S(1)}, f32[5,128,128]{2,1,0:T(8,128)S(1)}, u32[]{:S(2)}, u32[]{:S(2)}) collective-permute-start(f32[5,128,128]{2,1,0:T(8,128)S(1)} %collective-permute-done.12.refs_1_), channel_id=1, source_target_pairs={{0,1},{8,31},{1,2},{9,8},{2,3},{10,9},{3,4},{11,10},{4,5},{12,11},... | collective-permute-start | bytes 983048 | tf_op jit(solution)/shard_map/ppermute | solution.py:228
  83.7 0.0 collective-permute-done.17.refs_2_
  83.7 1.9 %collective-permute-start.21 = (f32[5,128,128]{2,1,0:T(8,128)S(1)}, f32[5,128,128]{2,1,0:T(8,128)S(1)}, u32[]{:S(2)}, u32[]{:S(2)}) collective-permute-start(f32[5,128,128]{2,1,0:T(8,128)S(1)} %collective-permute-done.17.refs_2_), channel_id=1, source_target_pairs={{0,1},{8,1023},{1,2},{9,8},{2,3},{10,9},{3,4},{11,10},{4,5},{12,11... | collective-permute-start | bytes 983048 | tf_op jit(solution)/shard_map/ppermute | solution.py:228
  85.7 0.0 collective-permute-done.18.refs_3_
  85.7 1.9 %collective-permute-start.22 = (f32[5,128,128]{2,1,0:T(8,128)S(1)}, f32[5,128,128]{2,1,0:T(8,128)S(1)}, u32[]{:S(2)}, u32[]{:S(2)}) collective-permute-start(f32[5,128,128]{2,1,0:T(8,128)S(1)} %collective-permute-done.18.refs_3_), channel_id=1, source_target_pairs={{0,1},{8,1023},{1,2},{9,8},{2,3},{10,9},{3,4},{11,10},{4,5},{12,11... | collective-permute-start | bytes 983048 | tf_op jit(solution)/shard_map/ppermute | solution.py:228
  87.6 3.3 %products.13 = (f32[10,128,128]{2,1,0:T(8,128)S(1)}, f32[10,128,128]{2,1,0:T(8,128)S(1)}, f32[10,128,128]{2,1,0:T(8,128)S(1)}) custom-call(s32[962]{0:T(1024)S(1)} %pad_add_fusion.info, f32[5,128,128]{2,1,0:T(8,128)S(1)} %collective-permute-done.7.refs_0_, ...), custom_call_target="tpu_custom_call", output_to_operand_aliasing={{0}: (8, {}), {1}: (9, {}), {2}: (10, {})} | custom-call | flops 200000000 | bytes 8000000 | tf_op jit(solution)/shard_map/products/pallas_call | solution.py:188
  90.9 1.9 %collective-permute-start.15 = (f32[5,128,128]{2,1,0:T(8,128)S(1)}, f32[5,128,128]{2,1,0:T(8,128)S(1)}, u32[]{:S(2)}, u32[]{:S(2)}) collective-permute-start(f32[5,128,128]{2,1,0:T(8,128)S(1)} %collective-permute-done.11.refs_0_), channel_id=1, source_target_pairs={{0,1},{8,31},{1,2},{9,8},{2,3},{10,9},{3,4},{11,10},{4,5},{12,11},... | collective-permute-start | bytes 983048 | tf_op jit(solution)/shard_map/ppermute | solution.py:228
  92.9 3.8 %collective-permute-start.20 = (f32[5,128,128]{2,1,0:T(8,128)S(1)}, f32[5,128,128]{2,1,0:T(8,128)S(1)}, u32[]{:S(2)}, u32[]{:S(2)}) collective-permute-start(f32[5,128,128]{2,1,0:T(8,128)S(1)} %collective-permute-done.16.refs_1_), channel_id=1, source_target_pairs={{0,1},{8,31},{1,2},{9,8},{2,3},{10,9},{3,4},{11,10},{4,5},{12,11},... | collective-permute-start | bytes 983048 | tf_op jit(solution)/shard_map/ppermute | solution.py:228
  96.7 1.9 %collective-permute-start.25 = (f32[5,128,128]{2,1,0:T(8,128)S(1)}, f32[5,128,128]{2,1,0:T(8,128)S(1)}, u32[]{:S(2)}, u32[]{:S(2)}) collective-permute-start(f32[5,128,128]{2,1,0:T(8,128)S(1)} %collective-permute-done.21.refs_2_), channel_id=1, source_target_pairs={{0,1},{8,1023},{1,2},{9,8},{2,3},{10,9},{3,4},{11,10},{4,5},{12,11... | collective-permute-start | bytes 983048 | tf_op jit(solution)/shard_map/ppermute | solution.py:228
  98.6 2.0 %collective-permute-start.26 = (f32[5,128,128]{2,1,0:T(8,128)S(1)}, f32[5,128,128]{2,1,0:T(8,128)S(1)}, u32[]{:S(2)}, u32[]{:S(2)}) collective-permute-start(f32[5,128,128]{2,1,0:T(8,128)S(1)} %collective-permute-done.22.refs_3_), channel_id=1, source_target_pairs={{0,1},{8,1023},{1,2},{9,8},{2,3},{10,9},{3,4},{11,10},{4,5},{12,11... | collective-permute-start | bytes 983048 | tf_op jit(solution)/shard_map/ppermute | solution.py:228
  100.7 3.1 %products.14 = (f32[10,128,128]{2,1,0:T(8,128)S(1)}, f32[10,128,128]{2,1,0:T(8,128)S(1)}, f32[10,128,128]{2,1,0:T(8,128)S(1)}) custom-call(s32[962]{0:T(1024)S(1)} %pad_add_fusion.info, f32[5,128,128]{2,1,0:T(8,128)S(1)} %collective-permute-done.11.refs_0_, ...), custom_call_target="tpu_custom_call", output_to_operand_aliasing={{0}: (8, {}), {1}: (9, {}), {2}: (10, {})} | custom-call | flops 200000000 | bytes 8000000 | tf_op jit(solution)/shard_map/products/pallas_call | solution.py:188
  103.8 3.5 %collective-permute-start.19 = (f32[5,128,128]{2,1,0:T(8,128)S(1)}, f32[5,128,128]{2,1,0:T(8,128)S(1)}, u32[]{:S(2)}, u32[]{:S(2)}) collective-permute-start(f32[5,128,128]{2,1,0:T(8,128)S(1)} %collective-permute-done.15.refs_0_), channel_id=1, source_target_pairs={{0,1},{8,31},{1,2},{9,8},{2,3},{10,9},{3,4},{11,10},{4,5},{12,11},... | collective-permute-start | bytes 983048 | tf_op jit(solution)/shard_map/ppermute | solution.py:228
  107.3 5.7 %collective-permute-start.24 = (f32[5,128,128]{2,1,0:T(8,128)S(1)}, f32[5,128,128]{2,1,0:T(8,128)S(1)}, u32[]{:S(2)}, u32[]{:S(2)}) collective-permute-start(f32[5,128,128]{2,1,0:T(8,128)S(1)} %collective-permute-done.20.refs_1_), channel_id=1, source_target_pairs={{0,1},{8,31},{1,2},{9,8},{2,3},{10,9},{3,4},{11,10},{4,5},{12,11},... | collective-permute-start | bytes 983048 | tf_op jit(solution)/shard_map/ppermute | solution.py:228
  113.1 1.9 %collective-permute-start.29 = (f32[10,128,128]{2,1,0:T(8,128)S(1)}, f32[10,128,128]{2,1,0:T(8,128)S(1)}, u32[]{:S(2)}, u32[]{:S(2)}) collective-permute-start(f32[10,128,128]{2,1,0:T(8,128)S(1)} %pad_maximum_fusion.1), channel_id=1, source_target_pairs={{0,1},{8,1023},{1,2},{9,8},{2,3},{10,9},{3,4},{11,10},{4,5},{12,11... | collective-permute-start | bytes 1966088 | tf_op jit(solution)/shard_map/ppermute | solution.py:228
  115.0 3.3 %products.15 = (f32[10,128,128]{2,1,0:T(8,128)S(1)}, f32[10,128,128]{2,1,0:T(8,128)S(1)}, f32[10,128,128]{2,1,0:T(8,128)S(1)}) custom-call(s32[962]{0:T(1024)S(1)} %pad_add_fusion.info, f32[5,128,128]{2,1,0:T(8,128)S(1)} %collective-permute-done.15.refs_0_, ...), custom_call_target="tpu_custom_call", output_to_operand_aliasing={{0}: (8, {}), {1}: (9, {}), {2}: (10, {})} | custom-call | flops 200000000 | bytes 8000000 | tf_op jit(solution)/shard_map/products/pallas_call | solution.py:188
  118.3 2.1 %collective-permute-start.23 = (f32[5,128,128]{2,1,0:T(8,128)S(1)}, f32[5,128,128]{2,1,0:T(8,128)S(1)}, u32[]{:S(2)}, u32[]{:S(2)}) collective-permute-start(f32[5,128,128]{2,1,0:T(8,128)S(1)} %collective-permute-done.19.refs_0_), channel_id=1, source_target_pairs={{0,1},{8,31},{1,2},{9,8},{2,3},{10,9},{3,4},{11,10},{4,5},{12,11},... | collective-permute-start | bytes 983048 | tf_op jit(solution)/shard_map/ppermute | solution.py:228
  120.4 4.4 %collective-permute-start.27 = (f32[5,128,128]{2,1,0:T(8,128)S(1)}, f32[5,128,128]{2,1,0:T(8,128)S(1)}, u32[]{:S(2)}, u32[]{:S(2)}) collective-permute-start(f32[5,128,128]{2,1,0:T(8,128)S(1)} %collective-permute-done.24.refs_1_), channel_id=1, source_target_pairs={{0,1},{8,31},{1,2},{9,8},{2,3},{10,9},{3,4},{11,10},{4,5},{12,11},... | collective-permute-start | bytes 983048 | tf_op jit(solution)/shard_map/ppermute | solution.py:228
  124.8 2.1 %products.16 = (f32[10,128,128]{2,1,0:T(8,128)S(1)}, f32[10,128,128]{2,1,0:T(8,128)S(1)}, f32[10,128,128]{2,1,0:T(8,128)S(1)}) custom-call(s32[962]{0:T(1024)S(1)} %pad_add_fusion.info, f32[5,128,128]{2,1,0:T(8,128)S(1)} %collective-permute-done.19.refs_0_, ...), custom_call_target="tpu_custom_call", output_to_operand_aliasing={{0}: (8, {}), {1}: (9, {}), {2}: (10, {})} | custom-call | flops 200000000 | bytes 8000000 | tf_op jit(solution)/shard_map/products/pallas_call | solution.py:188
  127.0 1.2 collective-permute-done.23.refs_0_
  128.2 3.5 %collective-permute-done.27.refs_1_ = f32[5,128,128]{2,1,0:T(8,128)S(1)} collective-permute-done((f32[5,128,128]{2,1,0:T(8,128)S(1)}, f32[5,128,128]{2,1,0:T(8,128)S(1)}, u32[]{:S(2)}, u32[]{:S(2)}) %collective-permute-start.27) | collective-permute-done | bytes 327712 | tf_op jit(solution)/shard_map/ppermute | solution.py:228
  131.8 12.4 %collective-permute-start.28 = (f32[10,128,128]{2,1,0:T(8,128)S(1)}, f32[10,128,128]{2,1,0:T(8,128)S(1)}, u32[]{:S(2)}, u32[]{:S(2)}) collective-permute-start(f32[10,128,128]{2,1,0:T(8,128)S(1)} %pad_maximum_fusion), channel_id=1, source_target_pairs={{0,9},{9,0},{10,1},{7,1016},{16,25},{25,16},{26,17},{23,8},{32,41}... | collective-permute-start | bytes 1966088 | tf_op jit(solution)/shard_map/ppermute | solution.py:260
  144.1 1.8 %products.19 = f32[10,128,128]{2,1,0:T(8,128)S(1)} custom-call(s32[962]{0:T(1024)S(1)} %pad_add_fusion.info, f32[5,128,128]{2,1,0:T(8,128)S(1)} %collective-permute-done.23.refs_0_, f32[5,128,128]{2,1,0:T(8,128)S(1)} %collective-permute-done.27.refs_1_, f32[10,128,128]{2,1,0:T(8,128)S(1)} %collective-permute-done.6.refs_6_.refs_2_, ...), custom_call_target="tpu_custom_call", output_to_operand_aliasing={{}: (4, {})} | custom-call | flops 200000000 | bytes 8000000 | tf_op jit(solution)/shard_map/products/pallas_call | solution.py:188
  145.9 1.9 %collective-permute-start.31 = (f32[10,128,128]{2,1,0:T(8,128)S(1)}, f32[10,128,128]{2,1,0:T(8,128)S(1)}, u32[]{:S(2)}, u32[]{:S(2)}) collective-permute-start(f32[10,128,128]{2,1,0:T(8,128)S(1)} %products.19), channel_id=1, source_target_pairs={{992,0},{993,1},{41,9},{994,2},{42,10},{995,3},{43,11},{996,4},{44... | collective-permute-start | bytes 1966088 | tf_op jit(solution)/shard_map/ppermute | solution.py:264
  147.9 2.0 %products.17 = (f32[10,128,128]{2,1,0:T(8,128)S(1)}, f32[10,128,128]{2,1,0:T(8,128)S(1)}) custom-call(s32[962]{0:T(1024)S(1)} %pad_add_fusion.info, f32[5,128,128]{2,1,0:T(8,128)S(1)} %collective-permute-done.23.refs_0_, f32[5,128,128]{2,1,0:T(8,128)S(1)} %collective-permute-done.27.refs_1_, ...), custom_call_target="tpu_custom_call", output_to_operand_aliasing={{0}: (6, {}), {1}: (7, {})} | custom-call | flops 200000000 | bytes 8000000 | tf_op jit(solution)/shard_map/products/pallas_call | solution.py:188
  149.9 1.9 %collective-permute-start.30 = (f32[10,128,128]{2,1,0:T(8,128)S(1)}, f32[10,128,128]{2,1,0:T(8,128)S(1)}, u32[]{:S(2)}, u32[]{:S(2)}) collective-permute-start(f32[10,128,128]{2,1,0:T(8,128)S(1)} %get-tuple-element.103), channel_id=1, source_target_pairs={{0,8},{1,9},{2,10},{3,11},{4,12},{5,13},{6,14},{7,15},{8,0},{9,1},... | collective-permute-start | bytes 1966088 | tf_op jit(solution)/shard_map/ppermute | solution.py:231
  151.9 0.8 collective-permute-done.28.refs_0_
  152.7 1.8 %products.18 = f32[10,128,128]{2,1,0:T(8,128)S(1)} custom-call(s32[962]{0:T(1024)S(1)} %pad_add_fusion.info, f32[10,128,128]{2,1,0:T(8,128)S(1)} %collective-permute-done.28.refs_0_, f32[10,128,128]{2,1,0:T(8,128)S(1)} %bitcast.22, f32[10,128,128]{2,1,0:T(8,128)S(1)} %get-tuple-element.102.refs_2_), custom_call_target="tpu_custom_call", output_to_operand_aliasing={{}: (3, {})} | custom-call | flops 200000000 | bytes 8000000 | tf_op jit(solution)/shard_map/products/pallas_call | solution.py:188
  154.5 6.1 %collective-permute-done.31 = f32[10,128,128]{2,1,0:T(8,128)S(1)} collective-permute-done((f32[10,128,128]{2,1,0:T(8,128)S(1)}, f32[10,128,128]{2,1,0:T(8,128)S(1)}, u32[]{:S(2)}, u32[]{:S(2)}) %collective-permute-start.31) | collective-permute-done | bytes 655392 | tf_op jit(solution)/shard_map/ppermute | solution.py:264
  160.6 0.9 add_bitcast_fusion
  (30 shorter events, 0.3 us)
Async XLA Ops:
  0.0 23.9 %collective-permute-start.1 = (f32[10,128,128]{2,1,0:T(8,128)}, f32[10,128,128]{2,1,0:T(8,128)S(1)}, u32[]{:S(2)}, u32[]{:S(2)}) collective-permute-start(f32[10,128,128]{2,1,0:T(8,128)} %bitcast.11), channel_id=1, source_target_pairs={{0,8},{1,9},{2,10},{3,11},{4,12},{5,13},{6,14},{7,15},{8,0},{9,1},... | collective-permute-start | bytes 1966088 | tf_op jit(solution)/shard_map/ppermute | solution.py:231
  2.6 20.4 %copy-start.1 = (s32[1024,10]{0,1:T(8,128)S(1)}, s32[1024,10]{0,1:T(8,128)}, u32[]{:S(2)}) copy-start(s32[1024,10]{0,1:T(8,128)} %param.3) | copy-start | bytes 122884
  3.8 26.0 %collective-permute-start = (f32[5,128,128]{2,1,0:T(8,128)S(1)}, f32[5,128,128]{2,1,0:T(8,128)S(1)}, u32[]{:S(2)}, u32[]{:S(2)}) collective-permute-start(f32[5,128,128]{2,1,0:T(8,128)S(1)} %get-tuple-element.108), channel_id=1, source_target_pairs={{0,1},{8,31},{1,2},{9,8},{2,3},{10,9},{3,4},{11,10},{4,5},{12,11},... | collective-permute-start | bytes 983048 | tf_op jit(solution)/shard_map/ppermute | solution.py:228
  5.7 41.5 %collective-permute-start.3 = (f32[5,128,128]{2,1,0:T(8,128)S(1)}, f32[5,128,128]{2,1,0:T(8,128)S(1)}, u32[]{:S(2)}, u32[]{:S(2)}) collective-permute-start(f32[5,128,128]{2,1,0:T(8,128)S(1)} %get-tuple-element.107), channel_id=1, source_target_pairs={{0,1},{8,31},{1,2},{9,8},{2,3},{10,9},{3,4},{11,10},{4,5},{12,11},... | collective-permute-start | bytes 983048 | tf_op jit(solution)/shard_map/ppermute | solution.py:228
  23.9 5.8 %copy-start = (f32[1,10,128,128]{3,2,1,0:T(8,128)S(1)}, f32[1,10,128,128]{3,2,1,0:T(8,128)}, u32[]{:S(2)}) copy-start(f32[1,10,128,128]{3,2,1,0:T(8,128)} %param.2) | copy-start | bytes 1966084
  24.8 14.0 %collective-permute-start.4 = (f32[5,128,128]{2,1,0:T(8,128)}, f32[5,128,128]{2,1,0:T(8,128)S(1)}, u32[]{:S(2)}, u32[]{:S(2)}) collective-permute-start(f32[5,128,128]{2,1,0:T(8,128)} %get-tuple-element.106), channel_id=1, source_target_pairs={{0,1},{8,1023},{1,2},{9,8},{2,3},{10,9},{3,4},{11,10},{4,5},{12,11... | collective-permute-start | bytes 983048 | tf_op jit(solution)/shard_map/ppermute | solution.py:228
  27.0 9.6 %collective-permute-start.5 = (f32[5,128,128]{2,1,0:T(8,128)}, f32[5,128,128]{2,1,0:T(8,128)S(1)}, u32[]{:S(2)}, u32[]{:S(2)}) collective-permute-start(f32[5,128,128]{2,1,0:T(8,128)} %get-tuple-element.105), channel_id=1, source_target_pairs={{0,1},{8,1023},{1,2},{9,8},{2,3},{10,9},{3,4},{11,10},{4,5},{12,11... | collective-permute-start | bytes 983048 | tf_op jit(solution)/shard_map/ppermute | solution.py:228
  29.7 27.3 %collective-permute-start.6 = (f32[10,128,128]{2,1,0:T(8,128)S(1)}, f32[10,128,128]{2,1,0:T(8,128)S(1)}, u32[]{:S(2)}, u32[]{:S(2)}) collective-permute-start(f32[10,128,128]{2,1,0:T(8,128)S(1)} %bitcast.12), channel_id=1, source_target_pairs={{0,992},{1,993},{9,41},{2,994},{10,42},{3,995},{11,43},{4,996},{12... | collective-permute-start | bytes 1966088 | tf_op jit(solution)/shard_map/ppermute | solution.py:247
  36.6 17.1 %collective-permute-start.10 = (f32[5,128,128]{2,1,0:T(8,128)S(1)}, f32[5,128,128]{2,1,0:T(8,128)S(1)}, u32[]{:S(2)}, u32[]{:S(2)}) collective-permute-start(f32[5,128,128]{2,1,0:T(8,128)S(1)} %collective-permute-done.5.refs_3_), channel_id=1, source_target_pairs={{0,1},{8,1023},{1,2},{9,8},{2,3},{10,9},{3,4},{11,10},{4,5},{12,11... | collective-permute-start | bytes 983048 | tf_op jit(solution)/shard_map/ppermute | solution.py:228
  38.8 13.0 %collective-permute-start.9 = (f32[5,128,128]{2,1,0:T(8,128)S(1)}, f32[5,128,128]{2,1,0:T(8,128)S(1)}, u32[]{:S(2)}, u32[]{:S(2)}) collective-permute-start(f32[5,128,128]{2,1,0:T(8,128)S(1)} %collective-permute-done.4.refs_2_), channel_id=1, source_target_pairs={{0,1},{8,1023},{1,2},{9,8},{2,3},{10,9},{3,4},{11,10},{4,5},{12,11... | collective-permute-start | bytes 983048 | tf_op jit(solution)/shard_map/ppermute | solution.py:228
  45.2 13.9 %collective-permute-start.2 = (f32[5,128,128]{2,1,0:T(8,128)S(1)}, f32[5,128,128]{2,1,0:T(8,128)S(1)}, u32[]{:S(2)}, u32[]{:S(2)}) collective-permute-start(f32[5,128,128]{2,1,0:T(8,128)S(1)} %collective-permute-done.refs_0_), channel_id=1, source_target_pairs={{0,1},{8,31},{1,2},{9,8},{2,3},{10,9},{3,4},{11,10},{4,5},{12,11},... | collective-permute-start | bytes 983048 | tf_op jit(solution)/shard_map/ppermute | solution.py:228
  47.2 15.1 %collective-permute-start.8 = (f32[5,128,128]{2,1,0:T(8,128)S(1)}, f32[5,128,128]{2,1,0:T(8,128)S(1)}, u32[]{:S(2)}, u32[]{:S(2)}) collective-permute-start(f32[5,128,128]{2,1,0:T(8,128)S(1)} %collective-permute-done.3.refs_1_), channel_id=1, source_target_pairs={{0,1},{8,31},{1,2},{9,8},{2,3},{10,9},{3,4},{11,10},{4,5},{12,11},... | collective-permute-start | bytes 983048 | tf_op jit(solution)/shard_map/ppermute | solution.py:228
  51.8 17.2 %collective-permute-start.13 = (f32[5,128,128]{2,1,0:T(8,128)S(1)}, f32[5,128,128]{2,1,0:T(8,128)S(1)}, u32[]{:S(2)}, u32[]{:S(2)}) collective-permute-start(f32[5,128,128]{2,1,0:T(8,128)S(1)} %collective-permute-done.9.refs_2_), channel_id=1, source_target_pairs={{0,1},{8,1023},{1,2},{9,8},{2,3},{10,9},{3,4},{11,10},{4,5},{12,11... | collective-permute-start | bytes 983048 | tf_op jit(solution)/shard_map/ppermute | solution.py:228
  53.8 17.2 %collective-permute-start.14 = (f32[5,128,128]{2,1,0:T(8,128)S(1)}, f32[5,128,128]{2,1,0:T(8,128)S(1)}, u32[]{:S(2)}, u32[]{:S(2)}) collective-permute-start(f32[5,128,128]{2,1,0:T(8,128)S(1)} %collective-permute-done.10.refs_3_), channel_id=1, source_target_pairs={{0,1},{8,1023},{1,2},{9,8},{2,3},{10,9},{3,4},{11,10},{4,5},{12,11... | collective-permute-start | bytes 983048 | tf_op jit(solution)/shard_map/ppermute | solution.py:228
  59.1 15.9 %collective-permute-start.7 = (f32[5,128,128]{2,1,0:T(8,128)S(1)}, f32[5,128,128]{2,1,0:T(8,128)S(1)}, u32[]{:S(2)}, u32[]{:S(2)}) collective-permute-start(f32[5,128,128]{2,1,0:T(8,128)S(1)} %collective-permute-done.2.refs_0_), channel_id=1, source_target_pairs={{0,1},{8,31},{1,2},{9,8},{2,3},{10,9},{3,4},{11,10},{4,5},{12,11},... | collective-permute-start | bytes 983048 | tf_op jit(solution)/shard_map/ppermute | solution.py:228
  62.3 15.7 %collective-permute-start.12 = (f32[5,128,128]{2,1,0:T(8,128)S(1)}, f32[5,128,128]{2,1,0:T(8,128)S(1)}, u32[]{:S(2)}, u32[]{:S(2)}) collective-permute-start(f32[5,128,128]{2,1,0:T(8,128)S(1)} %collective-permute-done.8.refs_1_), channel_id=1, source_target_pairs={{0,1},{8,31},{1,2},{9,8},{2,3},{10,9},{3,4},{11,10},{4,5},{12,11},... | collective-permute-start | bytes 983048 | tf_op jit(solution)/shard_map/ppermute | solution.py:228
  69.0 14.7 %collective-permute-start.17 = (f32[5,128,128]{2,1,0:T(8,128)S(1)}, f32[5,128,128]{2,1,0:T(8,128)S(1)}, u32[]{:S(2)}, u32[]{:S(2)}) collective-permute-start(f32[5,128,128]{2,1,0:T(8,128)S(1)} %collective-permute-done.13.refs_2_), channel_id=1, source_target_pairs={{0,1},{8,1023},{1,2},{9,8},{2,3},{10,9},{3,4},{11,10},{4,5},{12,11... | collective-permute-start | bytes 983048 | tf_op jit(solution)/shard_map/ppermute | solution.py:228
  71.0 14.7 %collective-permute-start.18 = (f32[5,128,128]{2,1,0:T(8,128)S(1)}, f32[5,128,128]{2,1,0:T(8,128)S(1)}, u32[]{:S(2)}, u32[]{:S(2)}) collective-permute-start(f32[5,128,128]{2,1,0:T(8,128)S(1)} %collective-permute-done.14.refs_3_), channel_id=1, source_target_pairs={{0,1},{8,1023},{1,2},{9,8},{2,3},{10,9},{3,4},{11,10},{4,5},{12,11... | collective-permute-start | bytes 983048 | tf_op jit(solution)/shard_map/ppermute | solution.py:228
  75.1 15.9 %collective-permute-start.11 = (f32[5,128,128]{2,1,0:T(8,128)S(1)}, f32[5,128,128]{2,1,0:T(8,128)S(1)}, u32[]{:S(2)}, u32[]{:S(2)}) collective-permute-start(f32[5,128,128]{2,1,0:T(8,128)S(1)} %collective-permute-done.7.refs_0_), channel_id=1, source_target_pairs={{0,1},{8,31},{1,2},{9,8},{2,3},{10,9},{3,4},{11,10},{4,5},{12,11},... | collective-permute-start | bytes 983048 | tf_op jit(solution)/shard_map/ppermute | solution.py:228
  78.0 14.9 %collective-permute-start.16 = (f32[5,128,128]{2,1,0:T(8,128)S(1)}, f32[5,128,128]{2,1,0:T(8,128)S(1)}, u32[]{:S(2)}, u32[]{:S(2)}) collective-permute-start(f32[5,128,128]{2,1,0:T(8,128)S(1)} %collective-permute-done.12.refs_1_), channel_id=1, source_target_pairs={{0,1},{8,31},{1,2},{9,8},{2,3},{10,9},{3,4},{11,10},{4,5},{12,11},... | collective-permute-start | bytes 983048 | tf_op jit(solution)/shard_map/ppermute | solution.py:228
  83.7 12.9 %collective-permute-start.21 = (f32[5,128,128]{2,1,0:T(8,128)S(1)}, f32[5,128,128]{2,1,0:T(8,128)S(1)}, u32[]{:S(2)}, u32[]{:S(2)}) collective-permute-start(f32[5,128,128]{2,1,0:T(8,128)S(1)} %collective-permute-done.17.refs_2_), channel_id=1, source_target_pairs={{0,1},{8,1023},{1,2},{9,8},{2,3},{10,9},{3,4},{11,10},{4,5},{12,11... | collective-permute-start | bytes 983048 | tf_op jit(solution)/shard_map/ppermute | solution.py:228
  85.7 12.9 %collective-permute-start.22 = (f32[5,128,128]{2,1,0:T(8,128)S(1)}, f32[5,128,128]{2,1,0:T(8,128)S(1)}, u32[]{:S(2)}, u32[]{:S(2)}) collective-permute-start(f32[5,128,128]{2,1,0:T(8,128)S(1)} %collective-permute-done.18.refs_3_), channel_id=1, source_target_pairs={{0,1},{8,1023},{1,2},{9,8},{2,3},{10,9},{3,4},{11,10},{4,5},{12,11... | collective-permute-start | bytes 983048 | tf_op jit(solution)/shard_map/ppermute | solution.py:228
  90.9 12.9 %collective-permute-start.15 = (f32[5,128,128]{2,1,0:T(8,128)S(1)}, f32[5,128,128]{2,1,0:T(8,128)S(1)}, u32[]{:S(2)}, u32[]{:S(2)}) collective-permute-start(f32[5,128,128]{2,1,0:T(8,128)S(1)} %collective-permute-done.11.refs_0_), channel_id=1, source_target_pairs={{0,1},{8,31},{1,2},{9,8},{2,3},{10,9},{3,4},{11,10},{4,5},{12,11},... | collective-permute-start | bytes 983048 | tf_op jit(solution)/shard_map/ppermute | solution.py:228
  92.9 14.4 %collective-permute-start.20 = (f32[5,128,128]{2,1,0:T(8,128)S(1)}, f32[5,128,128]{2,1,0:T(8,128)S(1)}, u32[]{:S(2)}, u32[]{:S(2)}) collective-permute-start(f32[5,128,128]{2,1,0:T(8,128)S(1)} %collective-permute-done.16.refs_1_), channel_id=1, source_target_pairs={{0,1},{8,31},{1,2},{9,8},{2,3},{10,9},{3,4},{11,10},{4,5},{12,11},... | collective-permute-start | bytes 983048 | tf_op jit(solution)/shard_map/ppermute | solution.py:228
  96.7 16.3 %collective-permute-start.25 = (f32[5,128,128]{2,1,0:T(8,128)S(1)}, f32[5,128,128]{2,1,0:T(8,128)S(1)}, u32[]{:S(2)}, u32[]{:S(2)}) collective-permute-start(f32[5,128,128]{2,1,0:T(8,128)S(1)} %collective-permute-done.21.refs_2_), channel_id=1, source_target_pairs={{0,1},{8,1023},{1,2},{9,8},{2,3},{10,9},{3,4},{11,10},{4,5},{12,11... | collective-permute-start | bytes 983048 | tf_op jit(solution)/shard_map/ppermute | solution.py:228
  98.6 14.4 %collective-permute-start.26 = (f32[5,128,128]{2,1,0:T(8,128)S(1)}, f32[5,128,128]{2,1,0:T(8,128)S(1)}, u32[]{:S(2)}, u32[]{:S(2)}) collective-permute-start(f32[5,128,128]{2,1,0:T(8,128)S(1)} %collective-permute-done.22.refs_3_), channel_id=1, source_target_pairs={{0,1},{8,1023},{1,2},{9,8},{2,3},{10,9},{3,4},{11,10},{4,5},{12,11... | collective-permute-start | bytes 983048 | tf_op jit(solution)/shard_map/ppermute | solution.py:228
  103.8 14.5 %collective-permute-start.19 = (f32[5,128,128]{2,1,0:T(8,128)S(1)}, f32[5,128,128]{2,1,0:T(8,128)S(1)}, u32[]{:S(2)}, u32[]{:S(2)}) collective-permute-start(f32[5,128,128]{2,1,0:T(8,128)S(1)} %collective-permute-done.15.refs_0_), channel_id=1, source_target_pairs={{0,1},{8,31},{1,2},{9,8},{2,3},{10,9},{3,4},{11,10},{4,5},{12,11},... | collective-permute-start | bytes 983048 | tf_op jit(solution)/shard_map/ppermute | solution.py:228
  107.3 13.1 %collective-permute-start.24 = (f32[5,128,128]{2,1,0:T(8,128)S(1)}, f32[5,128,128]{2,1,0:T(8,128)S(1)}, u32[]{:S(2)}, u32[]{:S(2)}) collective-permute-start(f32[5,128,128]{2,1,0:T(8,128)S(1)} %collective-permute-done.20.refs_1_), channel_id=1, source_target_pairs={{0,1},{8,31},{1,2},{9,8},{2,3},{10,9},{3,4},{11,10},{4,5},{12,11},... | collective-permute-start | bytes 983048 | tf_op jit(solution)/shard_map/ppermute | solution.py:228
  113.1 34.8 %collective-permute-start.29 = (f32[10,128,128]{2,1,0:T(8,128)S(1)}, f32[10,128,128]{2,1,0:T(8,128)S(1)}, u32[]{:S(2)}, u32[]{:S(2)}) collective-permute-start(f32[10,128,128]{2,1,0:T(8,128)S(1)} %pad_maximum_fusion.1), channel_id=1, source_target_pairs={{0,1},{8,1023},{1,2},{9,8},{2,3},{10,9},{3,4},{11,10},{4,5},{12,11... | collective-permute-start | bytes 1966088 | tf_op jit(solution)/shard_map/ppermute | solution.py:228
  118.3 9.9 %collective-permute-start.23 = (f32[5,128,128]{2,1,0:T(8,128)S(1)}, f32[5,128,128]{2,1,0:T(8,128)S(1)}, u32[]{:S(2)}, u32[]{:S(2)}) collective-permute-start(f32[5,128,128]{2,1,0:T(8,128)S(1)} %collective-permute-done.19.refs_0_), channel_id=1, source_target_pairs={{0,1},{8,31},{1,2},{9,8},{2,3},{10,9},{3,4},{11,10},{4,5},{12,11},... | collective-permute-start | bytes 983048 | tf_op jit(solution)/shard_map/ppermute | solution.py:228
  120.4 11.3 %collective-permute-start.27 = (f32[5,128,128]{2,1,0:T(8,128)S(1)}, f32[5,128,128]{2,1,0:T(8,128)S(1)}, u32[]{:S(2)}, u32[]{:S(2)}) collective-permute-start(f32[5,128,128]{2,1,0:T(8,128)S(1)} %collective-permute-done.24.refs_1_), channel_id=1, source_target_pairs={{0,1},{8,31},{1,2},{9,8},{2,3},{10,9},{3,4},{11,10},{4,5},{12,11},... | collective-permute-start | bytes 983048 | tf_op jit(solution)/shard_map/ppermute | solution.py:228
  131.8 20.9 %collective-permute-start.28 = (f32[10,128,128]{2,1,0:T(8,128)S(1)}, f32[10,128,128]{2,1,0:T(8,128)S(1)}, u32[]{:S(2)}, u32[]{:S(2)}) collective-permute-start(f32[10,128,128]{2,1,0:T(8,128)S(1)} %pad_maximum_fusion), channel_id=1, source_target_pairs={{0,9},{9,0},{10,1},{7,1016},{16,25},{25,16},{26,17},{23,8},{32,41}... | collective-permute-start | bytes 1966088 | tf_op jit(solution)/shard_map/ppermute | solution.py:260
  145.9 14.7 %collective-permute-start.31 = (f32[10,128,128]{2,1,0:T(8,128)S(1)}, f32[10,128,128]{2,1,0:T(8,128)S(1)}, u32[]{:S(2)}, u32[]{:S(2)}) collective-permute-start(f32[10,128,128]{2,1,0:T(8,128)S(1)} %products.19), channel_id=1, source_target_pairs={{992,0},{993,1},{41,9},{994,2},{42,10},{995,3},{43,11},{996,4},{44... | collective-permute-start | bytes 1966088 | tf_op jit(solution)/shard_map/ppermute | solution.py:264
  149.9 10.7 %collective-permute-start.30 = (f32[10,128,128]{2,1,0:T(8,128)S(1)}, f32[10,128,128]{2,1,0:T(8,128)S(1)}, u32[]{:S(2)}, u32[]{:S(2)}) collective-permute-start(f32[10,128,128]{2,1,0:T(8,128)S(1)} %get-tuple-element.103), channel_id=1, source_target_pairs={{0,8},{1,9},{2,10},{3,11},{4,12},{5,13},{6,14},{7,15},{8,0},{9,1},... | collective-permute-start | bytes 1966088 | tf_op jit(solution)/shard_map/ppermute | solution.py:231

commit v6 on v4

--- a/solution.py
+++ b/solution.py
@@ -231,9 +231,10 @@
         return lax.ppermute(value, ring, flip_pairs(depth))
 
     own = blocks[0]
-    other, info = lax.optimization_barrier((flip(own), info))
+    other = flip(own)
     away = line_pairs(lines, depth)
-    ghost = lax.ppermute(own, every, away)
+    later, info = lax.optimization_barrier((own, info))
+    ghost = lax.ppermute(later, every, away)
     factors = [own, other, ghost]
     sums = step_call(
         depth, 0, (0, 1), (0,), ((0, 0), (1, 0)), info, [[own], [other]], factors[:1]

time: 156 us -> 156 us (level)
  the two profiles are of different devices: /device:TPU:65 before, /device:TPU:95 now
where the time goes in v6:
time: 156 us; the launch traced here: 155 us
  starting transfers between devices  110 us (71%)
  Pallas kernels  20.8 us (13%)
  waiting for transfers between devices  20.5 us (13%)
  local copies, waits for them, and re-layouts  1.99 us (1%)
    ppermute x27, starting transfers between devices, hop(): return [lax.ppermute(piece, every, pairs) for piece in held[which]]  86.2 us
    pallas_call x10, Pallas kernels, step_call(): pl.pallas_call(functools.partial(step_kernel, depth, slots, step, rows, t...  20.8 us
    ppermute x27, waiting for transfers between devices, hop(): return [lax.ppermute(piece, every, pairs) for piece in held[which]]  12.4 us
    ppermute x1, starting transfers between devices, body(): far = [lax.ppermute(jnp.concatenate(held[0]), every, far)]  11.4 us
    ppermute x1, waiting for transfers between devices, body(): foreign = lax.ppermute(foreign, every, [(b, a) for a, b in away])  7.53 us
    ppermute x1, starting transfers between devices, body(): ghost = lax.ppermute(later, every, away)  6.14 us
    ppermute x2, starting transfers between devices, flip(): return lax.ppermute(value, ring, flip_pairs(depth))  4.49 us
  transfers between devices with their start and end apart: 32, of which 10 were waited for; matrix products, arithmetic and copies ran while one was open for 1% of the time, Pallas kernels for 13%

profile of v6, /device:TPU:95, one launch (start us, length us, event | category | flops | bytes accessed | tf_op | source)
XLA Modules:
  0.0 155.4 jit_solution(15266402681781220233)
XLA Ops:
  0.0 2.6 %collective-permute-start.1 = (f32[10,128,128]{2,1,0:T(8,128)}, f32[10,128,128]{2,1,0:T(8,128)S(1)}, u32[]{:S(2)}, u32[]{:S(2)}) collective-permute-start(f32[10,128,128]{2,1,0:T(8,128)} %bitcast.11), channel_id=1, source_target_pairs={{0,8},{1,9},{2,10},{3,11},{4,12},{5,13},{6,14},{7,15},{8,0},{9,1},... | collective-permute-start | bytes 1966088 | tf_op jit(solution)/shard_map/ppermute | solution.py:231
  2.6 1.1 copy.26
  3.7 0.6 gather_fusion
  4.3 0.1 subtract_add_fusion
  4.4 0.1 add.101
  4.6 0.0 copy-start
  4.7 2.1 %collective-permute-start.4 = (f32[5,128,128]{2,1,0:T(8,128)S(1)}, f32[5,128,128]{2,1,0:T(8,128)S(1)}, u32[]{:S(2)}, u32[]{:S(2)}) collective-permute-start(f32[5,128,128]{2,1,0:T(8,128)S(1)} %get-tuple-element.106), channel_id=1, source_target_pairs={{0,1},{8,1023},{1,2},{9,8},{2,3},{10,9},{3,4},{11,10},{4,5},{12,11... | collective-permute-start | bytes 983048 | tf_op jit(solution)/shard_map/ppermute | solution.py:228
  6.7 17.6 %collective-permute-start.5 = (f32[5,128,128]{2,1,0:T(8,128)S(1)}, f32[5,128,128]{2,1,0:T(8,128)S(1)}, u32[]{:S(2)}, u32[]{:S(2)}) collective-permute-start(f32[5,128,128]{2,1,0:T(8,128)S(1)} %get-tuple-element.105), channel_id=1, source_target_pairs={{0,1},{8,1023},{1,2},{9,8},{2,3},{10,9},{3,4},{11,10},{4,5},{12,11... | collective-permute-start | bytes 983048 | tf_op jit(solution)/shard_map/ppermute | solution.py:228
  24.3 0.1 pad_add_fusion.info
  24.4 6.1 %collective-permute-start.6 = (f32[10,128,128]{2,1,0:T(8,128)S(1)}, f32[10,128,128]{2,1,0:T(8,128)S(1)}, u32[]{:S(2)}, u32[]{:S(2)}) collective-permute-start(f32[10,128,128]{2,1,0:T(8,128)S(1)} %bitcast.12), channel_id=1, source_target_pairs={{0,992},{1,993},{9,41},{2,994},{10,42},{3,995},{11,43},{4,996},{12... | collective-permute-start | bytes 1966088 | tf_op jit(solution)/shard_map/ppermute | solution.py:237
  30.6 1.9 %collective-permute-start = (f32[5,128,128]{2,1,0:T(8,128)S(1)}, f32[5,128,128]{2,1,0:T(8,128)S(1)}, u32[]{:S(2)}, u32[]{:S(2)}) collective-permute-start(f32[5,128,128]{2,1,0:T(8,128)S(1)} %get-tuple-element.108), channel_id=1, source_target_pairs={{0,1},{8,31},{1,2},{9,8},{2,3},{10,9},{3,4},{11,10},{4,5},{12,11},... | collective-permute-start | bytes 983048 | tf_op jit(solution)/shard_map/ppermute | solution.py:228
  32.5 1.9 %collective-permute-start.3 = (f32[5,128,128]{2,1,0:T(8,128)S(1)}, f32[5,128,128]{2,1,0:T(8,128)S(1)}, u32[]{:S(2)}, u32[]{:S(2)}) collective-permute-start(f32[5,128,128]{2,1,0:T(8,128)S(1)} %get-tuple-element.107), channel_id=1, source_target_pairs={{0,1},{8,31},{1,2},{9,8},{2,3},{10,9},{3,4},{11,10},{4,5},{12,11},... | collective-permute-start | bytes 983048 | tf_op jit(solution)/shard_map/ppermute | solution.py:228
  34.4 0.0 collective-permute-done.4.refs_2_
  34.5 1.9 %collective-permute-start.9 = (f32[5,128,128]{2,1,0:T(8,128)S(1)}, f32[5,128,128]{2,1,0:T(8,128)S(1)}, u32[]{:S(2)}, u32[]{:S(2)}) collective-permute-start(f32[5,128,128]{2,1,0:T(8,128)S(1)} %collective-permute-done.4.refs_2_), channel_id=1, source_target_pairs={{0,1},{8,1023},{1,2},{9,8},{2,3},{10,9},{3,4},{11,10},{4,5},{12,11... | collective-permute-start | bytes 983048 | tf_op jit(solution)/shard_map/ppermute | solution.py:228
  36.4 1.9 %collective-permute-start.10 = (f32[5,128,128]{2,1,0:T(8,128)S(1)}, f32[5,128,128]{2,1,0:T(8,128)S(1)}, u32[]{:S(2)}, u32[]{:S(2)}) collective-permute-start(f32[5,128,128]{2,1,0:T(8,128)S(1)} %collective-permute-done.5.refs_3_), channel_id=1, source_target_pairs={{0,1},{8,1023},{1,2},{9,8},{2,3},{10,9},{3,4},{11,10},{4,5},{12,11... | collective-permute-start | bytes 983048 | tf_op jit(solution)/shard_map/ppermute | solution.py:228
  38.3 2.4 %products.10.refs_7_ = f32[10,128,128]{2,1,0:T(8,128)S(1)} custom-call(s32[962]{0:T(1024)S(1)} %pad_add_fusion.info, f32[10,128,128]{2,1,0:T(8,128)S(1)} %bitcast.13, f32[10,128,128]{2,1,0:T(8,128)S(1)} %collective-permute-done.1.refs_1_.refs_5_.refs_4_, f32[10,128,128]{2,1,0:T(8,128)S(1)} %bitcast.14), custom_call_target="tpu_custom_call" | custom-call | flops 200000000 | bytes 8000000 | tf_op jit(solution)/shard_map/products/pallas_call | solution.py:188
  40.7 1.9 %collective-permute-start.2 = (f32[5,128,128]{2,1,0:T(8,128)S(1)}, f32[5,128,128]{2,1,0:T(8,128)S(1)}, u32[]{:S(2)}, u32[]{:S(2)}) collective-permute-start(f32[5,128,128]{2,1,0:T(8,128)S(1)} %collective-permute-done.refs_0_), channel_id=1, source_target_pairs={{0,1},{8,31},{1,2},{9,8},{2,3},{10,9},{3,4},{11,10},{4,5},{12,11},... | collective-permute-start | bytes 983048 | tf_op jit(solution)/shard_map/ppermute | solution.py:228
  42.7 1.9 %collective-permute-start.8 = (f32[5,128,128]{2,1,0:T(8,128)S(1)}, f32[5,128,128]{2,1,0:T(8,128)S(1)}, u32[]{:S(2)}, u32[]{:S(2)}) collective-permute-start(f32[5,128,128]{2,1,0:T(8,128)S(1)} %collective-permute-done.3.refs_1_), channel_id=1, source_target_pairs={{0,1},{8,31},{1,2},{9,8},{2,3},{10,9},{3,4},{11,10},{4,5},{12,11},... | collective-permute-start | bytes 983048 | tf_op jit(solution)/shard_map/ppermute | solution.py:228
  44.6 0.8 collective-permute-done.9.refs_2_
  45.4 2.2 %collective-permute-start.13 = (f32[5,128,128]{2,1,0:T(8,128)S(1)}, f32[5,128,128]{2,1,0:T(8,128)S(1)}, u32[]{:S(2)}, u32[]{:S(2)}) collective-permute-start(f32[5,128,128]{2,1,0:T(8,128)S(1)} %collective-permute-done.9.refs_2_), channel_id=1, source_target_pairs={{0,1},{8,1023},{1,2},{9,8},{2,3},{10,9},{3,4},{11,10},{4,5},{12,11... | collective-permute-start | bytes 983048 | tf_op jit(solution)/shard_map/ppermute | solution.py:228
  47.6 1.6 %collective-permute-done.10.refs_3_ = f32[5,128,128]{2,1,0:T(8,128)S(1)} collective-permute-done((f32[5,128,128]{2,1,0:T(8,128)S(1)}, f32[5,128,128]{2,1,0:T(8,128)S(1)}, u32[]{:S(2)}, u32[]{:S(2)}) %collective-permute-start.10) | collective-permute-done | bytes 327712 | tf_op jit(solution)/shard_map/ppermute | solution.py:228
  49.2 1.9 %collective-permute-start.14 = (f32[5,128,128]{2,1,0:T(8,128)S(1)}, f32[5,128,128]{2,1,0:T(8,128)S(1)}, u32[]{:S(2)}, u32[]{:S(2)}) collective-permute-start(f32[5,128,128]{2,1,0:T(8,128)S(1)} %collective-permute-done.10.refs_3_), channel_id=1, source_target_pairs={{0,1},{8,1023},{1,2},{9,8},{2,3},{10,9},{3,4},{11,10},{4,5},{12,11... | collective-permute-start | bytes 983048 | tf_op jit(solution)/shard_map/ppermute | solution.py:228
  51.3 2.1 %products.11 = (f32[10,128,128]{2,1,0:T(8,128)S(1)}, f32[10,128,128]{2,1,0:T(8,128)S(1)}, f32[10,128,128]{2,1,0:T(8,128)S(1)}) custom-call(s32[962]{0:T(1024)S(1)} %pad_add_fusion.info, f32[5,128,128]{2,1,0:T(8,128)S(1)} %collective-permute-done.refs_0_, ...), custom_call_target="tpu_custom_call", output_to_operand_aliasing={{0}: (8, {}), {1}: (9, {}), {2}: (10, {})} | custom-call | flops 200000000 | bytes 8000000 | tf_op jit(solution)/shard_map/products/pallas_call | solution.py:188
  53.4 0.0 collective-permute-done.2.refs_0_
  53.4 3.4 %collective-permute-start.7 = (f32[5,128,128]{2,1,0:T(8,128)S(1)}, f32[5,128,128]{2,1,0:T(8,128)S(1)}, u32[]{:S(2)}, u32[]{:S(2)}) collective-permute-start(f32[5,128,128]{2,1,0:T(8,128)S(1)} %collective-permute-done.2.refs_0_), channel_id=1, source_target_pairs={{0,1},{8,31},{1,2},{9,8},{2,3},{10,9},{3,4},{11,10},{4,5},{12,11},... | collective-permute-start | bytes 983048 | tf_op jit(solution)/shard_map/ppermute | solution.py:228
  56.8 0.0 collective-permute-done.8.refs_1_
  56.8 3.6 %collective-permute-start.12 = (f32[5,128,128]{2,1,0:T(8,128)S(1)}, f32[5,128,128]{2,1,0:T(8,128)S(1)}, u32[]{:S(2)}, u32[]{:S(2)}) collective-permute-start(f32[5,128,128]{2,1,0:T(8,128)S(1)} %collective-permute-done.8.refs_1_), channel_id=1, source_target_pairs={{0,1},{8,31},{1,2},{9,8},{2,3},{10,9},{3,4},{11,10},{4,5},{12,11},... | collective-permute-start | bytes 983048 | tf_op jit(solution)/shard_map/ppermute | solution.py:228
  60.4 1.9 %collective-permute-start.17 = (f32[5,128,128]{2,1,0:T(8,128)S(1)}, f32[5,128,128]{2,1,0:T(8,128)S(1)}, u32[]{:S(2)}, u32[]{:S(2)}) collective-permute-start(f32[5,128,128]{2,1,0:T(8,128)S(1)} %collective-permute-done.13.refs_2_), channel_id=1, source_target_pairs={{0,1},{8,1023},{1,2},{9,8},{2,3},{10,9},{3,4},{11,10},{4,5},{12,11... | collective-permute-start | bytes 983048 | tf_op jit(solution)/shard_map/ppermute | solution.py:228
  62.3 0.9 collective-permute-done.14.refs_3_
  63.3 1.9 %collective-permute-start.18 = (f32[5,128,128]{2,1,0:T(8,128)S(1)}, f32[5,128,128]{2,1,0:T(8,128)S(1)}, u32[]{:S(2)}, u32[]{:S(2)}) collective-permute-start(f32[5,128,128]{2,1,0:T(8,128)S(1)} %collective-permute-done.14.refs_3_), channel_id=1, source_target_pairs={{0,1},{8,1023},{1,2},{9,8},{2,3},{10,9},{3,4},{11,10},{4,5},{12,11... | collective-permute-start | bytes 983048 | tf_op jit(solution)/shard_map/ppermute | solution.py:228
  65.2 2.1 %products.12 = (f32[10,128,128]{2,1,0:T(8,128)S(1)}, f32[10,128,128]{2,1,0:T(8,128)S(1)}, f32[10,128,128]{2,1,0:T(8,128)S(1)}) custom-call(s32[962]{0:T(1024)S(1)} %pad_add_fusion.info, f32[5,128,128]{2,1,0:T(8,128)S(1)} %collective-permute-done.2.refs_0_, ...), custom_call_target="tpu_custom_call", output_to_operand_aliasing={{0}: (8, {}), {1}: (9, {}), {2}: (10, {})} | custom-call | flops 200000000 | bytes 8000000 | tf_op jit(solution)/shard_map/products/pallas_call | solution.py:188
  67.3 0.0 collective-permute-done.7.refs_0_
  67.3 2.2 %collective-permute-start.11 = (f32[5,128,128]{2,1,0:T(8,128)S(1)}, f32[5,128,128]{2,1,0:T(8,128)S(1)}, u32[]{:S(2)}, u32[]{:S(2)}) collective-permute-start(f32[5,128,128]{2,1,0:T(8,128)S(1)} %collective-permute-done.7.refs_0_), channel_id=1, source_target_pairs={{0,1},{8,31},{1,2},{9,8},{2,3},{10,9},{3,4},{11,10},{4,5},{12,11},... | collective-permute-start | bytes 983048 | tf_op jit(solution)/shard_map/ppermute | solution.py:228
  69.5 0.8 collective-permute-done.12.refs_1_
  70.3 4.0 %collective-permute-start.16 = (f32[5,128,128]{2,1,0:T(8,128)S(1)}, f32[5,128,128]{2,1,0:T(8,128)S(1)}, u32[]{:S(2)}, u32[]{:S(2)}) collective-permute-start(f32[5,128,128]{2,1,0:T(8,128)S(1)} %collective-permute-done.12.refs_1_), channel_id=1, source_target_pairs={{0,1},{8,31},{1,2},{9,8},{2,3},{10,9},{3,4},{11,10},{4,5},{12,11},... | collective-permute-start | bytes 983048 | tf_op jit(solution)/shard_map/ppermute | solution.py:228
  74.3 0.0 collective-permute-done.17.refs_2_
  74.3 1.9 %collective-permute-start.21 = (f32[5,128,128]{2,1,0:T(8,128)S(1)}, f32[5,128,128]{2,1,0:T(8,128)S(1)}, u32[]{:S(2)}, u32[]{:S(2)}) collective-permute-start(f32[5,128,128]{2,1,0:T(8,128)S(1)} %collective-permute-done.17.refs_2_), channel_id=1, source_target_pairs={{0,1},{8,1023},{1,2},{9,8},{2,3},{10,9},{3,4},{11,10},{4,5},{12,11... | collective-permute-start | bytes 983048 | tf_op jit(solution)/shard_map/ppermute | solution.py:228
  76.3 1.0 collective-permute-done.18.refs_3_
  77.3 3.2 %collective-permute-start.22 = (f32[5,128,128]{2,1,0:T(8,128)S(1)}, f32[5,128,128]{2,1,0:T(8,128)S(1)}, u32[]{:S(2)}, u32[]{:S(2)}) collective-permute-start(f32[5,128,128]{2,1,0:T(8,128)S(1)} %collective-permute-done.18.refs_3_), channel_id=1, source_target_pairs={{0,1},{8,1023},{1,2},{9,8},{2,3},{10,9},{3,4},{11,10},{4,5},{12,11... | collective-permute-start | bytes 983048 | tf_op jit(solution)/shard_map/ppermute | solution.py:228
  80.5 2.1 %products.13 = (f32[10,128,128]{2,1,0:T(8,128)S(1)}, f32[10,128,128]{2,1,0:T(8,128)S(1)}, f32[10,128,128]{2,1,0:T(8,128)S(1)}) custom-call(s32[962]{0:T(1024)S(1)} %pad_add_fusion.info, f32[5,128,128]{2,1,0:T(8,128)S(1)} %collective-permute-done.7.refs_0_, ...), custom_call_target="tpu_custom_call", output_to_operand_aliasing={{0}: (8, {}), {1}: (9, {}), {2}: (10, {})} | custom-call | flops 200000000 | bytes 8000000 | tf_op jit(solution)/shard_map/products/pallas_call | solution.py:188
  82.6 4.0 %collective-permute-start.15 = (f32[5,128,128]{2,1,0:T(8,128)S(1)}, f32[5,128,128]{2,1,0:T(8,128)S(1)}, u32[]{:S(2)}, u32[]{:S(2)}) collective-permute-start(f32[5,128,128]{2,1,0:T(8,128)S(1)} %collective-permute-done.11.refs_0_), channel_id=1, source_target_pairs={{0,1},{8,31},{1,2},{9,8},{2,3},{10,9},{3,4},{11,10},{4,5},{12,11},... | collective-permute-start | bytes 983048 | tf_op jit(solution)/shard_map/ppermute | solution.py:228
  86.7 3.3 %collective-permute-start.20 = (f32[5,128,128]{2,1,0:T(8,128)S(1)}, f32[5,128,128]{2,1,0:T(8,128)S(1)}, u32[]{:S(2)}, u32[]{:S(2)}) collective-permute-start(f32[5,128,128]{2,1,0:T(8,128)S(1)} %collective-permute-done.16.refs_1_), channel_id=1, source_target_pairs={{0,1},{8,31},{1,2},{9,8},{2,3},{10,9},{3,4},{11,10},{4,5},{12,11},... | collective-permute-start | bytes 983048 | tf_op jit(solution)/shard_map/ppermute | solution.py:228
  90.0 3.1 %collective-permute-start.25 = (f32[5,128,128]{2,1,0:T(8,128)S(1)}, f32[5,128,128]{2,1,0:T(8,128)S(1)}, u32[]{:S(2)}, u32[]{:S(2)}) collective-permute-start(f32[5,128,128]{2,1,0:T(8,128)S(1)} %collective-permute-done.21.refs_2_), channel_id=1, source_target_pairs={{0,1},{8,1023},{1,2},{9,8},{2,3},{10,9},{3,4},{11,10},{4,5},{12,11... | collective-permute-start | bytes 983048 | tf_op jit(solution)/shard_map/ppermute | solution.py:228
  93.1 1.9 %collective-permute-start.26 = (f32[5,128,128]{2,1,0:T(8,128)S(1)}, f32[5,128,128]{2,1,0:T(8,128)S(1)}, u32[]{:S(2)}, u32[]{:S(2)}) collective-permute-start(f32[5,128,128]{2,1,0:T(8,128)S(1)} %collective-permute-done.22.refs_3_), channel_id=1, source_target_pairs={{0,1},{8,1023},{1,2},{9,8},{2,3},{10,9},{3,4},{11,10},{4,5},{12,11... | collective-permute-start | bytes 983048 | tf_op jit(solution)/shard_map/ppermute | solution.py:228
  95.0 3.3 %products.14 = (f32[10,128,128]{2,1,0:T(8,128)S(1)}, f32[10,128,128]{2,1,0:T(8,128)S(1)}, f32[10,128,128]{2,1,0:T(8,128)S(1)}) custom-call(s32[962]{0:T(1024)S(1)} %pad_add_fusion.info, f32[5,128,128]{2,1,0:T(8,128)S(1)} %collective-permute-done.11.refs_0_, ...), custom_call_target="tpu_custom_call", output_to_operand_aliasing={{0}: (8, {}), {1}: (9, {}), {2}: (10, {})} | custom-call | flops 200000000 | bytes 8000000 | tf_op jit(solution)/shard_map/products/pallas_call | solution.py:188
  98.3 1.9 %collective-permute-start.19 = (f32[5,128,128]{2,1,0:T(8,128)S(1)}, f32[5,128,128]{2,1,0:T(8,128)S(1)}, u32[]{:S(2)}, u32[]{:S(2)}) collective-permute-start(f32[5,128,128]{2,1,0:T(8,128)S(1)} %collective-permute-done.15.refs_0_), channel_id=1, source_target_pairs={{0,1},{8,31},{1,2},{9,8},{2,3},{10,9},{3,4},{11,10},{4,5},{12,11},... | collective-permute-start | bytes 983048 | tf_op jit(solution)/shard_map/ppermute | solution.py:228
  100.3 3.5 %collective-permute-start.24 = (f32[5,128,128]{2,1,0:T(8,128)S(1)}, f32[5,128,128]{2,1,0:T(8,128)S(1)}, u32[]{:S(2)}, u32[]{:S(2)}) collective-permute-start(f32[5,128,128]{2,1,0:T(8,128)S(1)} %collective-permute-done.20.refs_1_), channel_id=1, source_target_pairs={{0,1},{8,31},{1,2},{9,8},{2,3},{10,9},{3,4},{11,10},{4,5},{12,11},... | collective-permute-start | bytes 983048 | tf_op jit(solution)/shard_map/ppermute | solution.py:228
  103.9 1.6 %collective-permute-done.26.refs_3_ = f32[5,128,128]{2,1,0:T(8,128)S(1)} collective-permute-done((f32[5,128,128]{2,1,0:T(8,128)S(1)}, f32[5,128,128]{2,1,0:T(8,128)S(1)}, u32[]{:S(2)}, u32[]{:S(2)}) %collective-permute-start.26) | collective-permute-done | bytes 327712 | tf_op jit(solution)/shard_map/ppermute | solution.py:228
  105.5 1.9 %collective-permute-start.29 = (f32[10,128,128]{2,1,0:T(8,128)S(1)}, f32[10,128,128]{2,1,0:T(8,128)S(1)}, u32[]{:S(2)}, u32[]{:S(2)}) collective-permute-start(f32[10,128,128]{2,1,0:T(8,128)S(1)} %pad_maximum_fusion.1), channel_id=1, source_target_pairs={{0,1},{8,1023},{1,2},{9,8},{2,3},{10,9},{3,4},{11,10},{4,5},{12,11... | collective-permute-start | bytes 1966088 | tf_op jit(solution)/shard_map/ppermute | solution.py:228
  107.4 2.1 %products.15 = (f32[10,128,128]{2,1,0:T(8,128)S(1)}, f32[10,128,128]{2,1,0:T(8,128)S(1)}, f32[10,128,128]{2,1,0:T(8,128)S(1)}) custom-call(s32[962]{0:T(1024)S(1)} %pad_add_fusion.info, f32[5,128,128]{2,1,0:T(8,128)S(1)} %collective-permute-done.15.refs_0_, ...), custom_call_target="tpu_custom_call", output_to_operand_aliasing={{0}: (8, {}), {1}: (9, {}), {2}: (10, {})} | custom-call | flops 200000000 | bytes 8000000 | tf_op jit(solution)/shard_map/products/pallas_call | solution.py:188
  109.5 4.3 %collective-permute-start.23 = (f32[5,128,128]{2,1,0:T(8,128)S(1)}, f32[5,128,128]{2,1,0:T(8,128)S(1)}, u32[]{:S(2)}, u32[]{:S(2)}) collective-permute-start(f32[5,128,128]{2,1,0:T(8,128)S(1)} %collective-permute-done.19.refs_0_), channel_id=1, source_target_pairs={{0,1},{8,31},{1,2},{9,8},{2,3},{10,9},{3,4},{11,10},{4,5},{12,11},... | collective-permute-start | bytes 983048 | tf_op jit(solution)/shard_map/ppermute | solution.py:228
  113.8 4.9 %collective-permute-start.27 = (f32[5,128,128]{2,1,0:T(8,128)S(1)}, f32[5,128,128]{2,1,0:T(8,128)S(1)}, u32[]{:S(2)}, u32[]{:S(2)}) collective-permute-start(f32[5,128,128]{2,1,0:T(8,128)S(1)} %collective-permute-done.24.refs_1_), channel_id=1, source_target_pairs={{0,1},{8,31},{1,2},{9,8},{2,3},{10,9},{3,4},{11,10},{4,5},{12,11},... | collective-permute-start | bytes 983048 | tf_op jit(solution)/shard_map/ppermute | solution.py:228
  118.7 2.1 %products.16 = (f32[10,128,128]{2,1,0:T(8,128)S(1)}, f32[10,128,128]{2,1,0:T(8,128)S(1)}, f32[10,128,128]{2,1,0:T(8,128)S(1)}) custom-call(s32[962]{0:T(1024)S(1)} %pad_add_fusion.info, f32[5,128,128]{2,1,0:T(8,128)S(1)} %collective-permute-done.19.refs_0_, ...), custom_call_target="tpu_custom_call", output_to_operand_aliasing={{0}: (8, {}), {1}: (9, {}), {2}: (10, {})} | custom-call | flops 200000000 | bytes 8000000 | tf_op jit(solution)/shard_map/products/pallas_call | solution.py:188
  120.8 2.1 %collective-permute-done.23.refs_0_ = f32[5,128,128]{2,1,0:T(8,128)S(1)} collective-permute-done((f32[5,128,128]{2,1,0:T(8,128)S(1)}, f32[5,128,128]{2,1,0:T(8,128)S(1)}, u32[]{:S(2)}, u32[]{:S(2)}) %collective-permute-start.23) | collective-permute-done | bytes 327712 | tf_op jit(solution)/shard_map/ppermute | solution.py:228
  123.0 3.5 %collective-permute-done.27.refs_1_ = f32[5,128,128]{2,1,0:T(8,128)S(1)} collective-permute-done((f32[5,128,128]{2,1,0:T(8,128)S(1)}, f32[5,128,128]{2,1,0:T(8,128)S(1)}, u32[]{:S(2)}, u32[]{:S(2)}) %collective-permute-start.27) | collective-permute-done | bytes 327712 | tf_op jit(solution)/shard_map/ppermute | solution.py:228
  126.5 11.4 %collective-permute-start.28 = (f32[10,128,128]{2,1,0:T(8,128)S(1)}, f32[10,128,128]{2,1,0:T(8,128)S(1)}, u32[]{:S(2)}, u32[]{:S(2)}) collective-permute-start(f32[10,128,128]{2,1,0:T(8,128)S(1)} %pad_maximum_fusion), channel_id=1, source_target_pairs={{0,9},{9,0},{10,1},{7,1016},{16,25},{25,16},{26,17},{23,8},{32,41}... | collective-permute-start | bytes 1966088 | tf_op jit(solution)/shard_map/ppermute | solution.py:260
  138.0 1.8 %products.19 = f32[10,128,128]{2,1,0:T(8,128)S(1)} custom-call(s32[962]{0:T(1024)S(1)} %pad_add_fusion.info, f32[5,128,128]{2,1,0:T(8,128)S(1)} %collective-permute-done.23.refs_0_, f32[5,128,128]{2,1,0:T(8,128)S(1)} %collective-permute-done.27.refs_1_, f32[10,128,128]{2,1,0:T(8,128)S(1)} %collective-permute-done.6.refs_6_.refs_2_, ...), custom_call_target="tpu_custom_call", output_to_operand_aliasing={{}: (4, {})} | custom-call | flops 200000000 | bytes 8000000 | tf_op jit(solution)/shard_map/products/pallas_call | solution.py:188
  139.8 1.9 %collective-permute-start.31 = (f32[10,128,128]{2,1,0:T(8,128)S(1)}, f32[10,128,128]{2,1,0:T(8,128)S(1)}, u32[]{:S(2)}, u32[]{:S(2)}) collective-permute-start(f32[10,128,128]{2,1,0:T(8,128)S(1)} %products.19), channel_id=1, source_target_pairs={{992,0},{993,1},{41,9},{994,2},{42,10},{995,3},{43,11},{996,4},{44... | collective-permute-start | bytes 1966088 | tf_op jit(solution)/shard_map/ppermute | solution.py:264
  141.7 2.0 %products.17 = (f32[10,128,128]{2,1,0:T(8,128)S(1)}, f32[10,128,128]{2,1,0:T(8,128)S(1)}) custom-call(s32[962]{0:T(1024)S(1)} %pad_add_fusion.info, f32[5,128,128]{2,1,0:T(8,128)S(1)} %collective-permute-done.23.refs_0_, f32[5,128,128]{2,1,0:T(8,128)S(1)} %collective-permute-done.27.refs_1_, ...), custom_call_target="tpu_custom_call", output_to_operand_aliasing={{0}: (6, {}), {1}: (7, {})} | custom-call | flops 200000000 | bytes 8000000 | tf_op jit(solution)/shard_map/products/pallas_call | solution.py:188
  143.8 1.9 %collective-permute-start.30 = (f32[10,128,128]{2,1,0:T(8,128)S(1)}, f32[10,128,128]{2,1,0:T(8,128)S(1)}, u32[]{:S(2)}, u32[]{:S(2)}) collective-permute-start(f32[10,128,128]{2,1,0:T(8,128)S(1)} %get-tuple-element.103), channel_id=1, source_target_pairs={{0,8},{1,9},{2,10},{3,11},{4,12},{5,13},{6,14},{7,15},{8,0},{9,1},... | collective-permute-start | bytes 1966088 | tf_op jit(solution)/shard_map/ppermute | solution.py:231
  145.7 0.5 collective-permute-done.28.refs_0_
  146.2 0.7 products.18
  146.9 7.5 %collective-permute-done.31 = f32[10,128,128]{2,1,0:T(8,128)S(1)} collective-permute-done((f32[10,128,128]{2,1,0:T(8,128)S(1)}, f32[10,128,128]{2,1,0:T(8,128)S(1)}, u32[]{:S(2)}, u32[]{:S(2)}) %collective-permute-start.31) | collective-permute-done | bytes 655392 | tf_op jit(solution)/shard_map/ppermute | solution.py:264
  154.4 0.9 add_bitcast_fusion
  (28 shorter events, 0.4 us)
Async XLA Ops:
  0.0 4.6 %collective-permute-start.1 = (f32[10,128,128]{2,1,0:T(8,128)}, f32[10,128,128]{2,1,0:T(8,128)S(1)}, u32[]{:S(2)}, u32[]{:S(2)}) collective-permute-start(f32[10,128,128]{2,1,0:T(8,128)} %bitcast.11), channel_id=1, source_target_pairs={{0,8},{1,9},{2,10},{3,11},{4,12},{5,13},{6,14},{7,15},{8,0},{9,1},... | collective-permute-start | bytes 1966088 | tf_op jit(solution)/shard_map/ppermute | solution.py:231
  4.6 19.8 %copy-start = (f32[1,10,128,128]{3,2,1,0:T(8,128)S(1)}, f32[1,10,128,128]{3,2,1,0:T(8,128)}, u32[]{:S(2)}) copy-start(f32[1,10,128,128]{3,2,1,0:T(8,128)} %param.2) | copy-start | bytes 1966084
  4.7 29.8 %collective-permute-start.4 = (f32[5,128,128]{2,1,0:T(8,128)S(1)}, f32[5,128,128]{2,1,0:T(8,128)S(1)}, u32[]{:S(2)}, u32[]{:S(2)}) collective-permute-start(f32[5,128,128]{2,1,0:T(8,128)S(1)} %get-tuple-element.106), channel_id=1, source_target_pairs={{0,1},{8,1023},{1,2},{9,8},{2,3},{10,9},{3,4},{11,10},{4,5},{12,11... | collective-permute-start | bytes 983048 | tf_op jit(solution)/shard_map/ppermute | solution.py:228
  6.7 29.7 %collective-permute-start.5 = (f32[5,128,128]{2,1,0:T(8,128)S(1)}, f32[5,128,128]{2,1,0:T(8,128)S(1)}, u32[]{:S(2)}, u32[]{:S(2)}) collective-permute-start(f32[5,128,128]{2,1,0:T(8,128)S(1)} %get-tuple-element.105), channel_id=1, source_target_pairs={{0,1},{8,1023},{1,2},{9,8},{2,3},{10,9},{3,4},{11,10},{4,5},{12,11... | collective-permute-start | bytes 983048 | tf_op jit(solution)/shard_map/ppermute | solution.py:228
  24.4 26.9 %collective-permute-start.6 = (f32[10,128,128]{2,1,0:T(8,128)S(1)}, f32[10,128,128]{2,1,0:T(8,128)S(1)}, u32[]{:S(2)}, u32[]{:S(2)}) collective-permute-start(f32[10,128,128]{2,1,0:T(8,128)S(1)} %bitcast.12), channel_id=1, source_target_pairs={{0,992},{1,993},{9,41},{2,994},{10,42},{3,995},{11,43},{4,996},{12... | collective-permute-start | bytes 1966088 | tf_op jit(solution)/shard_map/ppermute | solution.py:237
  30.6 10.1 %collective-permute-start = (f32[5,128,128]{2,1,0:T(8,128)S(1)}, f32[5,128,128]{2,1,0:T(8,128)S(1)}, u32[]{:S(2)}, u32[]{:S(2)}) collective-permute-start(f32[5,128,128]{2,1,0:T(8,128)S(1)} %get-tuple-element.108), channel_id=1, source_target_pairs={{0,1},{8,31},{1,2},{9,8},{2,3},{10,9},{3,4},{11,10},{4,5},{12,11},... | collective-permute-start | bytes 983048 | tf_op jit(solution)/shard_map/ppermute | solution.py:228
  32.5 10.1 %collective-permute-start.3 = (f32[5,128,128]{2,1,0:T(8,128)S(1)}, f32[5,128,128]{2,1,0:T(8,128)S(1)}, u32[]{:S(2)}, u32[]{:S(2)}) collective-permute-start(f32[5,128,128]{2,1,0:T(8,128)S(1)} %get-tuple-element.107), channel_id=1, source_target_pairs={{0,1},{8,31},{1,2},{9,8},{2,3},{10,9},{3,4},{11,10},{4,5},{12,11},... | collective-permute-start | bytes 983048 | tf_op jit(solution)/shard_map/ppermute | solution.py:228
  34.5 11.0 %collective-permute-start.9 = (f32[5,128,128]{2,1,0:T(8,128)S(1)}, f32[5,128,128]{2,1,0:T(8,128)S(1)}, u32[]{:S(2)}, u32[]{:S(2)}) collective-permute-start(f32[5,128,128]{2,1,0:T(8,128)S(1)} %collective-permute-done.4.refs_2_), channel_id=1, source_target_pairs={{0,1},{8,1023},{1,2},{9,8},{2,3},{10,9},{3,4},{11,10},{4,5},{12,11... | collective-permute-start | bytes 983048 | tf_op jit(solution)/shard_map/ppermute | solution.py:228
  36.4 12.8 %collective-permute-start.10 = (f32[5,128,128]{2,1,0:T(8,128)S(1)}, f32[5,128,128]{2,1,0:T(8,128)S(1)}, u32[]{:S(2)}, u32[]{:S(2)}) collective-permute-start(f32[5,128,128]{2,1,0:T(8,128)S(1)} %collective-permute-done.5.refs_3_), channel_id=1, source_target_pairs={{0,1},{8,1023},{1,2},{9,8},{2,3},{10,9},{3,4},{11,10},{4,5},{12,11... | collective-permute-start | bytes 983048 | tf_op jit(solution)/shard_map/ppermute | solution.py:228
  40.7 12.7 %collective-permute-start.2 = (f32[5,128,128]{2,1,0:T(8,128)S(1)}, f32[5,128,128]{2,1,0:T(8,128)S(1)}, u32[]{:S(2)}, u32[]{:S(2)}) collective-permute-start(f32[5,128,128]{2,1,0:T(8,128)S(1)} %collective-permute-done.refs_0_), channel_id=1, source_target_pairs={{0,1},{8,31},{1,2},{9,8},{2,3},{10,9},{3,4},{11,10},{4,5},{12,11},... | collective-permute-start | bytes 983048 | tf_op jit(solution)/shard_map/ppermute | solution.py:228
  42.7 14.1 %collective-permute-start.8 = (f32[5,128,128]{2,1,0:T(8,128)S(1)}, f32[5,128,128]{2,1,0:T(8,128)S(1)}, u32[]{:S(2)}, u32[]{:S(2)}) collective-permute-start(f32[5,128,128]{2,1,0:T(8,128)S(1)} %collective-permute-done.3.refs_1_), channel_id=1, source_target_pairs={{0,1},{8,31},{1,2},{9,8},{2,3},{10,9},{3,4},{11,10},{4,5},{12,11},... | collective-permute-start | bytes 983048 | tf_op jit(solution)/shard_map/ppermute | solution.py:228
  45.4 15.0 %collective-permute-start.13 = (f32[5,128,128]{2,1,0:T(8,128)S(1)}, f32[5,128,128]{2,1,0:T(8,128)S(1)}, u32[]{:S(2)}, u32[]{:S(2)}) collective-permute-start(f32[5,128,128]{2,1,0:T(8,128)S(1)} %collective-permute-done.9.refs_2_), channel_id=1, source_target_pairs={{0,1},{8,1023},{1,2},{9,8},{2,3},{10,9},{3,4},{11,10},{4,5},{12,11... | collective-permute-start | bytes 983048 | tf_op jit(solution)/shard_map/ppermute | solution.py:228
  49.2 14.0 %collective-permute-start.14 = (f32[5,128,128]{2,1,0:T(8,128)S(1)}, f32[5,128,128]{2,1,0:T(8,128)S(1)}, u32[]{:S(2)}, u32[]{:S(2)}) collective-permute-start(f32[5,128,128]{2,1,0:T(8,128)S(1)} %collective-permute-done.10.refs_3_), channel_id=1, source_target_pairs={{0,1},{8,1023},{1,2},{9,8},{2,3},{10,9},{3,4},{11,10},{4,5},{12,11... | collective-permute-start | bytes 983048 | tf_op jit(solution)/shard_map/ppermute | solution.py:228
  53.4 13.9 %collective-permute-start.7 = (f32[5,128,128]{2,1,0:T(8,128)S(1)}, f32[5,128,128]{2,1,0:T(8,128)S(1)}, u32[]{:S(2)}, u32[]{:S(2)}) collective-permute-start(f32[5,128,128]{2,1,0:T(8,128)S(1)} %collective-permute-done.2.refs_0_), channel_id=1, source_target_pairs={{0,1},{8,31},{1,2},{9,8},{2,3},{10,9},{3,4},{11,10},{4,5},{12,11},... | collective-permute-start | bytes 983048 | tf_op jit(solution)/shard_map/ppermute | solution.py:228
  56.8 13.5 %collective-permute-start.12 = (f32[5,128,128]{2,1,0:T(8,128)S(1)}, f32[5,128,128]{2,1,0:T(8,128)S(1)}, u32[]{:S(2)}, u32[]{:S(2)}) collective-permute-start(f32[5,128,128]{2,1,0:T(8,128)S(1)} %collective-permute-done.8.refs_1_), channel_id=1, source_target_pairs={{0,1},{8,31},{1,2},{9,8},{2,3},{10,9},{3,4},{11,10},{4,5},{12,11},... | collective-permute-start | bytes 983048 | tf_op jit(solution)/shard_map/ppermute | solution.py:228
  60.4 13.9 %collective-permute-start.17 = (f32[5,128,128]{2,1,0:T(8,128)S(1)}, f32[5,128,128]{2,1,0:T(8,128)S(1)}, u32[]{:S(2)}, u32[]{:S(2)}) collective-permute-start(f32[5,128,128]{2,1,0:T(8,128)S(1)} %collective-permute-done.13.refs_2_), channel_id=1, source_target_pairs={{0,1},{8,1023},{1,2},{9,8},{2,3},{10,9},{3,4},{11,10},{4,5},{12,11... | collective-permute-start | bytes 983048 | tf_op jit(solution)/shard_map/ppermute | solution.py:228
  63.3 14.0 %collective-permute-start.18 = (f32[5,128,128]{2,1,0:T(8,128)S(1)}, f32[5,128,128]{2,1,0:T(8,128)S(1)}, u32[]{:S(2)}, u32[]{:S(2)}) collective-permute-start(f32[5,128,128]{2,1,0:T(8,128)S(1)} %collective-permute-done.14.refs_3_), channel_id=1, source_target_pairs={{0,1},{8,1023},{1,2},{9,8},{2,3},{10,9},{3,4},{11,10},{4,5},{12,11... | collective-permute-start | bytes 983048 | tf_op jit(solution)/shard_map/ppermute | solution.py:228
  67.3 15.3 %collective-permute-start.11 = (f32[5,128,128]{2,1,0:T(8,128)S(1)}, f32[5,128,128]{2,1,0:T(8,128)S(1)}, u32[]{:S(2)}, u32[]{:S(2)}) collective-permute-start(f32[5,128,128]{2,1,0:T(8,128)S(1)} %collective-permute-done.7.refs_0_), channel_id=1, source_target_pairs={{0,1},{8,31},{1,2},{9,8},{2,3},{10,9},{3,4},{11,10},{4,5},{12,11},... | collective-permute-start | bytes 983048 | tf_op jit(solution)/shard_map/ppermute | solution.py:228
  70.3 16.4 %collective-permute-start.16 = (f32[5,128,128]{2,1,0:T(8,128)S(1)}, f32[5,128,128]{2,1,0:T(8,128)S(1)}, u32[]{:S(2)}, u32[]{:S(2)}) collective-permute-start(f32[5,128,128]{2,1,0:T(8,128)S(1)} %collective-permute-done.12.refs_1_), channel_id=1, source_target_pairs={{0,1},{8,31},{1,2},{9,8},{2,3},{10,9},{3,4},{11,10},{4,5},{12,11},... | collective-permute-start | bytes 983048 | tf_op jit(solution)/shard_map/ppermute | solution.py:228
  74.3 15.6 %collective-permute-start.21 = (f32[5,128,128]{2,1,0:T(8,128)S(1)}, f32[5,128,128]{2,1,0:T(8,128)S(1)}, u32[]{:S(2)}, u32[]{:S(2)}) collective-permute-start(f32[5,128,128]{2,1,0:T(8,128)S(1)} %collective-permute-done.17.refs_2_), channel_id=1, source_target_pairs={{0,1},{8,1023},{1,2},{9,8},{2,3},{10,9},{3,4},{11,10},{4,5},{12,11... | collective-permute-start | bytes 983048 | tf_op jit(solution)/shard_map/ppermute | solution.py:228
  77.3 15.8 %collective-permute-start.22 = (f32[5,128,128]{2,1,0:T(8,128)S(1)}, f32[5,128,128]{2,1,0:T(8,128)S(1)}, u32[]{:S(2)}, u32[]{:S(2)}) collective-permute-start(f32[5,128,128]{2,1,0:T(8,128)S(1)} %collective-permute-done.18.refs_3_), channel_id=1, source_target_pairs={{0,1},{8,1023},{1,2},{9,8},{2,3},{10,9},{3,4},{11,10},{4,5},{12,11... | collective-permute-start | bytes 983048 | tf_op jit(solution)/shard_map/ppermute | solution.py:228
  82.6 15.7 %collective-permute-start.15 = (f32[5,128,128]{2,1,0:T(8,128)S(1)}, f32[5,128,128]{2,1,0:T(8,128)S(1)}, u32[]{:S(2)}, u32[]{:S(2)}) collective-permute-start(f32[5,128,128]{2,1,0:T(8,128)S(1)} %collective-permute-done.11.refs_0_), channel_id=1, source_target_pairs={{0,1},{8,31},{1,2},{9,8},{2,3},{10,9},{3,4},{11,10},{4,5},{12,11},... | collective-permute-start | bytes 983048 | tf_op jit(solution)/shard_map/ppermute | solution.py:228
  86.7 13.6 %collective-permute-start.20 = (f32[5,128,128]{2,1,0:T(8,128)S(1)}, f32[5,128,128]{2,1,0:T(8,128)S(1)}, u32[]{:S(2)}, u32[]{:S(2)}) collective-permute-start(f32[5,128,128]{2,1,0:T(8,128)S(1)} %collective-permute-done.16.refs_1_), channel_id=1, source_target_pairs={{0,1},{8,31},{1,2},{9,8},{2,3},{10,9},{3,4},{11,10},{4,5},{12,11},... | collective-permute-start | bytes 983048 | tf_op jit(solution)/shard_map/ppermute | solution.py:228
  90.0 13.9 %collective-permute-start.25 = (f32[5,128,128]{2,1,0:T(8,128)S(1)}, f32[5,128,128]{2,1,0:T(8,128)S(1)}, u32[]{:S(2)}, u32[]{:S(2)}) collective-permute-start(f32[5,128,128]{2,1,0:T(8,128)S(1)} %collective-permute-done.21.refs_2_), channel_id=1, source_target_pairs={{0,1},{8,1023},{1,2},{9,8},{2,3},{10,9},{3,4},{11,10},{4,5},{12,11... | collective-permute-start | bytes 983048 | tf_op jit(solution)/shard_map/ppermute | solution.py:228
  93.1 12.3 %collective-permute-start.26 = (f32[5,128,128]{2,1,0:T(8,128)S(1)}, f32[5,128,128]{2,1,0:T(8,128)S(1)}, u32[]{:S(2)}, u32[]{:S(2)}) collective-permute-start(f32[5,128,128]{2,1,0:T(8,128)S(1)} %collective-permute-done.22.refs_3_), channel_id=1, source_target_pairs={{0,1},{8,1023},{1,2},{9,8},{2,3},{10,9},{3,4},{11,10},{4,5},{12,11... | collective-permute-start | bytes 983048 | tf_op jit(solution)/shard_map/ppermute | solution.py:228
  98.3 11.2 %collective-permute-start.19 = (f32[5,128,128]{2,1,0:T(8,128)S(1)}, f32[5,128,128]{2,1,0:T(8,128)S(1)}, u32[]{:S(2)}, u32[]{:S(2)}) collective-permute-start(f32[5,128,128]{2,1,0:T(8,128)S(1)} %collective-permute-done.15.refs_0_), channel_id=1, source_target_pairs={{0,1},{8,31},{1,2},{9,8},{2,3},{10,9},{3,4},{11,10},{4,5},{12,11},... | collective-permute-start | bytes 983048 | tf_op jit(solution)/shard_map/ppermute | solution.py:228
  100.3 13.5 %collective-permute-start.24 = (f32[5,128,128]{2,1,0:T(8,128)S(1)}, f32[5,128,128]{2,1,0:T(8,128)S(1)}, u32[]{:S(2)}, u32[]{:S(2)}) collective-permute-start(f32[5,128,128]{2,1,0:T(8,128)S(1)} %collective-permute-done.20.refs_1_), channel_id=1, source_target_pairs={{0,1},{8,31},{1,2},{9,8},{2,3},{10,9},{3,4},{11,10},{4,5},{12,11},... | collective-permute-start | bytes 983048 | tf_op jit(solution)/shard_map/ppermute | solution.py:228
  105.5 36.2 %collective-permute-start.29 = (f32[10,128,128]{2,1,0:T(8,128)S(1)}, f32[10,128,128]{2,1,0:T(8,128)S(1)}, u32[]{:S(2)}, u32[]{:S(2)}) collective-permute-start(f32[10,128,128]{2,1,0:T(8,128)S(1)} %pad_maximum_fusion.1), channel_id=1, source_target_pairs={{0,1},{8,1023},{1,2},{9,8},{2,3},{10,9},{3,4},{11,10},{4,5},{12,11... | collective-permute-start | bytes 1966088 | tf_op jit(solution)/shard_map/ppermute | solution.py:228
  109.5 13.4 %collective-permute-start.23 = (f32[5,128,128]{2,1,0:T(8,128)S(1)}, f32[5,128,128]{2,1,0:T(8,128)S(1)}, u32[]{:S(2)}, u32[]{:S(2)}) collective-permute-start(f32[5,128,128]{2,1,0:T(8,128)S(1)} %collective-permute-done.19.refs_0_), channel_id=1, source_target_pairs={{0,1},{8,31},{1,2},{9,8},{2,3},{10,9},{3,4},{11,10},{4,5},{12,11},... | collective-permute-start | bytes 983048 | tf_op jit(solution)/shard_map/ppermute | solution.py:228
  113.8 12.7 %collective-permute-start.27 = (f32[5,128,128]{2,1,0:T(8,128)S(1)}, f32[5,128,128]{2,1,0:T(8,128)S(1)}, u32[]{:S(2)}, u32[]{:S(2)}) collective-permute-start(f32[5,128,128]{2,1,0:T(8,128)S(1)} %collective-permute-done.24.refs_1_), channel_id=1, source_target_pairs={{0,1},{8,31},{1,2},{9,8},{2,3},{10,9},{3,4},{11,10},{4,5},{12,11},... | collective-permute-start | bytes 983048 | tf_op jit(solution)/shard_map/ppermute | solution.py:228
  126.5 19.7 %collective-permute-start.28 = (f32[10,128,128]{2,1,0:T(8,128)S(1)}, f32[10,128,128]{2,1,0:T(8,128)S(1)}, u32[]{:S(2)}, u32[]{:S(2)}) collective-permute-start(f32[10,128,128]{2,1,0:T(8,128)S(1)} %pad_maximum_fusion), channel_id=1, source_target_pairs={{0,9},{9,0},{10,1},{7,1016},{16,25},{25,16},{26,17},{23,8},{32,41}... | collective-permute-start | bytes 1966088 | tf_op jit(solution)/shard_map/ppermute | solution.py:260
  139.8 14.7 %collective-permute-start.31 = (f32[10,128,128]{2,1,0:T(8,128)S(1)}, f32[10,128,128]{2,1,0:T(8,128)S(1)}, u32[]{:S(2)}, u32[]{:S(2)}) collective-permute-start(f32[10,128,128]{2,1,0:T(8,128)S(1)} %products.19), channel_id=1, source_target_pairs={{992,0},{993,1},{41,9},{994,2},{42,10},{995,3},{43,11},{996,4},{44... | collective-permute-start | bytes 1966088 | tf_op jit(solution)/shard_map/ppermute | solution.py:264
  143.8 10.7 %collective-permute-start.30 = (f32[10,128,128]{2,1,0:T(8,128)S(1)}, f32[10,128,128]{2,1,0:T(8,128)S(1)}, u32[]{:S(2)}, u32[]{:S(2)}) collective-permute-start(f32[10,128,128]{2,1,0:T(8,128)S(1)} %get-tuple-element.103), channel_id=1, source_target_pairs={{0,8},{1,9},{2,10},{3,11},{4,12},{5,13},{6,14},{7,15},{8,0},{9,1},... | collective-permute-start | bytes 1966088 | tf_op jit(solution)/shard_map/ppermute | solution.py:231
